TPU v7x, 32 devices: a whole 2x2x4 slice. The times are simulated.
32 devices in a mesh: seq: 16 (over z, y, x), frame: 2 (over core).
Axes of the slice: x: 2, y: 2, z: 4, core: 2. Of those that a mesh axis runs over, the one named last changes fastest.
Arguments:
- tokens: bfloat16 [16, 3136, 768], P('seq', 'frame'), may hold values from -6 to 6
- ln_gain_first: float32 [768], replicated, may hold values from 0.1 to 1.9
- ln_bias_first: float32 [768], replicated, may hold values from -2 to 2
- w_qkv: bfloat16 [768, 2304], replicated, may hold values from -0.21875 to 0.21875
- q_bias: float32 [768], replicated, may hold values from -3 to 3
- v_bias: float32 [768], replicated, may hold values from -3 to 3
- w_out: bfloat16 [768, 768], replicated, may hold values from -6 to 6
- out_bias: float32 [768], replicated, may hold values from -2 to 2
- ln_gain_second: float32 [768], replicated, may hold values from 0.1 to 1.9
- ln_bias_second: float32 [768], replicated, may hold values from -2 to 2
- w_up: bfloat16 [768, 3072], replicated, may hold values from -0.21875 to 0.21875
- up_bias: float32 [3072], replicated, may hold values from -3 to 3
- w_down: bfloat16 [3072, 768], replicated, may hold values from -0.109375 to 0.109375
- down_bias: float32 [768], replicated, may hold values from -2 to 2
- ln_gain_third: float32 [768], replicated, may hold values from 0.1 to 1.9
- ln_bias_third: float32 [768], replicated, may hold values from -2 to 2
- w_first: bfloat16 [768, 72], replicated, may hold values from -0.078125 to 0.078125
- conv_weights: float32 [3, 8, 72], replicated, may hold values from -0.75 to 0.75
- conv_biases: float32 [4, 8], replicated, may hold values from -3 to 3
- clip_lengths: int32 [16, 2], P('seq'), may hold values from 0 to 16, as said below
- frame_mask: int32 [16, 16], P('seq'), may hold values from 0 to 1, as said below
- out_cot: bfloat16 [16, 3136, 768], P('seq', 'frame'), may hold values from -6 to 6
- pool_cot: bfloat16 [16, 128, 768], P('seq', 'frame'), may hold values from -6 to 6
- penalty_scale: float32 [], replicated, may hold values from 25088 to 50176
Outputs:
- block_output: bfloat16 [16, 3136, 768], P('seq', 'frame')
- pooled_tokens: bfloat16 [16, 128, 768], P('seq', 'frame')
- penalty: float32 [], replicated
- tokens_grad: bfloat16 [16, 3136, 768], P('seq', 'frame')
- ln_gain_first_grad: float32 [768], replicated
- ln_bias_first_grad: float32 [768], replicated
- w_qkv_grad: float32 [768, 2304], P('seq', 'frame')
- q_bias_grad: float32 [768], replicated
- v_bias_grad: float32 [768], replicated
- w_out_grad: float32 [768, 768], P('seq', 'frame')
- out_bias_grad: float32 [768], replicated
- ln_gain_second_grad: float32 [768], replicated
- ln_bias_second_grad: float32 [768], replicated
- w_up_grad: float32 [768, 3072], P('seq', 'frame')
- up_bias_grad: float32 [3072], replicated
- w_down_grad: float32 [3072, 768], P('seq', 'frame')
- down_bias_grad: float32 [768], replicated
- ln_gain_third_grad: float32 [768], replicated
- ln_bias_third_grad: float32 [768], replicated
- w_first_grad: float32 [768, 72], P('seq', 'frame')
- conv_weights_grad: float32 [3, 8, 72], replicated
- conv_biases_grad: float32 [4, 8], replicated
Inputs may be any that keep to these rules, and one draw needn't show every extreme that they name: `clip_lengths`: in each row the first entry is 8, 12 or 16 and the second is 16 minus the first; in every aligned block of 4 rows one row has first entry 16. `frame_mask`: frame 0 and the first frame of the second clip are 1 in every row.
All inputs are finite; a program needn't handle non-finite values.
Results may differ from a plain program's by a relative error of at most 0.012.
Values may be sent and summed in bfloat16 or wider, within the bound.
No kernel may reach another device: no remote copies, remote signals or barrier semaphores. Data moves between devices by JAX's collectives and lax.ppermute only.
A program may use at most 512 MiB of HBM per device.

v0:
```python
import jax
import jax.numpy as jnp
from jax import lax
from jax.sharding import PartitionSpec as P

HEADS = 12
HEAD_DIM = 64
GRID = 14
MAPS = 8


EPS = 1e-06
NEG = -1e30
HIGHEST = lax.Precision.HIGHEST


def norm_rows(rows, gain, shift):
    center = rows - jnp.mean(rows, axis=-1, keepdims=True)
    spread = jnp.mean(center * center, axis=-1, keepdims=True)
    return center * lax.rsqrt(spread + EPS) * gain + shift


def shift_sum(taps):
    padded = jnp.pad(taps, ((0, 0), (1, 1), (1, 1), (0, 0), (0, 0)))
    total = padded[:, 0:GRID, 0:GRID, 0, :]
    for tap in range(1, 9):
        total = total + padded[:, tap // 3 : tap // 3 + GRID, tap % 3 : tap % 3 + GRID, tap, :]
    return total


def conv_tail(first, conv_biases, conv_weights):
    frames = first.shape[0]
    level = shift_sum(first.reshape(frames, GRID, GRID, 9, MAPS)) + conv_biases[0]
    for layer in range(3):
        hidden = jax.nn.gelu(level, approximate=False)
        taps = jnp.einsum("fijc,ck->fijk", hidden, conv_weights[layer], precision=HIGHEST)
        level = shift_sum(taps.reshape(frames, GRID, GRID, 9, MAPS)) + conv_biases[layer + 1]
    return jax.nn.sigmoid(level).reshape(frames, GRID * GRID, MAPS)


def exact_gelu(values):
    return jax.nn.gelu(values, approximate=False)


def pair_mask(query_code, key_code):
    return (query_code[:, :, None] == key_code[:, None, :])[:, None]


def score_rows(query_rows, key_rows):
    return jnp.einsum(
        "sqhe,skhe->shqk", query_rows, key_rows, preferred_element_type=jnp.float32
    ) * HEAD_DIM ** (-0.5)


def pair_terms(query_rows, dout_rows, lse_rows, delta_rows, key_rows, value_rows, allowed):
    scores = score_rows(query_rows, key_rows)
    probs = jnp.where(allowed, jnp.exp(scores - lse_rows[..., None]), 0.0)
    slopes = jnp.einsum(
        "sqhe,skhe->shqk", dout_rows, value_rows, preferred_element_type=jnp.float32
    )
    grads = (probs * (slopes - delta_rows[..., None])).astype(jnp.bfloat16)
    return (probs.astype(jnp.bfloat16), grads)


def column_sum(values):
    return jnp.sum(values.astype(jnp.float32), axis=0)


def per_device(
    tokens,
    ln_gain_first,
    ln_bias_first,
    w_qkv,
    q_bias,
    v_bias,
    w_out,
    out_bias,
    ln_gain_second,
    ln_bias_second,
    w_up,
    up_bias,
    w_down,
    down_bias,
    ln_gain_third,
    ln_bias_third,
    w_first,
    conv_weights,
    conv_biases,
    clip_lengths,
    frame_mask,
    out_cot,
    pool_cot,
    penalty_scale,
):
    seq_count, local, width = tokens.shape
    pixels = GRID * GRID
    frames_here = local // pixels
    frame_total = lax.axis_size("frame")
    frame_rank = lax.axis_index("frame")
    slot_frames = frames_here * frame_total
    length = local * frame_total
    rows = seq_count * local
    image_count = seq_count * frames_here
    scale = HEAD_DIM ** (-0.5)
    positions = jnp.arange(slot_frames, dtype=jnp.int32)[None, :]
    segment_frames = (positions >= clip_lengths[:, 0:1]).astype(jnp.int32)
    key_frames = jnp.where(frame_mask > 0, segment_frames, -1)
    first_frame = frame_rank * frames_here
    query_code = jnp.repeat(
        lax.dynamic_slice_in_dim(segment_frames, first_frame, frames_here, 1), pixels, axis=1
    )
    key_code = jnp.repeat(key_frames, pixels, axis=1)
    valid_here = (
        lax.dynamic_slice_in_dim(frame_mask, first_frame, frames_here, 1)
        .reshape(image_count)
        .astype(jnp.float32)
    )
    flat = tokens.reshape(rows, width).astype(jnp.float32)
    normed_one, back_one = jax.vjp(norm_rows, flat, ln_gain_first, ln_bias_first)
    normed_one = normed_one.astype(jnp.bfloat16)
    qkv_bias = jnp.concatenate([q_bias, jnp.zeros_like(q_bias), v_bias])
    qkv = (jnp.dot(normed_one, w_qkv, preferred_element_type=jnp.float32) + qkv_bias).astype(
        jnp.bfloat16
    )
    qkv = qkv.reshape(seq_count, local, 3, HEADS, HEAD_DIM)
    queries = qkv[:, :, 0]
    keys_here = qkv[:, :, 1]
    values_here = qkv[:, :, 2]
    keys_all, values_all = (
        lax.all_gather(keys_here, "frame", axis=1, tiled=True),
        lax.all_gather(values_here, "frame", axis=1, tiled=True),
    )

    def block_of(array, index):
        return lax.dynamic_slice_in_dim(array, index * local, local, 1)

    def stats_turn(index, carry):
        allowed = pair_mask(query_code, block_of(key_code, index))

        def stats_update(state):
            top, mass = state
            masked = jnp.where(allowed, score_rows(queries, block_of(keys_all, index)), NEG)
            new_top = jnp.maximum(top, jnp.max(masked, axis=-1))
            kept = jnp.where(allowed, jnp.exp(masked - new_top[..., None]), 0.0)
            return (new_top, mass * jnp.exp(top - new_top) + jnp.sum(kept, axis=-1))

        return lax.cond(jnp.any(allowed), stats_update, lambda state: state, carry)

    start_top = jnp.full((seq_count, HEADS, local), NEG, jnp.float32)
    top, mass = lax.fori_loop(0, frame_total, stats_turn, (start_top, jnp.zeros_like(start_top)))
    lse = top + jnp.log(mass)

    def value_turn(index, total):
        allowed = pair_mask(query_code, block_of(key_code, index))

        def value_update(state):
            scores = score_rows(queries, block_of(keys_all, index))
            probs = jnp.where(allowed, jnp.exp(scores - lse[..., None]), 0.0).astype(jnp.bfloat16)
            return state + jnp.einsum(
                "shqk,skhe->sqhe",
                probs,
                block_of(values_all, index),
                preferred_element_type=jnp.float32,
            )

        return lax.cond(jnp.any(allowed), value_update, lambda state: state, total)

    attended = lax.fori_loop(0, frame_total, value_turn, jnp.zeros(queries.shape, jnp.float32))
    attended_low = attended.astype(jnp.bfloat16).reshape(rows, width)
    middle = flat + jnp.dot(attended_low, w_out, preferred_element_type=jnp.float32) + out_bias
    normed_two, back_two = jax.vjp(norm_rows, middle, ln_gain_second, ln_bias_second)
    normed_two = normed_two.astype(jnp.bfloat16)
    upper = jnp.dot(normed_two, w_up, preferred_element_type=jnp.float32) + up_bias
    hidden, gelu_back = jax.vjp(exact_gelu, upper)
    hidden = hidden.astype(jnp.bfloat16)
    output = middle + jnp.dot(hidden, w_down, preferred_element_type=jnp.float32) + down_bias
    output_low = output.astype(jnp.bfloat16)
    normed_three, back_three = jax.vjp(norm_rows, output, ln_gain_third, ln_bias_third)
    normed_three = normed_three.astype(jnp.bfloat16)
    first = jnp.dot(normed_three, w_first, preferred_element_type=jnp.float32)
    maps, tail_back = jax.vjp(
        conv_tail, first.reshape(image_count, pixels, 9 * MAPS), conv_biases, conv_weights
    )
    maps_low = maps.astype(jnp.bfloat16)
    output_frames = output_low.reshape(image_count, pixels, width)
    pooled = (
        jnp.einsum("fpm,fpd->fmd", maps_low, output_frames, preferred_element_type=jnp.float32)
        * valid_here[:, None, None]
    )
    pooled_tokens = pooled.astype(jnp.bfloat16).reshape(seq_count, frames_here * MAPS, width)
    total_map = jnp.sum(maps, axis=-1)
    intersection = 0.5 * (total_map * total_map - jnp.sum(maps * maps, axis=-1))
    intersection_local = jnp.sum(intersection * valid_here[:, None])
    count_local = jnp.sum(valid_here)
    intersection_total, count_total = lax.psum((intersection_local, count_local), ("seq", "frame"))
    penalty = intersection_total / count_total
    pool_frames = pool_cot.reshape(image_count, MAPS, width)
    weight_cot = penalty_scale / count_total
    d_maps = (
        jnp.einsum("fmd,fpd->fpm", pool_frames, output_frames, preferred_element_type=jnp.float32)
        * valid_here[:, None, None]
    )
    d_maps = d_maps + (weight_cot * valid_here)[:, None, None] * (total_map[..., None] - maps)
    d_first, d_conv_biases, d_conv_weights = tail_back(d_maps)
    d_first = d_first.reshape(rows, 9 * MAPS).astype(jnp.bfloat16)
    grad_w_first = jnp.dot(normed_three.T, d_first, preferred_element_type=jnp.float32)
    d_normed_three = jnp.dot(d_first, w_first.T, preferred_element_type=jnp.float32)
    d_from_three, d_gain_three, d_bias_three = back_three(d_normed_three)
    d_pool_rows = (
        jnp.einsum("fpm,fmd->fpd", maps_low, pool_frames, preferred_element_type=jnp.float32)
        * valid_here[:, None, None]
    )
    d_output = (
        out_cot.reshape(rows, width).astype(jnp.float32)
        + d_from_three
        + d_pool_rows.reshape(rows, width)
    )
    d_down = d_output.astype(jnp.bfloat16)
    grad_w_down = jnp.dot(hidden.T, d_down, preferred_element_type=jnp.float32)
    grad_down_bias = column_sum(d_down)
    d_hidden = jnp.dot(d_down, w_down.T, preferred_element_type=jnp.float32)
    d_upper = gelu_back(d_hidden)[0].astype(jnp.bfloat16)
    grad_w_up = jnp.dot(normed_two.T, d_upper, preferred_element_type=jnp.float32)
    grad_up_bias = column_sum(d_upper)
    d_normed_two = jnp.dot(d_upper, w_up.T, preferred_element_type=jnp.float32)
    d_from_two, d_gain_two, d_bias_two = back_two(d_normed_two)
    d_middle = d_output + d_from_two
    d_branch = d_middle.astype(jnp.bfloat16)
    grad_w_out = jnp.dot(attended_low.T, d_branch, preferred_element_type=jnp.float32)
    grad_out_bias = column_sum(d_branch)
    dout_low = jnp.dot(d_branch, w_out.T, preferred_element_type=jnp.float32).astype(jnp.bfloat16)
    dout_low = dout_low.reshape(seq_count, local, HEADS, HEAD_DIM)
    delta = jnp.sum(dout_low.astype(jnp.float32) * attended, axis=-1).transpose(0, 2, 1)
    zeros_here = jnp.zeros(queries.shape, jnp.float32)
    full_zeros = jnp.zeros((seq_count, length, HEADS, HEAD_DIM), jnp.float32)

    def both_turn(index, carry):
        allowed = pair_mask(query_code, block_of(key_code, index))

        def both_update(state):
            grad_q, grad_k, grad_v = state
            key_rows = block_of(keys_all, index)
            probs, grads = pair_terms(
                queries, dout_low, lse, delta, key_rows, block_of(values_all, index), allowed
            )
            grad_q = (
                grad_q
                + jnp.einsum("shqk,skhe->sqhe", grads, key_rows, preferred_element_type=jnp.float32)
                * scale
            )
            part_k = (
                jnp.einsum("shqk,sqhe->skhe", grads, queries, preferred_element_type=jnp.float32)
                * scale
            )
            part_v = jnp.einsum(
                "shqk,sqhe->skhe", probs, dout_low, preferred_element_type=jnp.float32
            )
            grad_k = lax.dynamic_update_slice_in_dim(grad_k, part_k, index * local, 1)
            grad_v = lax.dynamic_update_slice_in_dim(grad_v, part_v, index * local, 1)
            return (grad_q, grad_k, grad_v)

        return lax.cond(jnp.any(allowed), both_update, lambda state: state, carry)

    grad_q, grad_k_all, grad_v_all = lax.fori_loop(
        0, frame_total, both_turn, (zeros_here, full_zeros, full_zeros)
    )
    grad_k, grad_v = (
        lax.psum_scatter(
            grad_k_all.astype(jnp.bfloat16), "frame", scatter_dimension=1, tiled=True
        ).astype(jnp.float32),
        lax.psum_scatter(
            grad_v_all.astype(jnp.bfloat16), "frame", scatter_dimension=1, tiled=True
        ).astype(jnp.float32),
    )
    grad_qkv = (
        jnp.stack([grad_q, grad_k, grad_v], axis=2).astype(jnp.bfloat16).reshape(rows, 3 * width)
    )
    grad_w_qkv = jnp.dot(normed_one.T, grad_qkv, preferred_element_type=jnp.float32)
    grad_q_bias = column_sum(grad_qkv[:, :width])
    grad_v_bias = column_sum(grad_qkv[:, 2 * width :])
    d_normed_one = jnp.dot(grad_qkv, w_qkv.T, preferred_element_type=jnp.float32)
    d_from_one, d_gain_one, d_bias_one = back_one(d_normed_one)
    tokens_grad = (d_middle + d_from_one).astype(jnp.bfloat16).reshape(seq_count, local, width)
    summed = (
        lax.psum_scatter(
            grad_w_qkv.astype(jnp.bfloat16), "seq", scatter_dimension=0, tiled=True
        ).astype(jnp.float32),
        lax.psum_scatter(
            grad_w_out.astype(jnp.bfloat16), "seq", scatter_dimension=0, tiled=True
        ).astype(jnp.float32),
        lax.psum_scatter(
            grad_w_up.astype(jnp.bfloat16), "seq", scatter_dimension=0, tiled=True
        ).astype(jnp.float32),
        lax.psum_scatter(
            grad_w_down.astype(jnp.bfloat16), "seq", scatter_dimension=0, tiled=True
        ).astype(jnp.float32),
        lax.psum_scatter(
            grad_w_first.astype(jnp.bfloat16), "seq", scatter_dimension=0, tiled=True
        ).astype(jnp.float32),
    )
    grad_w_qkv, grad_w_out, grad_w_up, grad_w_down, grad_w_first = (
        lax.psum_scatter(
            summed[0].astype(jnp.bfloat16), "frame", scatter_dimension=1, tiled=True
        ).astype(jnp.float32),
        lax.psum_scatter(
            summed[1].astype(jnp.bfloat16), "frame", scatter_dimension=1, tiled=True
        ).astype(jnp.float32),
        lax.psum_scatter(
            summed[2].astype(jnp.bfloat16), "frame", scatter_dimension=1, tiled=True
        ).astype(jnp.float32),
        lax.psum_scatter(
            summed[3].astype(jnp.bfloat16), "frame", scatter_dimension=1, tiled=True
        ).astype(jnp.float32),
        lax.psum_scatter(
            summed[4].astype(jnp.bfloat16), "frame", scatter_dimension=1, tiled=True
        ).astype(jnp.float32),
    )
    small = lax.psum(
        (
            d_gain_one,
            d_bias_one,
            d_gain_two,
            d_bias_two,
            d_gain_three,
            d_bias_three,
            grad_q_bias,
            grad_v_bias,
            grad_out_bias,
            grad_up_bias,
            grad_down_bias,
            d_conv_weights,
            d_conv_biases,
        ),
        ("seq", "frame"),
    )
    block_output = output_low.reshape(seq_count, local, width)
    return (
        block_output,
        pooled_tokens,
        penalty,
        tokens_grad,
        small[0],
        small[1],
        grad_w_qkv,
        small[6],
        small[7],
        grad_w_out,
        small[8],
        small[2],
        small[3],
        grad_w_up,
        small[9],
        grad_w_down,
        small[10],
        small[4],
        small[5],
        grad_w_first,
        small[11],
        small[12],
    )


def solution(mesh):
    return jax.shard_map(
        per_device,
        mesh=mesh,
        in_specs=(
            P("seq", "frame", None),
            P(),
            P(),
            P(),
            P(),
            P(),
            P(),
            P(),
            P(),
            P(),
            P(),
            P(),
            P(),
            P(),
            P(),
            P(),
            P(),
            P(),
            P(),
            P("seq", None),
            P("seq", None),
            P("seq", "frame", None),
            P("seq", "frame", None),
            P(),
        ),
        out_specs=(
            P("seq", "frame", None),
            P("seq", "frame", None),
            P(),
            P("seq", "frame", None),
            P(),
            P(),
            P("seq", "frame"),
            P(),
            P(),
            P("seq", "frame"),
            P(),
            P(),
            P(),
            P("seq", "frame"),
            P(),
            P("seq", "frame"),
            P(),
            P(),
            P(),
            P("seq", "frame"),
            P(),
            P(),
        ),
        check_vma=False,
    )
```

profile of v0, /device:TPU:0, one launch (start us, length us, event | category | flops | bytes accessed | tf_op | source)
XLA Modules:
  0.0 2035.4 jit_solution(15146906262924886991)
XLA Ops:
  58.6 42.7 %psum.106 = f32[]{:T(128)} all-reduce(f32[]{:T(128)} %convert_reduce_fusion.6), channel_id=1, replica_groups=mesh['seq'=16,'frame'=2] {'seq','frame'}, use_global_device_ids=true, to_apply=%region_23.24 | all-reduce | flops 1 | bytes 8 | tf_op jit(solution)/shard_map/psum | solution.py:195
  130.9 113.2 %while.51 = (s32[]{:T(128)}, f32[1,12,1568]{2,1,0:T(8,128)}, f32[1,12,1568]{2,1,0:T(8,128)}, s32[1,3136]{1,0:T(1,128)S(1)}, bf16[1,3136,12,64]{1,3,2,0:T(8,128)(...) while((s32[]{:T(128)}, f32[1,12,1568]{2,1,0:T(8,128)}, ...), condition=%wide.region_8.9_spmd.clone, body=%wide.region_2.8_spmd.clone.sunk | while | flops 4017428992 | bytes 249688784 | solution.py:150
  140.4 94.1 %conditional.9 = ((f32[1,12,1568]{2,1,0:T(8,128)}, f32[1,12,1568]{2,1,0:T(8,128)})) conditional(s32[]{:T(128)} %convert_element_type.395, (f32[1,12,1568]{2,1,0:T(8,128)}, f32[1,12,1568]{2,1,0:T(8,128)}) %tuple.172, (pred[1,1,1568,1568]{2,3,1,0:T(8,128)(4,1)}, s32[]{:T(128)}, bf16[1,3136,12,64]{1,3,2,0:T(8,128)(2,1)}, ...), branch_computations={%region_4.4_spmd, %region_5.7_spmd} | conditional | flops 4012511744 | bytes 247185984 | solution.py:147
  140.5 47.1 %fusion.6 = (f32[12,1568]{1,0:T(8,128)}, f32[12,1568,1568]{2,1,0:T(8,128)}) fusion(pred[1568,1568]{0,1:T(8,128)(4,1)} %bitcast.388, bf16[1,1568,12,64]{1,3,2,0:T(8,128)(2,1)} %get-tuple-element.509, bf16[1,3136,12,64]{1,3,2,0:T(8,128)(2,1)} %get-tuple-element.507, s32[]{:T(128)S(6)} %select_n.48), kind=kOutput, calls=%fused_computation.5 | convolution fusion | flops 3864937984 | bytes 125810176 | tf_op jit(solution)/shard_map/while/body/eval_jaxpr/cond/branch_1_fun/sqhe,skhe->shqk/dot_general | solution.py:50
  189.2 42.2 %select_reduce_fusion = f32[12,1568]{1,0:T(8,128)} fusion(f32[12,1568,1568]{2,1,0:T(8,128)} %get-tuple-element.883, f32[12,1568]{1,0:T(8,128)} %bitcast.396, pred[1568,1568]{0,1:T(8,128)(4,1)} %bitcast.389), kind=kLoop, calls=%fused_computation.4 | loop fusion | flops 147498624 | bytes 120623104 | tf_op jit(solution)/shard_map/while/body/eval_jaxpr/cond/branch_1_fun/reduce_sum | solution.py:145
  262.9 67.4 %while.52 = (s32[]{:T(128)}, f32[1,1568,12,64]{1,3,2,0:T(8,128)}, s32[1,3136]{1,0:T(1,128)S(1)}, bf16[1,3136,12,64]{1,3,2,0:T(8,128)(2,1)}, bf16[1,3136,12,64]{1...) while((s32[]{:T(128)}, f32[1,1568,12,64]{1,3,2,0:T(8,128)}, ...), condition=%wide.region_13.14_spmd.clone, body=%wide.region_9.13_spmd.clone.sunk | while | flops 7677028352 | bytes 22815940 | solution.py:168
  272.6 48.2 %conditional.10 = (f32[1,1568,12,64]{1,3,2,0:T(8,128)}) conditional(s32[]{:T(128)} %convert_element_type.396, f32[1,1568,12,64]{1,3,2,0:T(8,128)} %get-tuple-element.1163, (s32[]{:T(128)}, bf16[1,3136,12,64]{1,3,2,0:T(8,128)(2,1)}, pred[1,1,1568,1568]{2,3,1,0:T(8,128)(4,1)}, bf16[1,3136,12,64]{1,3,2,0:T(8,128)(2,1)}, ...), branch_computations={%region_11.11_spmd, %region_12.12_spmd} | conditional | flops 7672111104 | bytes 20313142 | solution.py:166
  272.6 48.2 %bitcast_add_fusion.1 = f32[1,1568,12,64]{1,3,2,0:T(8,128)} fusion(f32[1,1568,12,64]{1,3,2,0:T(8,128)} %get-tuple-element.521, f32[12,1568]{1,0:T(8,128)} %bitcast.433, pred[1568,1568]{0,1:T(8,128)(4,1)} %bitcast.393, bf16[1,1568,12,64]{1,3,2,0:T(8,128)(2,1)} %get-tuple-element.526, bf16[1,3136,12,64]{1,3,2,0:T(8,128)(2,1)} %get-tuple-element.525, ...), kind=kOutput, calls=%fused_computation.16 | convolution fusion | flops 7672111104 | bytes 20313088 | tf_op jit(solution)/shard_map/while/body/eval_jaxpr/cond/branch_1_fun/shqk,skhe->sqhe/dot_general | solution.py:159
  338.2 52.5 %multiply_convert_fusion = (bf16[1568,3072]{1,0:T(8,128)(2,1)S(1)}, f32[1568,3072]{1,0:T(8,128)}, f32[1568,3072]{1,0:T(8,128)}) fusion(f32[3072]{0:T(1024)S(1)} %copy-done.89, bf16[768,3072]{1,0:T(8,128)(2,1)S(1)} %bitcast.446, f32[1568,768]{1,0:T(8,128)S(1)} %get-tuple-element.903, f32[768]{0:T(1024)S(1)} %copy-done.93, f32[768]{0:T(1024)S(1)} %copy-done.76, ...), kind=kOutput, calls=%fused_computation.63 | convolution fusion | flops 7722688512 | bytes 57735424 | tf_op jit(solution)/shard_map/dot_general | solution.py:173
  512.2 28.1 %convert_reduce_fusion = (f32[3072]{0:T(1024)}, bf16[1568,3072]{1,0:T(8,128)(2,1)}) fusion(f32[1568,3072]{1,0:T(8,128)} %get-tuple-element.881, bf16[3072,768]{1,0:T(8,128)(2,1)} %param.48, f32[1568,768]{1,0:T(8,128)} %get-tuple-element.870, f32[1568,3072]{1,0:T(8,128)} %get-tuple-element.904, f32[3072]{0:T(1024)S(1)} %copy-done.90), kind=kOutput, calls=%fused_computation.61 | convolution fusion | flops 7481840640 | bytes 57729024 | tf_op jit(solution)/shard_map/dot_general | solution.py:221
  540.3 16.2 multiply_reduce_fusion.2
  591.3 299.9 %while.53 = (s32[]{:T(128)}, f32[1,1568,12,64]{1,3,2,0:T(8,128)}, bf16[1,3136,12,64]{1,3,2,0:T(8,128)(2,1)}, bf16[1,3136,12,64]{1,3,2,0:T(8,128)(2,1)}, s32[1,31...) while((s32[]{:T(128)}, f32[1,1568,12,64]{1,3,2,0:T(8,128)}, ...), condition=%wide.region_33.34_spmd.clone, body=%wide.region_29.33_spmd.clone.sunk | while | flops 19187001344 | bytes 591735744 | solution.py:264
  599.3 283.4 %conditional.11 = ((f32[1,1568,12,64]{1,3,2,0:T(8,128)}, bf16[1,3136,12,64]{1,3,2,0:T(8,128)(2,1)}, bf16[1,3136,12,64]{1,3,2,0:T(8,128)(2,1)})) conditional(s32[]{:T(128)} %convert_element_type.397, (f32[1,1568,12,64]{1,3,2,0:T(8,128)}, bf16[1,3136,12,64]{1,3,2,0:T(8,128)(2,1)}, bf16[1,3136,12,64]{1,3,2,0:T(8,128)(2,1)}) %tuple.179, (s32[]{:T(128)}, ...), branch_computations={%region_31.31_spmd, %region_32.32_spmd} | conditional | flops 19182084096 | bytes 589232704 | solution.py:262
  599.4 44.6 %fusion.38 = f32[12,1568,1568]{2,1,0:T(8,128)} fusion(bf16[1,1568,12,64]{1,3,2,0:T(8,128)(2,1)} %get-tuple-element.541, bf16[1,3136,12,64]{1,3,2,0:T(8,128)(2,1)} %get-tuple-element.538, s32[]{:T(128)S(6)} %select_n.55), kind=kOutput, calls=%fused_computation.38 | convolution fusion | flops 3776446464 | bytes 123125760 | tf_op jit(solution)/shard_map/while/body/eval_jaxpr/cond/branch_1_fun/sqhe,skhe->shqk/dot_general | solution.py:50
  644.0 47.9 %fusion.31 = bf16[1,1568,12,64]{1,3,2,0:T(8,128)(2,1)} fusion(f32[12,1568,1568]{2,1,0:T(8,128)} %fusion.38, f32[12,1568]{1,0:T(8,128)} %bitcast.434, pred[1568,1568]{0,1:T(8,128)(4,1)} %bitcast.391, bf16[1,1568,12,64]{1,3,2,0:T(8,128)(2,1)} %get-tuple-element.544), kind=kOutput, calls=%fused_computation.33 | convolution fusion | flops 3894460416 | bytes 125364736 | tf_op jit(solution)/shard_map/while/body/eval_jaxpr/cond/branch_1_fun/shqk,sqhe->skhe/dot_general | solution.py:255
  691.9 78.9 %fusion.26 = bf16[12,1568,1568]{1,2,0:T(8,128)(2,1)} fusion(f32[12,1568,1568]{2,1,0:T(8,128)} %fusion.38, f32[12,1568]{1,0:T(8,128)} %bitcast.432, f32[12,1568]{1,0:T(8,128)} %bitcast.435, pred[1568,1568]{0,1:T(8,128)(4,1)} %bitcast.392, bf16[1,1568,12,64]{1,3,2,0:T(8,128)(2,1)} %get-tuple-element.544, bf16[1,3136,12,64]{1,3,2,0:T(8,128)(2,1)} %get-tuple-element.543, ...), kind=kOutput, calls=%fused_computation.26 | convolution fusion | flops 3953467392 | bytes 192180224 | tf_op jit(solution)/shard_map/while/body/eval_jaxpr/cond/branch_1_fun/sqhe,skhe->shqk/dot_general | solution.py:58
  770.8 28.1 %multiply_bitcast_fusion = bf16[1,1568,12,64]{1,3,2,0:T(8,128)(2,1)} fusion(bf16[12,1568,1568]{1,2,0:T(8,128)(2,1)} %fusion.26, bf16[1,1568,12,64]{1,3,2,0:T(8,128)(2,1)} %get-tuple-element.541), kind=kOutput, calls=%fused_computation.32 | convolution fusion | flops 3778854912 | bytes 63823872 | tf_op jit(solution)/shard_map/while/body/eval_jaxpr/cond/branch_1_fun/shqk,sqhe->skhe/dot_general | solution.py:252
  798.9 27.6 %bitcast_add_fusion.2 = f32[1,1568,12,64]{1,3,2,0:T(8,128)} fusion(f32[1,1568,12,64]{1,3,2,0:T(8,128)} %get-tuple-element.537, bf16[12,1568,1568]{1,2,0:T(8,128)(2,1)} %fusion.26, bf16[1,3136,12,64]{1,3,2,0:T(8,128)(2,1)} %get-tuple-element.538, s32[]{:T(128)S(6)} %select_n.55), kind=kOutput, calls=%fused_computation.31 | convolution fusion | flops 3778854912 | bytes 75104256 | tf_op jit(solution)/shard_map/while/body/eval_jaxpr/cond/branch_1_fun/shqk,skhe->sqhe/dot_general | solution.py:248
  826.4 28.1 %dynamic_update_slice.4 = bf16[1,3136,12,64]{1,3,2,0:T(8,128)(2,1)} dynamic-update-slice(bf16[1,3136,12,64]{1,3,2,0:T(8,128)(2,1)} %get-tuple-element.546, bf16[1,1568,12,64]{1,3,2,0:T(8,128)(2,1)} %multiply_bitcast_fusion, s32[]{:T(128)} %constant.133.clone, s32[]{:T(128)S(6)} %select_n.55, s32[]{:T(128)} %constant.133.clone, s32[]{:T(128)} %constant.133.clone) | dynamic-update-slice | bytes 4816900 | tf_op jit(solution)/shard_map/while/body/eval_jaxpr/cond/branch_1_fun/dynamic_update_slice | solution.py:258
  854.6 28.2 %dynamic_update_slice.5 = bf16[1,3136,12,64]{1,3,2,0:T(8,128)(2,1)} dynamic-update-slice(bf16[1,3136,12,64]{1,3,2,0:T(8,128)(2,1)} %get-tuple-element.547, bf16[1,1568,12,64]{1,3,2,0:T(8,128)(2,1)} %fusion.31, s32[]{:T(128)} %constant.133.clone, s32[]{:T(128)S(6)} %select_n.55, s32[]{:T(128)} %constant.133.clone, s32[]{:T(128)} %constant.133.clone) | dynamic-update-slice | bytes 4816900 | tf_op jit(solution)/shard_map/while/body/eval_jaxpr/cond/branch_1_fun/dynamic_update_slice | solution.py:259
  891.2 15.8 copy.160
  907.0 16.3 reshape.756
  923.4 15.8 copy.158
  939.2 16.3 reshape.754
  975.1 15.7 convolution_convert_fusion.2
  990.9 374.2 %reduce-scatter.37.cloned.1.call-done = bf16[1568,768]{1,0:T(8,128)(2,1)} async-done(((bf16[3136,768]{1,0:T(8,128)(2,1)}), bf16[1568,768]{1,0:T(8,128)(2,1)}) %reduce-scatter.37.cloned.1.call-update) | async-done | bytes 2408464
  1381.6 15.9 reduce-scatter.35.cloned.1.call-done
  1454.8 86.7 %reduce-scatter.31.cloned.1.call-done = bf16[192,768]{1,0:T(8,128)(2,1)} async-done(((bf16[3072,768]{1,0:T(8,128)(2,1)}), bf16[192,768]{1,0:T(8,128)(2,1)}) %reduce-scatter.31.cloned.1.call-update) | async-done | bytes 294928 | tf_op jit(solution)/shard_map/reduce_scatter | solution.py:294
  1549.2 118.8 %reduce-scatter.33.cloned.1.call-done = bf16[48,72]{1,0:T(8,128)(2,1)} async-done(((bf16[768,72]{1,0:T(8,128)(2,1)}), bf16[48,72]{1,0:T(8,128)(2,1)}) %reduce-scatter.33.cloned.1.call-update) | async-done | bytes 6928 | tf_op jit(solution)/shard_map/reduce_scatter | solution.py:297
  1680.6 141.8 %reduce-scatter.27.cloned.1.call-done = bf16[48,3072]{1,0:T(8,128)(2,1)} async-done(((bf16[768,3072]{1,0:T(8,128)(2,1)}), bf16[48,3072]{1,0:T(8,128)(2,1)}) %reduce-scatter.27.cloned.1.call-update) | async-done | bytes 294928 | tf_op jit(solution)/shard_map/reduce_scatter | solution.py:291
  1837.4 123.3 %reduce-scatter.23.cloned.1.call-done = bf16[48,2304]{1,0:T(8,128)(2,1)} async-done(((bf16[768,2304]{1,0:T(8,128)(2,1)}), bf16[48,2304]{1,0:T(8,128)(2,1)}) %reduce-scatter.23.cloned.1.call-update) | async-done | bytes 221200 | tf_op jit(solution)/shard_map/reduce_scatter | solution.py:285
  1975.3 42.6 %all-reduce.48 = (f32[]{:T(128)}, f32[768]{0:T(1024)}, f32[768]{0:T(1024)}, f32[768]{0:T(1024)}, f32[768]{0:T(1024)}, /*index=5*/f32[768]{0:T(1024)}, f32[768]{0...) all-reduce(f32[]{:T(128)} %multiply_reduce_fusion.8, ...), channel_id=1, replica_groups=mesh['seq'=16,'frame'=2] {'seq','frame'}, use_global_device_ids=true, to_apply=%region_21.22 | all-reduce | flops 12513 | bytes 100104 | tf_op jit(solution)/shard_map/psum | solution.py:195
  (397 shorter events, 467.5 us)
Async XLA Ops:
  7.3 108.0 %all-gather.7.cloned.1.call-start = ((), (), s32[]{:S(2)}) async-start(), calls=%async_computation.18 | async-start | bytes 19267584 | tf_op jit(solution)/shard_map/all_gather | solution.py:130
  48.2 196.0 %all-gather.5.cloned.1.call-start = ((), (), s32[]{:S(2)}) async-start(), calls=%async_computation.17 | async-start | bytes 19267584 | tf_op jit(solution)/shard_map/all_gather | solution.py:131
  57.3 44.7 %copy-start.96 = (s32[1,2]{1,0:T(1,128)S(1)}, s32[1,2]{1,0:T(1,128)}, u32[]{:S(2)}) copy-start(s32[1,2]{1,0:T(1,128)} %param.55) | copy-start | bytes 28
  57.3 916.0 %reduce-scatter.25.cloned.1.call-start = ((), (), s32[]{:S(2)}) async-start(), calls=%async_computation.12 | async-start | bytes 1253376 | tf_op jit(solution)/shard_map/reduce_scatter | solution.py:288
  333.8 57.0 %slice-start.2 = ((s8[4718592]{0:T(1024)(128)(4,1)}), s8[4194304]{0:T(1024)(128)(4,1)S(1)}, s32[]{:S(2)}) async-start(s8[4718592]{0:T(1024)(128)(4,1)} %bitcast.443), calls=%async_computation.26 | async-start | bytes 8388608
  336.4 54.4 %copy-start.10 = (f32[1568,768]{1,0:T(8,128)}, f32[1568,768]{1,0:T(8,128)S(1)}, u32[]{:S(2)}) copy-start(f32[1568,768]{1,0:T(8,128)S(1)} %get-tuple-element.903) | copy-start | bytes 14450692
  336.5 54.3 %copy-start.44 = (f32[1568]{0:T(1024)}, f32[1568]{0:T(1024)S(1)}, u32[]{:S(2)}) copy-start(f32[1568]{0:T(1024)S(1)} %broadcast_multiply_fusion.2) | copy-start | bytes 18820
  338.2 52.5 %copy-start.58 = (f32[1568]{0:T(1024)}, f32[1568]{0:T(1024)S(1)}, u32[]{:S(2)}) copy-start(f32[1568]{0:T(1024)S(1)} %fusion.239) | copy-start | bytes 18820
  338.2 52.6 %slice-start.3 = ((s8[4718592]{0:T(1024)(128)(4,1)}), s8[524288]{0:T(1024)(128)(4,1)S(1)}, s32[]{:S(2)}) async-start(s8[4718592]{0:T(1024)(128)(4,1)} %bitcast.443), calls=%async_computation.27 | async-start | bytes 1048576
  338.2 52.6 %copy-start.92 = (f32[768]{0:T(1024)S(1)}, f32[768]{0:T(1024)}, u32[]{:S(2)}) copy-start(f32[768]{0:T(1024)} %param.49) | copy-start | bytes 9220
  512.1 28.1 %copy-start.45 = (f32[1568]{0:T(1024)S(1)}, f32[1568]{0:T(1024)}, u32[]{:S(2)}) copy-start(f32[1568]{0:T(1024)} %copy-done.44) | copy-start | bytes 18820
  512.2 28.1 %copy-start.59 = (f32[1568]{0:T(1024)S(1)}, f32[1568]{0:T(1024)}, u32[]{:S(2)}) copy-start(f32[1568]{0:T(1024)} %copy-done.58) | copy-start | bytes 18820
  512.2 28.1 %copy-start.77 = (f32[768]{0:T(1024)S(1)}, f32[768]{0:T(1024)}, u32[]{:S(2)}) copy-start(f32[768]{0:T(1024)} %param.44) | copy-start | bytes 9220
  540.3 16.2 copy-start.50
  568.0 797.1 %reduce-scatter.37.cloned.1.call-start = ((), (), s32[]{:S(2)}) async-start(), calls=%async_computation.20 | async-start | bytes 7225344
  599.3 283.4 %copy-start.36 = (s32[8]{0:T(128)S(1)}, s32[8]{0:T(128)}, u32[]{:S(2)}) copy-start(s32[8]{0:T(128)} %get-tuple-element.1316) | copy-start | bytes 100 | tf_op jit(solution)/shard_map/while
  923.3 474.1 %reduce-scatter.35.cloned.1.call-start = ((), (), s32[]{:S(2)}) async-start(), calls=%async_computation.19 | async-start | bytes 7225344
  955.5 586.0 %reduce-scatter.31.cloned.1.call-start = ((), (), s32[]{:S(2)}) async-start(), calls=%async_computation.15 | async-start | bytes 5013504 | tf_op jit(solution)/shard_map/reduce_scatter | solution.py:294
  969.9 698.1 %reduce-scatter.33.cloned.1.call-start = ((), (), s32[]{:S(2)}) async-start(), calls=%async_computation.16 | async-start | bytes 208896 | tf_op jit(solution)/shard_map/reduce_scatter | solution.py:297
  973.3 704.4 %reduce-scatter.41.cloned.1.call-start = ((), (), s32[]{:S(2)}) async-start(), calls=%async_computation.22 | async-start | bytes 294912
  975.1 847.4 %reduce-scatter.27.cloned.1.call-start = ((), (), s32[]{:S(2)}) async-start(), calls=%async_computation.13 | async-start | bytes 5013504 | tf_op jit(solution)/shard_map/reduce_scatter | solution.py:291
  990.8 969.9 %reduce-scatter.23.cloned.1.call-start = ((), (), s32[]{:S(2)}) async-start(), calls=%async_computation.11 | async-start | bytes 3760128 | tf_op jit(solution)/shard_map/reduce_scatter | solution.py:285
  1422.3 12.0 copy-start.72
  1431.8 587.4 %reduce-scatter.43.cloned.1.call-start = ((), (), s32[]{:S(2)}) async-start(), calls=%async_computation.23 | async-start | bytes 589824
  1434.8 14.8 slice-start
  1449.6 96.8 %copy-start.68 = (f32[8]{0:T(128)S(1)}, f32[8]{0:T(128)}, u32[]{:S(2)}) copy-start(f32[8]{0:T(128)} %get-tuple-element.901) | copy-start | bytes 100
  1543.4 479.2 %reduce-scatter.29.cloned.1.call-start = ((), (), s32[]{:S(2)}) async-start(), calls=%async_computation.14 | async-start | bytes 442368 | tf_op jit(solution)/shard_map/reduce_scatter | solution.py:308
  1822.4 201.8 %reduce-scatter.39.cloned.1.call-start = ((), (), s32[]{:S(2)}) async-start(), calls=%async_computation.21 | async-start | bytes 884736
  1822.5 11.7 copy-start.7
  1822.5 11.6 copy-start.43
  1822.5 11.6 copy-start.64
  1834.1 128.7 %copy-start.39 = (f32[1568]{0:T(1024)S(1)}, f32[1568]{0:T(1024)}, u32[]{:S(2)}) copy-start(f32[1568]{0:T(1024)} %copy-done.38) | copy-start | bytes 18820
  (86 other events, 375.5 us)
Sparse Core Ops, SparseCore 0:
  48.3 27.8 all-gather.6
  77.8 26.4 all-gather.4
  568.1 266.5 reduce-scatter.24
  923.5 441.5 reduce-scatter.36
  1367.3 30.0 reduce-scatter.34
  1402.5 138.9 reduce-scatter.30
  1547.4 120.5 reduce-scatter.32
  1670.9 6.7 reduce-scatter.40
  1683.6 138.7 reduce-scatter.26
  1827.4 133.2 reduce-scatter.22
  1962.9 6.9 reduce-scatter.42
  1972.1 8.8 reduce-scatter.28
  1983.4 9.2 reduce-scatter.38
where the time goes:
time: 2050 us; the launch traced here: 2040 us
  waiting for transfers between devices  863 us (42%)
  matrix products  567 us (28%)
  local copies, waits for them, and re-layouts  323 us (16%)
  other arithmetic  167 us (8%)
  blocking collectives  89.8 us (4%)
    unnamed x18, waiting for transfers between devices  393 us
    unnamed x224, local copies, waits for them, and re-layouts  151 us
    reduce_scatter x1, waiting for transfers between devices, per_device(): lax.psum_scatter(grad_w_up.astype(jnp.bfloat16), 'seq', scatter_dimension...  142 us
    reduce_scatter x1, waiting for transfers between devices, per_device(): lax.psum_scatter(grad_w_qkv.astype(jnp.bfloat16), 'seq', scatter_dimensio...  123 us
    reduce_scatter x1, waiting for transfers between devices, per_device(): lax.psum_scatter(grad_w_first.astype(jnp.bfloat16), 'seq', scatter_dimens...  119 us
    dot_general x2, matrix products, score_rows(): jnp.einsum('sqhe,skhe->shqk', query_rows, key_rows, preferred_element_typ...  91.7 us
    reduce_scatter x1, waiting for transfers between devices, per_device(): lax.psum_scatter(grad_w_down.astype(jnp.bfloat16), 'seq', scatter_dimensi...  86.7 us
    psum x2, blocking collectives, per_device(): lax.psum((intersection_local, count_local), ('seq', 'frame'))  85.2 us
  transfers between devices with their start and end apart: 13, of which 7 were waited for; matrix products, arithmetic and copies ran while one was open for 34% of the time, Pallas kernels for 0%

commit v1 on v0

--- a/solution.py
+++ b/solution.py
@@ -1,6 +1,11 @@
+import functools
+
 import jax
 import jax.numpy as jnp
+import numpy as np
 from jax import lax
+from jax.experimental import pallas as pl
+from jax.experimental.pallas import tpu as pltpu
 from jax.sharding import PartitionSpec as P
 
 HEADS = 12
@@ -66,7 +71,7 @@
     return jnp.sum(values.astype(jnp.float32), axis=0)
 
 
-def per_device(
+def plain_device(
     tokens,
     ln_gain_first,
     ln_bias_first,
@@ -359,6 +364,959 @@
         small[12],
     )
 
+FAR = -3e30
+LOG2E = 1.4426950408889634
+LN2 = 0.6931471805599453
+NN = (((1,), (0,)), ((), ()))
+NT = (((1,), (1,)), ((), ()))
+TN = (((0,), (0,)), ((), ()))
+PIXELS = 196
+FRAME_ROWS = 208
+CHUNK = 512
+VMEM_LIMIT = 60 * 1024 * 1024
+
+
+def dot(a, b, dims=NN):
+    return lax.dot_general(a, b, dims, preferred_element_type=jnp.float32)
+
+
+def compact_rows(frame_total):
+    chunks = -(-frame_total * FRAME_ROWS // CHUNK) + 1
+    return chunks * CHUNK
+
+
+def compact_kernel(frames_here, info_ref, own_k, own_v, other_k, other_v, kc_ref, vc_ref, valid_ref, table_ref):
+    total = 2 * frames_here
+    length = info_ref[total]
+    rank = info_ref[total + 1]
+    count = [jnp.int32(0), jnp.int32(0)]
+    places = []
+    for f in range(total):
+        kept = info_ref[f]
+        late = (f >= length).astype(jnp.int32)
+        places.append((kept, late, jnp.where(late == 1, count[1], count[0])))
+        count[0] = count[0] + kept * (1 - late)
+        count[1] = count[1] + kept * late
+    chunks = [(c * FRAME_ROWS + CHUNK - 1) // CHUNK for c in count]
+    base = [jnp.int32(0), chunks[0] * CHUNK]
+    table_ref[total] = chunks[0]
+    table_ref[total + 1] = chunks[0] + chunks[1]
+    width = own_k.shape[1]
+    zeros = jnp.zeros((CHUNK, width), jnp.bfloat16)
+    valid_ref[...] = jnp.zeros_like(valid_ref)
+    row = lax.broadcasted_iota(jnp.int32, (FRAME_ROWS, width), 0)
+
+    def first_row(f):
+        side = f // frames_here
+        local = f % frames_here
+        start = local * PIXELS // 16 * 16
+        a = own_k[start : start + 16, :].astype(jnp.float32)
+        b = other_k[start : start + 16, :].astype(jnp.float32)
+        block = jnp.where(rank == side, a, b)
+        at = local * PIXELS - start
+        return block[at : at + 1, :]
+
+    fills = [first_row(0), first_row(total // 2)]
+    for f in range(total // 2 + 1, total):
+        if (f * PIXELS) % 16 == 0:
+            fills[1] = jnp.where(length == f, first_row(f), fills[1])
+    for s in range(2):
+        at = pl.multiple_of(base[s] + count[s] * FRAME_ROWS, 16)
+        kc_ref[pl.ds(at, CHUNK), :] = jnp.broadcast_to(fills[s], (CHUNK, width)).astype(jnp.bfloat16)
+        vc_ref[pl.ds(at, CHUNK), :] = zeros
+    for f in range(total):
+        kept, late, place = places[f]
+        at = pl.multiple_of(jnp.where(late == 1, base[1], base[0]) + place * FRAME_ROWS, 16)
+        table_ref[f] = jnp.where(kept == 1, at, -1)
+        side = f // frames_here
+        local = f % frames_here
+        start = local * PIXELS // 16 * 16
+        lo = local * PIXELS - start
+        inside = (row >= lo) & (row < lo + PIXELS)
+
+        def put(k_ref, v_ref):
+            k = k_ref[start : start + FRAME_ROWS, :].astype(jnp.float32)
+            v = v_ref[start : start + FRAME_ROWS, :].astype(jnp.float32)
+            kc_ref[pl.ds(at, FRAME_ROWS), :] = jnp.where(inside, k, k[lo : lo + 1, :]).astype(jnp.bfloat16)
+            vc_ref[pl.ds(at, FRAME_ROWS), :] = jnp.where(inside, v, 0.0).astype(jnp.bfloat16)
+            valid_ref[pl.ds(at, FRAME_ROWS), :] = inside[:, :128].astype(jnp.bfloat16)
+
+        @pl.when((kept == 1) & (rank == side))
+        def _():
+            put(own_k, own_v)
+
+        @pl.when((kept == 1) & (rank != side))
+        def _():
+            put(other_k, other_v)
+
+
+def compact(info, own_k, own_v, other_k, other_v, frames_here):
+    rows, width = own_k.shape
+    length = compact_rows(2 * frames_here)
+    vm = pl.BlockSpec(memory_space=pltpu.VMEM)
+    sm = pl.BlockSpec(memory_space=pltpu.SMEM)
+    return pl.pallas_call(
+        functools.partial(compact_kernel, frames_here),
+        out_shape=(
+            jax.ShapeDtypeStruct((length + CHUNK, width), jnp.bfloat16),
+            jax.ShapeDtypeStruct((length + CHUNK, width), jnp.bfloat16),
+            jax.ShapeDtypeStruct((length + CHUNK, 128), jnp.bfloat16),
+            jax.ShapeDtypeStruct((2 * frames_here + 2,), jnp.int32),
+        ),
+        in_specs=[sm, vm, vm, vm, vm],
+        out_specs=(vm, vm, vm, sm),
+        compiler_params=pltpu.CompilerParams(vmem_limit_bytes=VMEM_LIMIT),
+        name="compact",
+    )(info, own_k, own_v, other_k, other_v)
+
+
+def query_tiles(rows):
+    parts = max(1, rows // 512)
+    tiles = [(i * 512, 512) for i in range(parts)]
+    last = tiles[-1][0]
+    tiles[-1] = (last, rows - last)
+    return tiles
+
+
+def chunk_range(frames_here, table_ref, info_ref):
+    total = 2 * frames_here
+    length = info_ref[total]
+    rank = info_ref[total + 1]
+    first = rank * frames_here
+    low = jnp.where(first >= length, table_ref[total], 0)
+    high = jnp.where(first + frames_here <= length, table_ref[total], table_ref[total + 1])
+    edge = jnp.clip((length - first) * PIXELS, 0, frames_here * PIXELS)
+    return low, high, table_ref[total], edge
+
+
+def split_heads(rows):
+    lane = lax.broadcasted_iota(jnp.int32, rows.shape, 1)
+    zero = jnp.zeros_like(rows)
+    return jnp.where(lane < 64, rows, zero), jnp.where(lane < 64, zero, rows)
+
+
+def bias_row(c, split, edge, at, size):
+    column = lax.broadcasted_iota(jnp.int32, (1, size), 1) + at
+    same = (column >= edge) == (c >= split)
+    return jnp.where(same, 0.0, FAR)
+
+
+def attn_fwd_kernel(frames_here, info_ref, table_ref, q_ref, k_ref, v_ref, valid_ref, o_ref, lse_ref, qm, vt, acc, top):
+    rows = q_ref.shape[0]
+    low, high, split, edge = chunk_range(frames_here, table_ref, info_ref)
+    qm[0], qm[1] = split_heads(q_ref[...])
+    acc[...] = jnp.zeros_like(acc)
+    top[...] = jnp.full_like(top, NEG)
+    tiles = query_tiles(rows)
+    work = [(h, at, size) for h in range(2) for at, size in tiles]
+
+    def prepare(c, carry):
+        span = pl.ds(pl.multiple_of(c * CHUNK, CHUNK), CHUNK)
+        turned = v_ref[span, :].T
+        ones = valid_ref[span, :].T[:16]
+        for h in range(2):
+            vt[h, 0:64, span] = turned[64 * h : 64 * h + 64]
+            vt[h, 64:80, span] = ones
+        return carry
+
+    lax.fori_loop(low, high, prepare, 0)
+
+    def body(c, carry):
+        span = pl.ds(pl.multiple_of(c * CHUNK, CHUNK), CHUNK)
+        keys = k_ref[span, :]
+
+        def scores(item):
+            h, at, size = item
+            return dot(keys, qm[h, at : at + size, :], NT)
+
+        ahead = scores(work[0])
+        for i, (h, at, size) in enumerate(work):
+            s = ahead
+            if i + 1 < len(work):
+                ahead = scores(work[i + 1])
+            bias = bias_row(c, split, edge, at, size)
+            old = top[h : h + 1, at : at + size]
+            new = jnp.maximum(old, jnp.max(s, axis=0, keepdims=True) + bias)
+            p = jnp.exp2(s - (new - bias)).astype(jnp.bfloat16)
+            top[h : h + 1, at : at + size] = new
+            acc[h, :, at : at + size] = acc[h, :, at : at + size] * jnp.exp2(old - new) + dot(
+                vt[h, :, span], p
+            )
+        return carry
+
+    lax.fori_loop(low, high, body, 0)
+    for at, size in tiles:
+        halves = []
+        for h in range(2):
+            mass = acc[h, 64:65, at : at + size]
+            halves.append(acc[h, 0:64, at : at + size] / mass)
+            lse_ref[0, h : h + 1, at : at + size] = top[h : h + 1, at : at + size] + jnp.log2(mass)
+        o_ref[at : at + size, :] = jnp.concatenate(halves, axis=0).T.astype(jnp.bfloat16)
+
+
+def attn_fwd(info, table, q, kc, vc, valid, frames_here):
+    rows, width = q.shape
+    length = kc.shape[0]
+    pairs = width // 128
+    return pl.pallas_call(
+        functools.partial(attn_fwd_kernel, frames_here),
+        out_shape=(
+            jax.ShapeDtypeStruct((rows, width), jnp.bfloat16),
+            jax.ShapeDtypeStruct((pairs, 8, rows), jnp.float32),
+        ),
+        grid_spec=pltpu.PrefetchScalarGridSpec(
+            num_scalar_prefetch=2,
+            grid=(pairs,),
+            in_specs=[
+                pl.BlockSpec((rows, 128), lambda p, *_: (0, p)),
+                pl.BlockSpec((length, 128), lambda p, *_: (0, p)),
+                pl.BlockSpec((length, 128), lambda p, *_: (0, p)),
+                pl.BlockSpec((length, 128), lambda p, *_: (0, 0)),
+            ],
+            out_specs=[
+                pl.BlockSpec((rows, 128), lambda p, *_: (0, p)),
+                pl.BlockSpec((1, 8, rows), lambda p, *_: (p, 0, 0)),
+            ],
+            scratch_shapes=[
+                pltpu.VMEM((2, rows, 128), jnp.bfloat16),
+                pltpu.VMEM((2, 80, length), jnp.bfloat16),
+                pltpu.VMEM((2, 80, rows), jnp.float32),
+                pltpu.VMEM((8, rows), jnp.float32),
+            ],
+        ),
+        compiler_params=pltpu.CompilerParams(
+            vmem_limit_bytes=VMEM_LIMIT, dimension_semantics=("arbitrary",)
+        ),
+        cost_estimate=pl.CostEstimate(flops=int(8e10), bytes_accessed=int(2e7), transcendentals=0),
+        name="attn_fwd",
+    )(info, table, q, kc, vc, valid)
+
+
+def attn_bwd_kernel(
+    frames_here, info_ref, table_ref, q_ref, k_ref, v_ref, valid_ref, o_ref, do_ref, lse_ref,
+    dq_ref, dk_ref, dv_ref, qm, dom, kt, dqt, delta,
+):
+    rows = q_ref.shape[0]
+    low, high, split, edge = chunk_range(frames_here, table_ref, info_ref)
+    qm[0], qm[1] = split_heads(q_ref[...])
+    dom[0], dom[1] = split_heads(do_ref[...])
+    dqt[...] = jnp.zeros_like(dqt)
+    tiles = query_tiles(rows)
+    work = [(h, at, size) for h in range(2) for at, size in tiles]
+    for at, size in tiles:
+        span = slice(at, at + size)
+        prod = (o_ref[span, :].astype(jnp.float32) * do_ref[span, :].astype(jnp.float32)).T
+        for h in range(2):
+            delta[h : h + 1, span] = jnp.sum(prod[64 * h : 64 * h + 64], axis=0, keepdims=True)
+
+    def prepare(c, carry):
+        span = pl.ds(pl.multiple_of(c * CHUNK, CHUNK), CHUNK)
+        turned = (k_ref[span, :] * valid_ref[span, :]).T
+        for h in range(2):
+            kt[h, :, span] = turned[64 * h : 64 * h + 64]
+        return carry
+
+    lax.fori_loop(low, high, prepare, 0)
+
+    def body(c, carry):
+        span = pl.ds(pl.multiple_of(c * CHUNK, CHUNK), CHUNK)
+        keys = k_ref[span, :]
+        values = v_ref[span, :]
+
+        def scores(item):
+            h, at, size = item
+            return (
+                dot(keys, qm[h, at : at + size, :], NT),
+                dot(values, dom[h, at : at + size, :], NT),
+            )
+
+        dk = jnp.zeros((CHUNK, 128), jnp.float32)
+        dv = jnp.zeros((CHUNK, 128), jnp.float32)
+        ahead = scores(work[0])
+        for i, (h, at, size) in enumerate(work):
+            s, dp = ahead
+            if i + 1 < len(work):
+                ahead = scores(work[i + 1])
+            bias = bias_row(c, split, edge, at, size)
+            p = jnp.exp2(s - (lse_ref[0, h : h + 1, at : at + size] - bias))
+            ds = (p * (dp - delta[h : h + 1, at : at + size])).astype(jnp.bfloat16)
+            dv = dv + dot(p.astype(jnp.bfloat16), dom[h, at : at + size, :])
+            dk = dk + dot(ds, qm[h, at : at + size, :])
+            dqt[h, :, at : at + size] += dot(kt[h, :, span], ds)
+        dk_ref[span, :] = (dk * LN2).astype(jnp.bfloat16)
+        dv_ref[span, :] = dv.astype(jnp.bfloat16)
+        return carry
+
+    lax.fori_loop(low, high, body, 0)
+    for at, size in tiles:
+        both = jnp.concatenate([dqt[0, :, at : at + size], dqt[1, :, at : at + size]], axis=0)
+        dq_ref[at : at + size, :] = (both * 0.125).T.astype(jnp.bfloat16)
+
+
+def attn_bwd(info, table, q, kc, vc, valid, o, do, lse, frames_here, group):
+    rows, width = q.shape
+    length = kc.shape[0]
+    apart = width // 256
+    rowspec = pl.BlockSpec((rows, 128), lambda p, *_: (0, group + apart * p))
+    keyspec = pl.BlockSpec((length, 128), lambda p, *_: (0, group + apart * p))
+    rowout = pl.BlockSpec((rows, 128), lambda p, *_: (0, p))
+    keyout = pl.BlockSpec((length, 128), lambda p, *_: (0, p))
+    return pl.pallas_call(
+        functools.partial(attn_bwd_kernel, frames_here),
+        out_shape=(
+            jax.ShapeDtypeStruct((rows, 256), jnp.bfloat16),
+            jax.ShapeDtypeStruct((length, 256), jnp.bfloat16),
+            jax.ShapeDtypeStruct((length, 256), jnp.bfloat16),
+        ),
+        grid_spec=pltpu.PrefetchScalarGridSpec(
+            num_scalar_prefetch=2,
+            grid=(2,),
+            in_specs=[
+                rowspec,
+                keyspec,
+                keyspec,
+                pl.BlockSpec((length, 128), lambda p, *_: (0, 0)),
+                rowspec,
+                rowspec,
+                pl.BlockSpec((1, 8, rows), lambda p, *_: (group + apart * p, 0, 0)),
+            ],
+            out_specs=[rowout, keyout, keyout],
+            scratch_shapes=[
+                pltpu.VMEM((2, rows, 128), jnp.bfloat16),
+                pltpu.VMEM((2, rows, 128), jnp.bfloat16),
+                pltpu.VMEM((2, 64, length), jnp.bfloat16),
+                pltpu.VMEM((2, 64, rows), jnp.float32),
+                pltpu.VMEM((8, rows), jnp.float32),
+            ],
+        ),
+        compiler_params=pltpu.CompilerParams(
+            vmem_limit_bytes=VMEM_LIMIT, dimension_semantics=("arbitrary",)
+        ),
+        cost_estimate=pl.CostEstimate(flops=int(5e10), bytes_accessed=int(1e7), transcendentals=0),
+        name="attn_bwd",
+    )(info, table, q, kc, vc, valid, o, do, lse)
+
+
+def spread_kernel(frames_here, info_ref, table_ref, dk_ref, dv_ref, ok_ref, ov_ref, xk_ref, xv_ref):
+    total = 2 * frames_here
+    length = info_ref[total]
+    rank = info_ref[total + 1]
+    first = rank * frames_here
+    early = first < length
+    late = first + frames_here > length
+    quad = 4
+    for f0 in range(0, total, quad):
+        side = f0 // frames_here
+        start = f0 % frames_here * PIXELS
+
+        def put(k_out, v_out):
+            for src, dst in ((dk_ref, k_out), (dv_ref, v_out)):
+                parts = []
+                for f in range(f0, f0 + quad):
+                    lo = f % frames_here * PIXELS % 16
+                    at = table_ref[f]
+                    met = jnp.where(f >= length, late, early)
+                    use = (at >= 0) & met
+                    block = src[pl.ds(pl.multiple_of(jnp.maximum(at, 0), 16), FRAME_ROWS), :].astype(jnp.float32)
+                    parts.append(jnp.where(use, block[lo : lo + PIXELS, :], 0.0))
+                dst[start : start + quad * PIXELS, :] = jnp.concatenate(parts, axis=0).astype(jnp.bfloat16)
+
+        @pl.when(rank == side)
+        def _():
+            put(ok_ref, ov_ref)
+
+        @pl.when(rank != side)
+        def _():
+            put(xk_ref, xv_ref)
+
+
+def spread(info, table, dk, dv, frames_here):
+    rows = frames_here * PIXELS
+    width = dk.shape[1]
+    vm = pl.BlockSpec(memory_space=pltpu.VMEM)
+    sm = pl.BlockSpec(memory_space=pltpu.SMEM)
+    one = jax.ShapeDtypeStruct((rows, 256), jnp.bfloat16)
+    return pl.pallas_call(
+        functools.partial(spread_kernel, frames_here),
+        out_shape=(one, one, one, one),
+        in_specs=[sm, sm, vm, vm],
+        out_specs=(vm, vm, vm, vm),
+        compiler_params=pltpu.CompilerParams(vmem_limit_bytes=VMEM_LIMIT),
+        name="spread",
+    )(info, table, dk, dv)
+
+
+TILE = 224
+INV_SQRT2 = 0.7071067811865476
+INV_SQRT_2PI = 0.3989422804014327
+QUERY_SCALE = 0.125 * LOG2E
+
+
+def params(**kw):
+    return pltpu.CompilerParams(
+        vmem_limit_bytes=VMEM_LIMIT, dimension_semantics=("arbitrary",), **kw
+    )
+
+
+def cost(flops, moved):
+    return pl.CostEstimate(flops=int(flops), bytes_accessed=int(moved), transcendentals=0)
+
+
+def tile_spec(width):
+    return pl.BlockSpec((TILE, width), lambda i: (i, 0))
+
+
+def whole_spec(shape):
+    return pl.BlockSpec(shape, lambda i: (0,) * len(shape), pipeline_mode=pl.Buffered(1))
+
+
+def low_shape(rows, width):
+    return jax.ShapeDtypeStruct((rows, width), jnp.bfloat16)
+
+
+def ln_parts(x):
+    center = x - jnp.mean(x, axis=-1, keepdims=True)
+    rstd = lax.rsqrt(jnp.mean(center * center, axis=-1, keepdims=True) + EPS)
+    return center * rstd, rstd
+
+
+def ln_back(dy, gain, xhat, rstd):
+    dxhat = dy * gain
+    along = jnp.mean(dxhat * xhat, axis=-1, keepdims=True)
+    return rstd * (dxhat - jnp.mean(dxhat, axis=-1, keepdims=True) - xhat * along)
+
+
+def rows_sum(x):
+    return jnp.sum(x, axis=0, keepdims=True)
+
+
+def project_kernel(x_ref, gain_ref, shift_ref, w_ref, bias_ref, n_ref, q_ref, k_ref, v_ref):
+    width = x_ref.shape[1]
+    xhat, _ = ln_parts(x_ref[...].astype(jnp.float32))
+    normed = (xhat * gain_ref[...] + shift_ref[...]).astype(jnp.bfloat16)
+    n_ref[...] = normed
+    for i, (out, scale) in enumerate(((q_ref, QUERY_SCALE), (k_ref, None), (v_ref, None))):
+        span = slice(i * width, (i + 1) * width)
+        got = dot(normed, w_ref[:, span]) + bias_ref[:, span]
+        out[...] = (got if scale is None else got * scale).astype(jnp.bfloat16)
+
+
+def project(x, gain, shift, w, bias):
+    rows, width = x.shape
+    return pl.pallas_call(
+        project_kernel,
+        out_shape=(low_shape(rows, width),) * 4,
+        grid=(rows // TILE,),
+        in_specs=[
+            tile_spec(width),
+            whole_spec((1, width)),
+            whole_spec((1, width)),
+            whole_spec(w.shape),
+            whole_spec((1, 3 * width)),
+        ],
+        out_specs=[tile_spec(width)] * 4,
+        compiler_params=params(),
+        cost_estimate=cost(6 * rows * width * width, 10 * rows * width + 6 * width * width),
+        name="project",
+    )(x, gain, shift, w, bias)
+
+
+def mlp_fwd_kernel(
+    x_ref, a_ref, w_out, b_out, gain2, shift2, w_up, b_up, w_down, b_down, gain3, shift3,
+    mid_ref, n2_ref, hid_ref, slope_ref, out_ref, n3_ref,
+):
+    width = x_ref.shape[1]
+    inner = w_up.shape[1]
+    parts = inner // width
+    middle = x_ref[...].astype(jnp.float32) + dot(a_ref[...], w_out[...]) + b_out[...]
+    mid_ref[...] = middle.astype(jnp.bfloat16)
+    xhat, _ = ln_parts(middle)
+    n2 = (xhat * gain2[...] + shift2[...]).astype(jnp.bfloat16)
+    n2_ref[...] = n2
+    out = middle + b_down[...]
+
+    def raise_part(j):
+        span = slice(j * width, (j + 1) * width)
+        return dot(n2, w_up[:, span]) + b_up[:, span]
+
+    ahead = raise_part(0)
+    for j in range(parts):
+        span = slice(j * width, (j + 1) * width)
+        up = ahead
+        if j + 1 < parts:
+            ahead = raise_part(j + 1)
+        area = 0.5 + 0.5 * lax.erf(up * INV_SQRT2)
+        bell = jnp.exp2(up * up * (-0.5 * LOG2E)) * INV_SQRT_2PI
+        hid = (up * area).astype(jnp.bfloat16)
+        hid_ref[:, span] = hid
+        slope_ref[:, span] = (area + up * bell).astype(jnp.bfloat16)
+        out = out + dot(hid, w_down[span, :])
+    out_ref[...] = out.astype(jnp.bfloat16)
+    xhat, _ = ln_parts(out)
+    n3_ref[...] = (xhat * gain3[...] + shift3[...]).astype(jnp.bfloat16)
+
+
+def mlp_fwd(x, attended, w_out, b_out, gain2, shift2, w_up, b_up, w_down, b_down, gain3, shift3):
+    rows, width = x.shape
+    inner = w_up.shape[1]
+    vec = whole_spec((1, width))
+    return pl.pallas_call(
+        mlp_fwd_kernel,
+        out_shape=(
+            low_shape(rows, width), low_shape(rows, width), low_shape(rows, inner),
+            low_shape(rows, inner), low_shape(rows, width), low_shape(rows, width),
+        ),
+        grid=(rows // TILE,),
+        in_specs=[
+            tile_spec(width), tile_spec(width), whole_spec(w_out.shape), vec, vec, vec,
+            whole_spec(w_up.shape), whole_spec((1, inner)), whole_spec(w_down.shape), vec, vec, vec,
+        ],
+        out_specs=[
+            tile_spec(width), tile_spec(width), tile_spec(inner),
+            tile_spec(inner), tile_spec(width), tile_spec(width),
+        ],
+        compiler_params=params(),
+        cost_estimate=cost(
+            2 * rows * width * (width + 2 * inner), 2 * rows * (6 * width + 2 * inner)
+        ),
+        name="mlp_fwd",
+    )(x, attended, w_out, b_out, gain2, shift2, w_up, b_up, w_down, b_down, gain3, shift3)
+
+
+def mlp_bwd_kernel(
+    cot_ref, out_ref, side_ref, pool_ref, w_first, gain3, w_down, slope_ref, w_up, mid_ref,
+    gain2, w_out, ddown_ref, dup_ref, dbranch_ref, datt_ref, sums_ref,
+):
+    width = cot_ref.shape[1]
+    inner = w_up.shape[1]
+    parts = inner // width
+
+    @pl.when(pl.program_id(0) == 0)
+    def _():
+        sums_ref[...] = jnp.zeros_like(sums_ref)
+
+    def add(row, value):
+        sums_ref[row : row + 1, :] += rows_sum(value)
+
+    dn3 = dot(side_ref[:, :128], w_first[...])
+    xhat, rstd = ln_parts(out_ref[...].astype(jnp.float32))
+    add(2, dn3 * xhat)
+    add(3, dn3)
+    d_out = (
+        cot_ref[...].astype(jnp.float32)
+        + ln_back(dn3, gain3[...], xhat, rstd)
+        + dot(side_ref[:, 128:192], pool_ref[...])
+    )
+    d_down = d_out.astype(jnp.bfloat16)
+    ddown_ref[...] = d_down
+    add(4, d_down.astype(jnp.float32))
+
+    def lower_part(j):
+        return dot(d_down, w_down[j * width : (j + 1) * width, :], NT)
+
+    ahead = lower_part(0)
+    dn2 = jnp.zeros(cot_ref.shape, jnp.float32)
+    for j in range(parts):
+        span = slice(j * width, (j + 1) * width)
+        d_hid = ahead
+        if j + 1 < parts:
+            ahead = lower_part(j + 1)
+        d_up = (d_hid * slope_ref[:, span].astype(jnp.float32)).astype(jnp.bfloat16)
+        dup_ref[:, span] = d_up
+        add(6 + j, d_up.astype(jnp.float32))
+        dn2 = dn2 + dot(d_up, w_up[:, span], NT)
+    xhat, rstd = ln_parts(mid_ref[...].astype(jnp.float32))
+    add(0, dn2 * xhat)
+    add(1, dn2)
+    d_branch = (d_out + ln_back(dn2, gain2[...], xhat, rstd)).astype(jnp.bfloat16)
+    dbranch_ref[...] = d_branch
+    add(5, d_branch.astype(jnp.float32))
+    datt_ref[...] = dot(d_branch, w_out[...], NT).astype(jnp.bfloat16)
+
+
+def mlp_bwd(cot, out, side, pool, w_first, gain3, w_down, slope, w_up, mid, gain2, w_out):
+    rows, width = cot.shape
+    inner = w_up.shape[1]
+    vec = whole_spec((1, width))
+    return pl.pallas_call(
+        mlp_bwd_kernel,
+        out_shape=(
+            low_shape(rows, width), low_shape(rows, inner), low_shape(rows, width),
+            low_shape(rows, width), jax.ShapeDtypeStruct((16, width), jnp.float32),
+        ),
+        grid=(rows // TILE,),
+        in_specs=[
+            tile_spec(width), tile_spec(width), tile_spec(256), whole_spec(pool.shape),
+            whole_spec(w_first.shape), vec, whole_spec(w_down.shape), tile_spec(inner),
+            whole_spec(w_up.shape), tile_spec(width), vec, whole_spec(w_out.shape),
+        ],
+        out_specs=[
+            tile_spec(width), tile_spec(inner), tile_spec(width), tile_spec(width),
+            pl.BlockSpec((16, width), lambda i: (0, 0)),
+        ],
+        compiler_params=params(),
+        cost_estimate=cost(
+            2 * rows * width * (width + 2 * inner), 2 * rows * (6 * width + 2 * inner)
+        ),
+        name="mlp_bwd",
+    )(cot, out, side, pool, w_first, gain3, w_down, slope, w_up, mid, gain2, w_out)
+
+
+def final_bwd_kernel(dq_ref, dk_ref, dv_ref, x_ref, branch_ref, gain, w_ref, grad_ref, sums_ref):
+    width = x_ref.shape[1]
+
+    @pl.when(pl.program_id(0) == 0)
+    def _():
+        sums_ref[...] = jnp.zeros_like(sums_ref)
+
+    def add(row, value):
+        sums_ref[row : row + 1, :] += rows_sum(value)
+
+    dn = (
+        dot(dq_ref[...], w_ref[:, :width], NT)
+        + dot(dk_ref[...], w_ref[:, width : 2 * width], NT)
+        + dot(dv_ref[...], w_ref[:, 2 * width :], NT)
+    )
+    xhat, rstd = ln_parts(x_ref[...].astype(jnp.float32))
+    add(0, dn * xhat)
+    add(1, dn)
+    add(2, dq_ref[...].astype(jnp.float32))
+    add(3, dv_ref[...].astype(jnp.float32))
+    grad_ref[...] = (
+        branch_ref[...].astype(jnp.float32) + ln_back(dn, gain[...], xhat, rstd)
+    ).astype(jnp.bfloat16)
+
+
+def final_bwd(dq, dk, dv, x, branch, gain, w):
+    rows, width = x.shape
+    return pl.pallas_call(
+        final_bwd_kernel,
+        out_shape=(low_shape(rows, width), jax.ShapeDtypeStruct((8, width), jnp.float32)),
+        grid=(rows // TILE,),
+        in_specs=[tile_spec(width)] * 5 + [whole_spec((1, width)), whole_spec(w.shape)],
+        out_specs=[tile_spec(width), pl.BlockSpec((8, width), lambda i: (0, 0))],
+        compiler_params=params(),
+        cost_estimate=cost(6 * rows * width * width, 12 * rows * width),
+        name="final_bwd",
+    )(dq, dk, dv, x, branch, gain, w)
+
+
+def grid_masks(frames, lanes):
+    table = np.zeros((16, lanes), np.float32)
+    lane = np.arange(lanes)
+    pixel = lane % PIXELS
+    i, j = pixel // GRID, pixel % GRID
+    inside = lane < frames * PIXELS
+    for a in range(3):
+        for b in range(3):
+            ok = (i + a - 1 >= 0) & (i + a - 1 < GRID) & (j + b - 1 >= 0) & (j + b - 1 < GRID)
+            table[3 * a + b] = ok & inside
+    table[9] = np.where(inside, lane // PIXELS, -1)
+    return table
+
+
+def learner_kernel(
+    frames, info_ref, weight_ref, n3_ref, out_ref, pool_ref, wt_ref, cw_ref, cwt_ref, cb_ref,
+    mask_ref, side_ref, pooled_ref, small_ref, gfirst_ref,
+):
+    rows = n3_ref.shape[0]
+    lanes = mask_ref.shape[1]
+    extra = lanes - rows
+    rank = info_ref[2 * frames + 1]
+    frame_of = mask_ref[9:10, :]
+    live = jnp.zeros((1, lanes), jnp.float32)
+    for f in range(frames):
+        kept = info_ref[rank * frames + f].astype(jnp.float32)
+        live = live + jnp.where(frame_of == f, kept, 0.0)
+    inside = (frame_of >= 0).astype(jnp.float32)
+
+    def widen(x):
+        return jnp.concatenate([x, jnp.zeros((x.shape[0], extra), jnp.float32)], axis=1)
+
+    def turn(x, by):
+        return x if by % lanes == 0 else pltpu.roll(x, by % lanes, 1)
+
+    def gather_taps(taps):
+        total = jnp.zeros((8, lanes), jnp.float32)
+        for t in range(9):
+            step = (t // 3 - 1) * GRID + t % 3 - 1
+            total = total + turn(taps[8 * t : 8 * t + 8, :], -step) * mask_ref[t : t + 1, :]
+        return total
+
+    def spread_taps(level):
+        parts = []
+        for t in range(9):
+            step = (t // 3 - 1) * GRID + t % 3 - 1
+            parts.append(turn(level, step) * mask_ref[8 - t : 9 - t, :])
+        return jnp.concatenate(parts, axis=0)
+
+    def exact(a, b, dims=NN):
+        return lax.dot_general(
+            a, b, dims, precision=HIGHEST, preferred_element_type=jnp.float32
+        )
+
+    def area_of(x):
+        return 0.5 + 0.5 * lax.erf(x * INV_SQRT2)
+
+    taps = widen(dot(wt_ref[...], n3_ref[...], NT))
+    levels = [gather_taps(taps) + cb_ref[:, 0:1]]
+    hiddens = []
+    for n in range(3):
+        hiddens.append(levels[n] * area_of(levels[n]))
+        levels.append(gather_taps(exact(cwt_ref[n], hiddens[n])) + cb_ref[:, n + 1 : n + 2])
+    maps = 1.0 / (1.0 + jnp.exp(-levels[3]))
+    total = rows_sum(maps)
+    meet = 0.5 * (total * total - rows_sum(maps * maps)) * live
+    small_ref[3] = jnp.zeros((8, 128), jnp.float32) + jnp.sum(meet)
+
+    owner = lax.broadcasted_iota(jnp.int32, (8 * frames, lanes), 0) // 8
+    mine = owner.astype(jnp.float32) == frame_of
+    low_maps = maps.astype(jnp.bfloat16).astype(jnp.float32) * live
+    stacked = jnp.where(mine, jnp.concatenate([low_maps] * frames, axis=0), 0.0)
+    out = out_ref[...]
+    pooled_ref[...] = dot(stacked[:, :rows].astype(jnp.bfloat16), out).astype(jnp.bfloat16)
+    pairs = jnp.where(mine, widen(dot(pool_ref[...], out, NT)), 0.0)
+    d_maps = pairs[0:8]
+    for f in range(1, frames):
+        d_maps = d_maps + pairs[8 * f : 8 * f + 8]
+    d_maps = d_maps * live + weight_ref[0] * live * (total - maps)
+    d_level = d_maps * maps * (1.0 - maps)
+    for n in (2, 1, 0):
+        small_ref[4 + n + 1] = jnp.broadcast_to(
+            jnp.sum(d_level, axis=1, keepdims=True), (8, 128)
+        )
+        d_taps = spread_taps(d_level)
+        small_ref[n] = jnp.concatenate(
+            [exact(hiddens[n], d_taps, NT), jnp.zeros((8, 56), jnp.float32)], axis=1
+        )
+        d_hidden = exact(cw_ref[n], d_taps)
+        x = levels[n]
+        bell = jnp.exp(-0.5 * x * x) * INV_SQRT_2PI
+        d_level = d_hidden * (area_of(x) + x * bell) * inside
+    small_ref[4] = jnp.broadcast_to(jnp.sum(d_level, axis=1, keepdims=True), (8, 128))
+    d_first = spread_taps(d_level)[:, :rows]
+    gfirst_ref[...] = dot(d_first.astype(jnp.bfloat16), n3_ref[...])
+    tall = jnp.concatenate(
+        [
+            d_first,
+            jnp.zeros((56, rows), jnp.float32),
+            stacked[:, :rows],
+            jnp.zeros((128 - 8 * frames, rows), jnp.float32),
+        ],
+        axis=0,
+    )
+    side_ref[...] = tall.T.astype(jnp.bfloat16)
+
+
+def learner(info, weight, n3, out, pool, w_first, conv_weights, conv_biases):
+    rows, width = n3.shape
+    frames = rows // PIXELS
+    lanes = -(-rows // 128) * 128
+    vm = pl.BlockSpec(memory_space=pltpu.VMEM)
+    sm = pl.BlockSpec(memory_space=pltpu.SMEM)
+    masks = jnp.asarray(grid_masks(frames, lanes))
+    return pl.pallas_call(
+        functools.partial(learner_kernel, frames),
+        out_shape=(
+            low_shape(rows, 256),
+            low_shape(8 * frames, width),
+            jax.ShapeDtypeStruct((8, 8, 128), jnp.float32),
+            jax.ShapeDtypeStruct((9 * MAPS, width), jnp.float32),
+        ),
+        in_specs=[sm, sm] + [vm] * 8,
+        out_specs=(vm, vm, vm, vm),
+        compiler_params=pltpu.CompilerParams(vmem_limit_bytes=VMEM_LIMIT),
+        cost_estimate=cost(2e10, 4 * rows * width),
+        name="learner",
+    )(
+        info, weight, n3, out, pool, w_first.T, conv_weights,
+        conv_weights.transpose(0, 2, 1), conv_biases.T, masks,
+    )
+
+
+def flip(count, bit):
+    return [(i, i ^ bit) for i in range(count)]
+
+
+def halve_frame(parts, rank):
+    first, second = parts
+    keep = jnp.where(rank == 0, first, second)
+    send = jnp.where(rank == 0, second, first)
+    got = lax.ppermute(send, "frame", flip(2, 1))
+    return (keep.astype(jnp.float32) + got.astype(jnp.float32)).astype(jnp.bfloat16)
+
+
+def halve_seq(x, order):
+    count = lax.axis_size("seq")
+    index = lax.axis_index("seq")
+    bits = count.bit_length() - 1
+    left = list(range(bits))[::-1]
+    x = x.reshape((2,) * bits + x.shape[1:])
+    for bit in order:
+        axis = left.index(bit)
+        left.remove(bit)
+        mine = (index >> bit) & 1
+        keep = lax.dynamic_index_in_dim(x, mine, axis, keepdims=False)
+        send = lax.dynamic_index_in_dim(x, 1 - mine, axis, keepdims=False)
+        got = lax.ppermute(send, "seq", flip(count, 1 << bit))
+        x = (keep.astype(jnp.float32) + got.astype(jnp.float32)).astype(jnp.bfloat16)
+    return x
+
+
+def everywhere(x):
+    count = lax.axis_size("seq")
+    x = x + lax.ppermute(x, "frame", flip(2, 1))
+    bit = 1
+    while bit < count:
+        x = x + lax.ppermute(x, "seq", flip(count, bit))
+        bit *= 2
+    return x
+
+
+def weight_grad(a, b):
+    return dot(a, b, TN).astype(jnp.bfloat16)
+
+
+def orders(bits):
+    low = list(range(bits))
+    return [low[i:] + low[:i] for i in range(3)]
+
+
+def quick_device(
+    tokens, ln_gain_first, ln_bias_first, w_qkv, q_bias, v_bias, w_out, out_bias, ln_gain_second,
+    ln_bias_second, w_up, up_bias, w_down, down_bias, ln_gain_third, ln_bias_third, w_first,
+    conv_weights, conv_biases, clip_lengths, frame_mask, out_cot, pool_cot, penalty_scale,
+):
+    _, rows, width = tokens.shape
+    frames = rows // PIXELS
+    inner = w_up.shape[1]
+    seqs = lax.axis_size("seq")
+    rank = lax.axis_index("frame")
+    share = width // seqs
+    half = width // 2
+    axis_orders = orders(seqs.bit_length() - 1)
+
+    def row(x):
+        return x.reshape(1, -1)
+
+    all_masks = lax.all_gather(frame_mask, "seq", axis=0, tiled=True)
+    count = jnp.sum(all_masks).astype(jnp.float32)
+    weight = (penalty_scale / count).reshape(1)
+    info = jnp.concatenate(
+        [frame_mask[0], clip_lengths[0, 0:1], rank.reshape(1).astype(jnp.int32)]
+    )
+    x = tokens[0]
+    qkv_bias = jnp.concatenate([q_bias, jnp.zeros_like(q_bias), v_bias])
+    n1, q, k, v = project(x, row(ln_gain_first), row(ln_bias_first), w_qkv, row(qkv_bias))
+    far_k = lax.ppermute(k, "frame", flip(2, 1))
+    far_v = lax.ppermute(v, "frame", flip(2, 1))
+    kc, vc, valid, table = compact(info, k, v, far_k, far_v, frames)
+    attended, lse = attn_fwd(info, table, q, kc, vc, valid, frames)
+    mid, n2, hidden, slope, out, n3 = mlp_fwd(
+        x, attended, w_out, row(out_bias), row(ln_gain_second), row(ln_bias_second), w_up,
+        row(up_bias), w_down, row(down_bias), row(ln_gain_third), row(ln_bias_third),
+    )
+    side, pooled, small, grad_first = learner(
+        info, weight, n3, out, pool_cot[0], w_first, conv_weights, conv_biases
+    )
+    first_pad = jnp.concatenate(
+        [w_first.T, jnp.zeros((128 - 9 * MAPS, width), jnp.bfloat16)], axis=0
+    )
+    d_down, d_up, d_branch, d_att, sums = mlp_bwd(
+        out_cot[0], out, side, pool_cot[0], first_pad, row(ln_gain_third), w_down, slope, w_up,
+        mid, row(ln_gain_second), w_out,
+    )
+    def halves(a, b):
+        middle = b.shape[1] // 2
+        return weight_grad(a, b[:, :middle]), weight_grad(a, b[:, middle:])
+
+    up_sum = halve_frame(halves(n2, d_up), rank).reshape(seqs, share, inner // 2)
+    down_sum = halve_frame(halves(hidden, d_down), rank).reshape(seqs, inner // seqs, half)
+    wout_sum = halve_frame(halves(attended, d_branch), rank).reshape(seqs, share, half)
+    grad_first = grad_first.astype(jnp.bfloat16).T
+    columns = grad_first.shape[1] // 2
+    first_sum = halve_frame((grad_first[:, :columns], grad_first[:, columns:]), rank)
+    grad_up = halve_seq(up_sum, axis_orders[0])
+    grad_down = halve_seq(down_sum, axis_orders[1])
+    grad_out = halve_seq(wout_sum, axis_orders[2])
+    grad_first = halve_seq(first_sum.reshape(seqs, share, columns), axis_orders[2])
+    early = everywhere(jnp.concatenate([sums.reshape(-1), small.reshape(-1)]))
+
+    groups = width // 128 // 2
+    parts_q, parts_k, parts_v, parts_w = [], [], [], []
+    for g in range(groups):
+        dq, dkc, dvc = attn_bwd(info, table, q, kc, vc, valid, attended, d_att, lse, frames, g)
+        own_k, own_v, other_k, other_v = spread(info, table, dkc, dvc, frames)
+
+        def joined(own, other):
+            got = lax.ppermute(other, "frame", flip(2, 1))
+            return (own.astype(jnp.float32) + got.astype(jnp.float32)).astype(jnp.bfloat16)
+
+        dk, dv = joined(own_k, other_k), joined(own_v, other_v)
+        parts_q.append(dq)
+        parts_k.append(dk)
+        parts_v.append(dv)
+        pair = (
+            weight_grad(n1, jnp.concatenate([dq, dk[:, :128]], axis=1)),
+            weight_grad(n1, jnp.concatenate([dk[:, 128:], dv], axis=1)),
+        )
+        summed = halve_frame(pair, rank).reshape(seqs, share, 384)
+        parts_w.append(halve_seq(summed, axis_orders[g % 3]))
+
+    def heads(parts):
+        return jnp.concatenate([p[:, :128] for p in parts] + [p[:, 128:] for p in parts], axis=1)
+
+    tokens_grad, late = final_bwd(
+        heads(parts_q), heads(parts_k), heads(parts_v), x, d_branch, row(ln_gain_first), w_qkv
+    )
+    grad_qkv = jnp.concatenate(
+        [p[:, 128 * i : 128 * i + 128] for i in range(3) for p in parts_w], axis=1
+    )
+    late = everywhere(late)
+    sums = early[: 16 * width].reshape(16, width)
+    small = early[16 * width :].reshape(8, 8, 128)
+    penalty = small[3, 0, 0] / count
+    f32 = jnp.float32
+    return (
+        out[None],
+        pooled[None],
+        penalty,
+        tokens_grad[None],
+        late[0],
+        late[1],
+        grad_qkv.astype(f32),
+        late[2],
+        late[3],
+        grad_out.astype(f32),
+        sums[5],
+        sums[0],
+        sums[1],
+        grad_up.astype(f32),
+        sums[6 : 6 + inner // width].reshape(-1),
+        grad_down.astype(f32),
+        sums[4],
+        sums[2],
+        sums[3],
+        grad_first.astype(f32),
+        small[:3, :, : 9 * MAPS],
+        small[4:8, :, 0],
+    )
+
+
+def per_device(*arrays):
+    tokens, clip_lengths = arrays[0], arrays[19]
+    frames = tokens.shape[1] // PIXELS
+    seqs = lax.axis_size("seq")
+    fits = (
+        tokens.shape[0] == 1
+        and lax.axis_size("frame") == 2
+        and frames % 4 == 0
+        and tokens.shape[1] % TILE == 0
+        and tokens.shape[2] == HEADS * HEAD_DIM
+        and seqs & (seqs - 1) == 0
+    )
+    return (quick_device if fits else plain_device)(*arrays)
+
 
 def solution(mesh):
     return jax.shard_map(

time: 2050 us -> 723 us (0.35)
  waiting for transfers between devices: 863 us -> 89 us
  matrix products: 567 us -> 45.6 us
  local copies, waits for them, and re-layouts: 323 us -> 28.8 us
  starting transfers between devices: 1 us -> 290 us
  Pallas kernels: 0 us -> 200 us
  other arithmetic: 167 us -> 18 us
  blocking collectives: 89.8 us -> 42.2 us
    dot_general x34 -> x12, matrix products: 567 us -> 45.6 us  [dot(): return lax.dot_general(a, b, dims, preferred_element_type=jnp.float32)]
    reduce_scatter x6 -> x0, waiting for transfers between devices: 471 us -> none  [the longest x1 142 us: per_device(): lax.psum_scatter(grad_w_up.astype(jnp.bfloat16), 'seq', scatter_dimension...]
    unnamed x18 -> x0, waiting for transfers between devices: 393 us -> none
    ppermute x0 -> x53, starting transfers between devices: none -> 290 us  [the longest x28 266 us: halve_seq(): got = lax.ppermute(send, 'seq', flip(count, 1 << bit))]
    pallas_call x0 -> x13, Pallas kernels: none -> 200 us  [the longest x3 47.6 us: attn_bwd(): pl.pallas_call(functools.partial(attn_bwd_kernel, frames_here), out_shape...]
    unnamed x224 -> x122, local copies, waits for them, and re-layouts: 151 us -> 10.3 us
    ppermute x0 -> x53, waiting for transfers between devices: none -> 89 us  [the longest x28 71.9 us: halve_seq(): got = lax.ppermute(send, 'seq', flip(count, 1 << bit))]
    psum x2 -> x0, blocking collectives: 85.2 us -> none  [per_device(): lax.psum((intersection_local, count_local), ('seq', 'frame'))]
  transfers between devices with their start and end apart: 13 -> 53, of which waited for: 7 -> 29; matrix products, arithmetic and copies ran while one was open for 34% -> 12% of each run, Pallas kernels for 0% -> 4%
where the time goes in v1:
time: 723 us; the launch traced here: 719 us
  starting transfers between devices  290 us (40%)
  Pallas kernels  200 us (28%)
  waiting for transfers between devices  89 us (12%)
  matrix products  45.6 us (6%)
  blocking collectives  42.2 us (6%)
  local copies, waits for them, and re-layouts  28.8 us (4%)
  other arithmetic  18 us (2%)
    ppermute x28, starting transfers between devices, halve_seq(): got = lax.ppermute(send, 'seq', flip(count, 1 << bit))  266 us
    ppermute x28, waiting for transfers between devices, halve_seq(): got = lax.ppermute(send, 'seq', flip(count, 1 << bit))  71.9 us
    pallas_call x3, Pallas kernels, attn_bwd(): pl.pallas_call(functools.partial(attn_bwd_kernel, frames_here), out_shape...  47.6 us
    dot_general x12, matrix products, dot(): return lax.dot_general(a, b, dims, preferred_element_type=jnp.float32)  45.6 us
    all_gather x1, blocking collectives, quick_device(): all_masks = lax.all_gather(frame_mask, 'seq', axis=0, tiled=True)  42.2 us
    pallas_call x1, Pallas kernels, mlp_bwd(): pl.pallas_call(mlp_bwd_kernel, out_shape=(low_shape(rows, width), low_sha...  37.1 us
    pallas_call x1, Pallas kernels, mlp_fwd(): pl.pallas_call(mlp_fwd_kernel, out_shape=(low_shape(rows, width), low_sha...  31.9 us
    pallas_call x1, Pallas kernels, attn_fwd(): pl.pallas_call(functools.partial(attn_fwd_kernel, frames_here), out_shape...  21.9 us
  transfers between devices with their start and end apart: 53, of which 29 were waited for; matrix products, arithmetic and copies ran while one was open for 12% of the time, Pallas kernels for 4%

profile of v1, /device:TPU:0, one launch (start us, length us, event | category | flops | bytes accessed | tf_op | source)
XLA Modules:
  0.0 718.9 jit_solution(10225404616369391506)
XLA Ops:
  4.6 11.5 %project.1 = (bf16[1568,768]{1,0:T(8,128)(2,1)}, bf16[1568,768]{1,0:T(8,128)(2,1)}, bf16[1568,768]{1,0:T(8,128)(2,1)}, bf16[1568,768]{1,0:T(8,128)(2,1)}) custom-call(bf16[1568,768]{1,0:T(8,128)(2,1)} %bitcast.230, f32[1,768]{1,0:T(1,128)} %reshape.171.gain_ref.gain, f32[1,768]{1,0:T(1,128)} %reshape.172.shift_ref, bf16[768,2304]{1,0:T(8,128)(2,1)} %w_ref.3, ...), custom_call_target="tpu_custom_call" | custom-call | flops 5549064192 | bytes 15581184 | tf_op jit(solution)/shard_map/project/pallas_call | solution.py:806
  21.4 42.2 %all-gather = s32[16,1,16]{2,1,0:T(1,128)S(1)} all-gather(s32[1,1,16]{2,1,0:T(1,128)S(1)} %bitcast.226), channel_id=1, replica_groups=mesh['seq'=16,'frame'=2] {'seq'}, dimensions={0}, use_global_device_ids=true | all-gather | bytes 1088 | tf_op jit(solution)/shard_map/all_gather | solution.py:1202
  68.5 10.5 %compact.1 = (bf16[4608,768]{1,0:T(8,128)(2,1)}, bf16[4608,768]{1,0:T(8,128)(2,1)}, bf16[4608,128]{1,0:T(8,128)(2,1)}, s32[18]{0:T(128)}) custom-call(s32[18]{0:T(128)} %pad_add_fusion.info_ref, bf16[1568,768]{1,0:T(8,128)(2,1)} %get-tuple-element.70.own_k, bf16[1568,768]{1,0:T(8,128)(2,1)} %get-tuple-element.71.own_v, bf16[1568,768]{1,0:T(8,128)(2,1)} %copy-done, ...), custom_call_target="tpu_custom_call" | custom-call | tf_op jit(solution)/shard_map/compact/pallas_call | solution.py:458
  79.0 21.9 %attn_fwd.1 = (bf16[1568,768]{1,0:T(8,128)(2,1)}, f32[6,8,1568]{2,1,0:T(8,128)}) custom-call(s32[18]{0:T(128)} %pad_add_fusion.info_ref, s32[18]{0:T(128)} %get-tuple-element.72.table_ref, bf16[1568,768]{1,0:T(8,128)(2,1)} %get-tuple-element.73.q_ref, bf16[4608,768]{1,0:T(8,128)(2,1)} %get-tuple-element.74.k_ref, bf16[4608,768]{1,0:T(8,128)(2,1)} %get-tuple-element.75.v_ref, ...), custom_call_target="tpu_custom_call" | custom-call | flops 80000000000 | bytes 20000000 | tf_op jit(solution)/shard_map/attn_fwd/pallas_call | solution.py:561
  101.0 31.9 %mlp_fwd.1 = (bf16[1568,768]{1,0:T(8,128)(2,1)}, bf16[1568,768]{1,0:T(8,128)(2,1)}, bf16[1568,3072]{1,0:T(8,128)(2,1)}, bf16[1568,3072]{1,0:T(8,128)(2,1)}, bf16...) custom-call(bf16[1568,768]{1,0:T(8,128)(2,1)} %bitcast.231, bf16[1568,768]{1,0:T(8,128)(2,1)} %get-tuple-element.77.a_ref.o_ref, ...), custom_call_target="tpu_custom_call" | custom-call | flops 16647192576 | bytes 33718272 | tf_op jit(solution)/shard_map/mlp_fwd/pallas_call | solution.py:863
  132.8 10.0 %learner.1 = (bf16[1568,256]{1,0:T(8,128)(2,1)}, bf16[64,768]{1,0:T(8,128)(2,1)}, f32[8,8,128]{2,1,0:T(8,128)}, f32[72,768]{1,0:T(8,128)}) custom-call(s32[18]{0:T(128)} %pad_add_fusion.info_ref, f32[1]{0:T(128)} %bitcast.7.weight_ref, bf16[1568,768]{1,0:T(8,128)(2,1)} %get-tuple-element.79.n3_ref, bf16[1568,768]{1,0:T(8,128)(2,1)} %get-tuple-element.78.out_ref, ...), custom_call_target="tpu_custom_call" | custom-call | flops 20000000000 | bytes 4816896 | tf_op jit(solution)/shard_map/learner/pallas_call | solution.py:1118
  142.9 37.1 %mlp_bwd.1 = (bf16[1568,768]{1,0:T(8,128)(2,1)}, bf16[1568,3072]{1,0:T(8,128)(2,1)}, bf16[1568,768]{1,0:T(8,128)(2,1)}, bf16[1568,768]{1,0:T(8,128)(2,1)}, f32[16,768]{1,0:T(8,128)}) custom-call(bf16[1568,768]{1,0:T(8,128)(2,1)} %bitcast.229, bf16[1568,768]{1,0:T(8,128)(2,1)} %get-tuple-element.78.out_ref, bf16[1568,256]{1,0:T(8,128)(2,1)} %get-tuple-element.81.side_ref, ...), custom_call_target="tpu_custom_call" | custom-call | flops 16647192576 | bytes 33718272 | tf_op jit(solution)/shard_map/mlp_bwd/pallas_call | solution.py:941
  180.0 15.6 %attn_bwd.5 = (bf16[1568,256]{1,0:T(8,128)(2,1)}, bf16[4608,256]{1,0:T(8,128)(2,1)}, bf16[4608,256]{1,0:T(8,128)(2,1)}) custom-call(s32[18]{0:T(128)} %pad_add_fusion.info_ref, s32[18]{0:T(128)} %get-tuple-element.72.table_ref, bf16[1568,768]{1,0:T(8,128)(2,1)} %get-tuple-element.73.q_ref, bf16[4608,768]{1,0:T(8,128)(2,1)} %get-tuple-element.74.k_ref, ...), custom_call_target="tpu_custom_call" | custom-call | flops 49999998976 | bytes 10000000 | tf_op jit(solution)/shard_map/attn_bwd/pallas_call | solution.py:664
  195.6 15.9 %attn_bwd.4 = (bf16[1568,256]{1,0:T(8,128)(2,1)}, bf16[4608,256]{1,0:T(8,128)(2,1)}, bf16[4608,256]{1,0:T(8,128)(2,1)}) custom-call(s32[18]{0:T(128)} %pad_add_fusion.info_ref, s32[18]{0:T(128)} %get-tuple-element.72.table_ref, bf16[1568,768]{1,0:T(8,128)(2,1)} %get-tuple-element.73.q_ref, bf16[4608,768]{1,0:T(8,128)(2,1)} %get-tuple-element.74.k_ref, ...), custom_call_target="tpu_custom_call" | custom-call | flops 49999998976 | bytes 10000000 | tf_op jit(solution)/shard_map/attn_bwd/pallas_call | solution.py:664
  211.5 16.2 %attn_bwd.3 = (bf16[1568,256]{1,0:T(8,128)(2,1)}, bf16[4608,256]{1,0:T(8,128)(2,1)}, bf16[4608,256]{1,0:T(8,128)(2,1)}) custom-call(s32[18]{0:T(128)} %pad_add_fusion.info_ref, s32[18]{0:T(128)} %get-tuple-element.72.table_ref, bf16[1568,768]{1,0:T(8,128)(2,1)} %get-tuple-element.73.q_ref, bf16[4608,768]{1,0:T(8,128)(2,1)} %get-tuple-element.74.k_ref, ...), custom_call_target="tpu_custom_call" | custom-call | flops 49999998976 | bytes 10000000 | tf_op jit(solution)/shard_map/attn_bwd/pallas_call | solution.py:664
  232.1 4.9 broadcast_select_fusion.2
  237.1 4.9 fusion.4
  242.0 6.5 broadcast_select_fusion.1
  248.5 6.1 convolution_convert_fusion.1
  254.7 7.8 %broadcast_select_fusion = (bf16[3072,384]{1,0:T(8,128)(2,1)}, bf16[3072,384]{1,0:T(8,128)(2,1)}) fusion(bf16[3072,384]{1,0:T(8,128)(2,1)S(1)} %convolution_convert_fusion.1, pred[]{:T(512)S(6)} %eq.2, bf16[1568,3072]{1,0:T(8,128)(2,1)S(1)} %bitcast.240, bf16[1568,768]{1,0:T(8,128)(2,1)S(1)} %copy-done.46), kind=kOutput, calls=%fused_computation.14 | convolution fusion | flops 3701735424 | bytes 17915904 | tf_op jit(solution)/shard_map/dot_general | solution.py:380
  265.2 71.0 %collective-permute-start.49 = (bf16[2,2,2,48,36]{3,4,1,2,0:T(8,128)(2,1)S(1)}, bf16[2,2,2,48,36]{3,4,1,2,0:T(8,128)(2,1)S(1)}, u32[]{:S(2)}, u32[]{:S(2)}) collective-permute-start(bf16[2,2,2,48,36]{3,4,1,2,0:T(8,128)(2,1)S(1)} %bitcast.224), channel_id=1, source_target_pairs={{0,8},{2,10},{4,12},{6,14},{8,0},{10,2},{12,4},{14,6},{16,24},{18,... | collective-permute-start | bytes 82952 | tf_op jit(solution)/shard_map/ppermute | solution.py:1161
  338.8 91.4 %collective-permute-start.50 = (bf16[2,2,48,36]{2,3,0,1:T(8,128)(2,1)S(1)}, bf16[2,2,48,36]{2,3,0,1:T(8,128)(2,1)S(1)}, u32[]{:S(2)}, u32[]{:S(2)}) collective-permute-start(bf16[2,2,48,36]{2,3,0,1:T(8,128)(2,1)S(1)} %dynamic-slice_bitcast_fusion.14), channel_id=1, source_target_pairs={{0,16},{2,18},{4,20},{6,22},{8,24},{10,26},{12,28},{14,30},{16,0},... | collective-permute-start | bytes 41480 | tf_op jit(solution)/shard_map/ppermute | solution.py:1161
  432.7 76.8 %collective-permute-start.51 = (bf16[2,48,36]{1,2,0:T(8,128)(2,1)S(1)}, bf16[2,48,36]{1,2,0:T(8,128)(2,1)S(1)}, u32[]{:S(2)}, u32[]{:S(2)}) collective-permute-start(bf16[2,48,36]{1,2,0:T(8,128)(2,1)S(1)} %dynamic-slice_bitcast_fusion.19), channel_id=1, source_target_pairs={{0,2},{2,0},{4,6},{6,4},{8,10},{10,8},{12,14},{14,12},{16,18},{18,... | collective-permute-start | bytes 20744 | tf_op jit(solution)/shard_map/ppermute | solution.py:1161
  514.0 12.1 %collective-permute-start.4 = (f32[20480]{0:T(1024)S(1)}, f32[20480]{0:T(1024)S(1)}, u32[]{:S(2)}, u32[]{:S(2)}) collective-permute-start(f32[20480]{0:T(1024)S(1)} %add.253), channel_id=1, source_target_pairs={{0,4},{2,6},{4,0},{6,2},{8,12},{10,14},{12,8},{14,10},{16,20},{18,... | collective-permute-start | bytes 245768 | tf_op jit(solution)/shard_map/ppermute | solution.py:1171
  530.7 4.7 spread.5
  535.4 4.7 spread.3
  540.1 4.7 spread.4
  548.7 4.0 collective-permute-done.6
  571.6 14.9 %final_bwd.1 = (bf16[1568,768]{1,0:T(8,128)(2,1)}, f32[8,768]{1,0:T(8,128)}) custom-call(bf16[1568,768]{1,0:T(8,128)(2,1)} %slice_dynamic-update-slice_fusion.6.dq_ref, bf16[1568,768]{1,0:T(8,128)(2,1)} %constant_dynamic-update-slice_fusion.dk_ref, bf16[1568,768]{1,0:T(8,128)(2,1)} %copy-done.28, bf16[1568,768]{1,0:T(8,128)(2,1)} %bitcast.232, ...), custom_call_target="tpu_custom_call" | custom-call | flops 5549064192 | bytes 14450688 | tf_op jit(solution)/shard_map/final_bwd/pallas_call | solution.py:992
  613.1 6.2 collective-permute-done.19
  623.9 5.4 collective-permute-done.34
  632.7 9.2 %collective-permute-done.30 = bf16[2,2,48,384]{3,2,0,1:T(8,128)(2,1)S(1)} collective-permute-done((bf16[2,2,48,384]{3,2,0,1:T(8,128)(2,1)S(1)}, bf16[2,2,48,384]{3,2,0,1:T(8,128)(2,1)S(1)}, u32[]{:S(2)}, u32[]{:S(2)}) %collective-permute-start.30) | collective-permute-done | bytes 147488 | tf_op jit(solution)/shard_map/ppermute | solution.py:1161
  641.9 4.2 collective-permute-done.35
  665.4 16.7 %collective-permute-done.44 = bf16[2,2,2,192,384]{4,3,2,0,1:T(8,128)(2,1)S(1)} collective-permute-done((bf16[2,2,2,192,384]{4,3,2,0,1:T(8,128)(2,1)S(1)}, bf16[2,2,2,192,384]{4,3,2,0,1:T(8,128)(2,1)S(1)}, u32[]{:S(2)}, u32[]{:S(2)}) %collective-permute-start.44) | collective-permute-done | bytes 1179680 | tf_op jit(solution)/shard_map/ppermute | solution.py:1161
  688.4 6.9 collective-permute-done.45
  700.7 6.1 collective-permute-done.46
  713.0 3.8 collective-permute-done.42
  (342 shorter events, 128.1 us)
Async XLA Ops:
  16.1 51.0 %collective-permute-start = (bf16[1568,768]{1,0:T(8,128)(2,1)}, bf16[1568,768]{1,0:T(8,128)(2,1)S(1)}, u32[]{:S(2)}, u32[]{:S(2)}) collective-permute-start(bf16[1568,768]{1,0:T(8,128)(2,1)} %get-tuple-element.70.own_k), channel_id=1, source_target_pairs={{0,1},{1,0},{2,3},{3,2},{4,5},{5,4},{6,7},{7,6},{8,9},{9,8},{10,11... | collective-permute-start | bytes 7225352 | tf_op jit(solution)/shard_map/ppermute | solution.py:1211
  16.5 50.5 %collective-permute-start.1 = (bf16[1568,768]{1,0:T(8,128)(2,1)}, bf16[1568,768]{1,0:T(8,128)(2,1)}, u32[]{:S(2)}, u32[]{:S(2)}) collective-permute-start(bf16[1568,768]{1,0:T(8,128)(2,1)} %get-tuple-element.71.own_v), channel_id=1, source_target_pairs={{0,1},{1,0},{2,3},{3,2},{4,5},{5,4},{6,7},{7,6},{8,9},{9,8},{10,11... | collective-permute-start | bytes 7225352 | tf_op jit(solution)/shard_map/ppermute | solution.py:1212
  227.7 35.6 %collective-permute-start.48 = (bf16[768,36]{0,1:T(8,128)(2,1)S(1)}, bf16[768,36]{0,1:T(8,128)(2,1)S(1)}, u32[]{:S(2)}, u32[]{:S(2)}) collective-permute-start(bf16[768,36]{0,1:T(8,128)(2,1)S(1)} %broadcast_select_fusion.6), channel_id=1, source_target_pairs={{0,1},{1,0},{2,3},{3,2},{4,5},{5,4},{6,7},{7,6},{8,9},{9,8},{10,11... | collective-permute-start | bytes 165896 | tf_op jit(solution)/shard_map/ppermute | solution.py:1145
  227.8 281.6 %collective-permute-start.2 = (f32[20480]{0:T(1024)S(1)}, f32[20480]{0:T(1024)S(1)}, u32[]{:S(2)}, u32[]{:S(2)}) collective-permute-start(f32[20480]{0:T(1024)S(1)} %pad_maximum_fusion), channel_id=1, source_target_pairs={{0,1},{1,0},{2,3},{3,2},{4,5},{5,4},{6,7},{7,6},{8,9},{9,8},{10,11... | collective-permute-start | bytes 245768 | tf_op jit(solution)/shard_map/ppermute | solution.py:1168
  237.1 319.4 %collective-permute-start.33 = (bf16[768,384]{1,0:T(8,128)(2,1)}, bf16[768,384]{1,0:T(8,128)(2,1)}, u32[]{:S(2)}, u32[]{:S(2)}) collective-permute-start(bf16[768,384]{1,0:T(8,128)(2,1)} %get-tuple-element.157), channel_id=1, source_target_pairs={{0,1},{1,0},{2,3},{3,2},{4,5},{5,4},{6,7},{7,6},{8,9},{9,8},{10,11... | collective-permute-start | bytes 1769480 | tf_op jit(solution)/shard_map/ppermute | solution.py:1145
  262.5 393.0 %collective-permute-start.43 = (bf16[3072,384]{1,0:T(8,128)(2,1)}, bf16[3072,384]{1,0:T(8,128)(2,1)}, u32[]{:S(2)}, u32[]{:S(2)}) collective-permute-start(bf16[3072,384]{1,0:T(8,128)(2,1)} %get-tuple-element.161), channel_id=1, source_target_pairs={{0,1},{1,0},{2,3},{3,2},{4,5},{5,4},{6,7},{7,6},{8,9},{9,8},{10,11... | collective-permute-start | bytes 7077896 | tf_op jit(solution)/shard_map/ppermute | solution.py:1145
  263.0 396.1 %collective-permute-start.38 = (bf16[768,1536]{1,0:T(8,128)(2,1)}, bf16[768,1536]{1,0:T(8,128)(2,1)}, u32[]{:S(2)}, u32[]{:S(2)}) collective-permute-start(bf16[768,1536]{1,0:T(8,128)(2,1)} %get-tuple-element.159), channel_id=1, source_target_pairs={{0,1},{1,0},{2,3},{3,2},{4,5},{5,4},{6,7},{7,6},{8,9},{9,8},{10,11... | collective-permute-start | bytes 7077896 | tf_op jit(solution)/shard_map/ppermute | solution.py:1145
  265.2 73.6 %collective-permute-start.49 = (bf16[2,2,2,48,36]{3,4,1,2,0:T(8,128)(2,1)S(1)}, bf16[2,2,2,48,36]{3,4,1,2,0:T(8,128)(2,1)S(1)}, u32[]{:S(2)}, u32[]{:S(2)}) collective-permute-start(bf16[2,2,2,48,36]{3,4,1,2,0:T(8,128)(2,1)S(1)} %bitcast.224), channel_id=1, source_target_pairs={{0,8},{2,10},{4,12},{6,14},{8,0},{10,2},{12,4},{14,6},{16,24},{18,... | collective-permute-start | bytes 82952 | tf_op jit(solution)/shard_map/ppermute | solution.py:1161
  338.8 93.8 %collective-permute-start.50 = (bf16[2,2,48,36]{2,3,0,1:T(8,128)(2,1)S(1)}, bf16[2,2,48,36]{2,3,0,1:T(8,128)(2,1)S(1)}, u32[]{:S(2)}, u32[]{:S(2)}) collective-permute-start(bf16[2,2,48,36]{2,3,0,1:T(8,128)(2,1)S(1)} %dynamic-slice_bitcast_fusion.14), channel_id=1, source_target_pairs={{0,16},{2,18},{4,20},{6,22},{8,24},{10,26},{12,28},{14,30},{16,0},... | collective-permute-start | bytes 41480 | tf_op jit(solution)/shard_map/ppermute | solution.py:1161
  432.7 78.7 %collective-permute-start.51 = (bf16[2,48,36]{1,2,0:T(8,128)(2,1)S(1)}, bf16[2,48,36]{1,2,0:T(8,128)(2,1)S(1)}, u32[]{:S(2)}, u32[]{:S(2)}) collective-permute-start(bf16[2,48,36]{1,2,0:T(8,128)(2,1)S(1)} %dynamic-slice_bitcast_fusion.19), channel_id=1, source_target_pairs={{0,2},{2,0},{4,6},{6,4},{8,10},{10,8},{12,14},{14,12},{16,18},{18,... | collective-permute-start | bytes 20744 | tf_op jit(solution)/shard_map/ppermute | solution.py:1161
  514.0 14.5 %collective-permute-start.4 = (f32[20480]{0:T(1024)S(1)}, f32[20480]{0:T(1024)S(1)}, u32[]{:S(2)}, u32[]{:S(2)}) collective-permute-start(f32[20480]{0:T(1024)S(1)} %add.253), channel_id=1, source_target_pairs={{0,4},{2,6},{4,0},{6,2},{8,12},{10,14},{12,8},{14,10},{16,20},{18,... | collective-permute-start | bytes 245768 | tf_op jit(solution)/shard_map/ppermute | solution.py:1171
  526.1 18.9 %collective-permute-start.52 = (bf16[48,36]{0,1:T(8,128)(2,1)S(1)}, bf16[48,36]{0,1:T(8,128)(2,1)S(1)}, u32[]{:S(2)}, u32[]{:S(2)}) collective-permute-start(bf16[48,36]{0,1:T(8,128)(2,1)S(1)} %fusion.64), channel_id=1, source_target_pairs={{0,4},{2,6},{4,0},{6,2},{8,12},{10,14},{12,8},{14,10},{16,20},{18,... | collective-permute-start | bytes 10376 | tf_op jit(solution)/shard_map/ppermute | solution.py:1161
  528.5 16.3 %collective-permute-start.5 = (f32[20480]{0:T(1024)S(1)}, f32[20480]{0:T(1024)S(1)}, u32[]{:S(2)}, u32[]{:S(2)}) collective-permute-start(f32[20480]{0:T(1024)S(1)} %add.254), channel_id=1, source_target_pairs={{0,8},{2,10},{4,12},{6,14},{8,0},{10,2},{12,4},{14,6},{16,24},{18,... | collective-permute-start | bytes 245768 | tf_op jit(solution)/shard_map/ppermute | solution.py:1171
  544.8 21.7 %collective-permute-start.9 = (bf16[1568,256]{1,0:T(8,128)(2,1)}, bf16[1568,256]{1,0:T(8,128)(2,1)}, u32[]{:S(2)}, u32[]{:S(2)}) collective-permute-start(bf16[1568,256]{1,0:T(8,128)(2,1)} %get-tuple-element.102), channel_id=1, source_target_pairs={{0,1},{1,0},{2,3},{3,2},{4,5},{5,4},{6,7},{7,6},{8,9},{9,8},{10,11... | collective-permute-start | bytes 2408456 | tf_op jit(solution)/shard_map/ppermute | solution.py:1252
  592.2 17.3 %collective-permute-start.18 = (bf16[768,384]{1,0:T(8,128)(2,1)S(1)}, bf16[768,384]{1,0:T(8,128)(2,1)S(1)}, u32[]{:S(2)}, u32[]{:S(2)}) collective-permute-start(bf16[768,384]{1,0:T(8,128)(2,1)S(1)} %get-tuple-element.151), channel_id=1, source_target_pairs={{0,1},{1,0},{2,3},{3,2},{4,5},{5,4},{6,7},{7,6},{8,9},{9,8},{10,11... | collective-permute-start | bytes 1769480 | tf_op jit(solution)/shard_map/ppermute | solution.py:1145
  600.1 9.9 %collective-permute-start.23 = (bf16[768,384]{1,0:T(8,128)(2,1)S(1)}, bf16[768,384]{1,0:T(8,128)(2,1)S(1)}, u32[]{:S(2)}, u32[]{:S(2)}) collective-permute-start(bf16[768,384]{1,0:T(8,128)(2,1)S(1)} %get-tuple-element.153), channel_id=1, source_target_pairs={{0,1},{1,0},{2,3},{3,2},{4,5},{5,4},{6,7},{7,6},{8,9},{9,8},{10,11... | collective-permute-start | bytes 1769480 | tf_op jit(solution)/shard_map/ppermute | solution.py:1145
  609.9 9.5 %collective-permute-start.19 = (bf16[2,2,2,48,384]{4,3,0,1,2:T(8,128)(2,1)S(1)}, bf16[2,2,2,48,384]{4,3,0,1,2:T(8,128)(2,1)S(1)}, u32[]{:S(2)}, u32[]{:S(2)}) collective-permute-start(bf16[2,2,2,48,384]{4,3,0,1,2:T(8,128)(2,1)S(1)} %bitcast.215), channel_id=1, source_target_pairs={{0,2},{2,0},{4,6},{6,4},{8,10},{10,8},{12,14},{14,12},{16,18},{18,... | collective-permute-start | bytes 884744 | tf_op jit(solution)/shard_map/ppermute | solution.py:1161
  610.4 9.6 %collective-permute-start.24 = (bf16[2,2,2,48,384]{4,3,2,0,1:T(8,128)(2,1)S(1)}, bf16[2,2,2,48,384]{4,3,2,0,1:T(8,128)(2,1)S(1)}, u32[]{:S(2)}, u32[]{:S(2)}) collective-permute-start(bf16[2,2,2,48,384]{4,3,2,0,1:T(8,128)(2,1)S(1)} %bitcast.217), channel_id=1, source_target_pairs={{0,4},{2,6},{4,0},{6,2},{8,12},{10,14},{12,8},{14,10},{16,20},{18,... | collective-permute-start | bytes 884744 | tf_op jit(solution)/shard_map/ppermute | solution.py:1161
  613.0 9.4 %collective-permute-start.29 = (bf16[2,2,2,48,384]{4,3,1,2,0:T(8,128)(2,1)S(1)}, bf16[2,2,2,48,384]{4,3,1,2,0:T(8,128)(2,1)S(1)}, u32[]{:S(2)}, u32[]{:S(2)}) collective-permute-start(bf16[2,2,2,48,384]{4,3,1,2,0:T(8,128)(2,1)S(1)} %bitcast.218), channel_id=1, source_target_pairs={{0,8},{2,10},{4,12},{6,14},{8,0},{10,2},{12,4},{14,6},{16,24},{18,... | collective-permute-start | bytes 884744 | tf_op jit(solution)/shard_map/ppermute | solution.py:1161
  619.4 9.9 %collective-permute-start.34 = (bf16[2,2,2,48,384]{4,3,1,2,0:T(8,128)(2,1)S(1)}, bf16[2,2,2,48,384]{4,3,1,2,0:T(8,128)(2,1)S(1)}, u32[]{:S(2)}, u32[]{:S(2)}) collective-permute-start(bf16[2,2,2,48,384]{4,3,1,2,0:T(8,128)(2,1)S(1)} %bitcast.216), channel_id=1, source_target_pairs={{0,8},{2,10},{4,12},{6,14},{8,0},{10,2},{12,4},{14,6},{16,24},{18,... | collective-permute-start | bytes 884744 | tf_op jit(solution)/shard_map/ppermute | solution.py:1161
  620.1 10.5 %collective-permute-start.20 = (bf16[2,2,48,384]{3,2,0,1:T(8,128)(2,1)S(1)}, bf16[2,2,48,384]{3,2,0,1:T(8,128)(2,1)S(1)}, u32[]{:S(2)}, u32[]{:S(2)}) collective-permute-start(bf16[2,2,48,384]{3,2,0,1:T(8,128)(2,1)S(1)} %dynamic-slice_bitcast_fusion.9), channel_id=1, source_target_pairs={{0,4},{2,6},{4,0},{6,2},{8,12},{10,14},{12,8},{14,10},{16,20},{18,... | collective-permute-start | bytes 442376 | tf_op jit(solution)/shard_map/ppermute | solution.py:1161
  622.4 10.1 %collective-permute-start.25 = (bf16[2,2,48,384]{3,2,1,0:T(8,128)(2,1)S(1)}, bf16[2,2,48,384]{3,2,1,0:T(8,128)(2,1)S(1)}, u32[]{:S(2)}, u32[]{:S(2)}) collective-permute-start(bf16[2,2,48,384]{3,2,1,0:T(8,128)(2,1)S(1)} %dynamic-slice_bitcast_fusion.8), channel_id=1, source_target_pairs={{0,8},{2,10},{4,12},{6,14},{8,0},{10,2},{12,4},{14,6},{16,24},{18,... | collective-permute-start | bytes 442376 | tf_op jit(solution)/shard_map/ppermute | solution.py:1161
  629.3 12.6 %collective-permute-start.30 = (bf16[2,2,48,384]{3,2,0,1:T(8,128)(2,1)S(1)}, bf16[2,2,48,384]{3,2,0,1:T(8,128)(2,1)S(1)}, u32[]{:S(2)}, u32[]{:S(2)}) collective-permute-start(bf16[2,2,48,384]{3,2,0,1:T(8,128)(2,1)S(1)} %dynamic-slice_bitcast_fusion.7), channel_id=1, source_target_pairs={{0,16},{2,18},{4,20},{6,22},{8,24},{10,26},{12,28},{14,30},{16,0},... | collective-permute-start | bytes 442376 | tf_op jit(solution)/shard_map/ppermute | solution.py:1161
  630.6 15.5 %collective-permute-start.35 = (bf16[2,2,48,384]{3,2,0,1:T(8,128)(2,1)S(1)}, bf16[2,2,48,384]{3,2,0,1:T(8,128)(2,1)S(1)}, u32[]{:S(2)}, u32[]{:S(2)}) collective-permute-start(bf16[2,2,48,384]{3,2,0,1:T(8,128)(2,1)S(1)} %dynamic-slice_bitcast_fusion.6), channel_id=1, source_target_pairs={{0,16},{2,18},{4,20},{6,22},{8,24},{10,26},{12,28},{14,30},{16,0},... | collective-permute-start | bytes 442376 | tf_op jit(solution)/shard_map/ppermute | solution.py:1161
  632.5 14.5 %collective-permute-start.21 = (bf16[2,48,384]{2,1,0:T(8,128)(2,1)S(1)}, bf16[2,48,384]{2,1,0:T(8,128)(2,1)S(1)}, u32[]{:S(2)}, u32[]{:S(2)}) collective-permute-start(bf16[2,48,384]{2,1,0:T(8,128)(2,1)S(1)} %dynamic-slice_bitcast_fusion.13), channel_id=1, source_target_pairs={{0,8},{2,10},{4,12},{6,14},{8,0},{10,2},{12,4},{14,6},{16,24},{18,... | collective-permute-start | bytes 221192 | tf_op jit(solution)/shard_map/ppermute | solution.py:1161
  653.3 34.5 %collective-permute-start.37 = (bf16[48,384]{1,0:T(8,128)(2,1)S(1)}, bf16[48,384]{1,0:T(8,128)(2,1)S(1)}, u32[]{:S(2)}, u32[]{:S(2)}) collective-permute-start(bf16[48,384]{1,0:T(8,128)(2,1)S(1)} %dynamic-slice_bitcast_fusion.15), channel_id=1, source_target_pairs={{0,4},{2,6},{4,0},{6,2},{8,12},{10,14},{12,8},{14,10},{16,20},{18,... | collective-permute-start | bytes 110600 | tf_op jit(solution)/shard_map/ppermute | solution.py:1161
  658.7 23.3 %collective-permute-start.44 = (bf16[2,2,2,192,384]{4,3,2,0,1:T(8,128)(2,1)S(1)}, bf16[2,2,2,192,384]{4,3,2,0,1:T(8,128)(2,1)S(1)}, u32[]{:S(2)}, u32[]{:S(2)}) collective-permute-start(bf16[2,2,2,192,384]{4,3,2,0,1:T(8,128)(2,1)S(1)} %bitcast.213), channel_id=1, source_target_pairs={{0,4},{2,6},{4,0},{6,2},{8,12},{10,14},{12,8},{14,10},{16,20},{18,... | collective-permute-start | bytes 3538952 | tf_op jit(solution)/shard_map/ppermute | solution.py:1161
  663.3 22.9 %collective-permute-start.39 = (bf16[2,2,2,48,1536]{4,3,0,1,2:T(8,128)(2,1)S(1)}, bf16[2,2,2,48,1536]{4,3,0,1,2:T(8,128)(2,1)S(1)}, u32[]{:S(2)}, u32[]{:S(2)}) collective-permute-start(bf16[2,2,2,48,1536]{4,3,0,1,2:T(8,128)(2,1)S(1)} %bitcast.214), channel_id=1, source_target_pairs={{0,2},{2,0},{4,6},{6,4},{8,10},{10,8},{12,14},{14,12},{16,18},{18,... | collective-permute-start | bytes 3538952 | tf_op jit(solution)/shard_map/ppermute | solution.py:1161
  682.4 12.8 %collective-permute-start.45 = (bf16[2,2,192,384]{3,2,1,0:T(8,128)(2,1)S(1)}, bf16[2,2,192,384]{3,2,1,0:T(8,128)(2,1)S(1)}, u32[]{:S(2)}, u32[]{:S(2)}) collective-permute-start(bf16[2,2,192,384]{3,2,1,0:T(8,128)(2,1)S(1)} %dynamic-slice_bitcast_fusion), channel_id=1, source_target_pairs={{0,8},{2,10},{4,12},{6,14},{8,0},{10,2},{12,4},{14,6},{16,24},{18,... | collective-permute-start | bytes 1769480 | tf_op jit(solution)/shard_map/ppermute | solution.py:1161
  686.6 12.4 %collective-permute-start.40 = (bf16[2,2,48,1536]{3,2,0,1:T(8,128)(2,1)S(1)}, bf16[2,2,48,1536]{3,2,0,1:T(8,128)(2,1)S(1)}, u32[]{:S(2)}, u32[]{:S(2)}) collective-permute-start(bf16[2,2,48,1536]{3,2,0,1:T(8,128)(2,1)S(1)} %dynamic-slice_bitcast_fusion.1), channel_id=1, source_target_pairs={{0,4},{2,6},{4,0},{6,2},{8,12},{10,14},{12,8},{14,10},{16,20},{18,... | collective-permute-start | bytes 1769480 | tf_op jit(solution)/shard_map/ppermute | solution.py:1161
  695.4 11.4 %collective-permute-start.46 = (bf16[2,192,384]{2,1,0:T(8,128)(2,1)S(1)}, bf16[2,192,384]{2,1,0:T(8,128)(2,1)S(1)}, u32[]{:S(2)}, u32[]{:S(2)}) collective-permute-start(bf16[2,192,384]{2,1,0:T(8,128)(2,1)S(1)} %dynamic-slice_bitcast_fusion.2), channel_id=1, source_target_pairs={{0,16},{2,18},{4,20},{6,22},{8,24},{10,26},{12,28},{14,30},{16,0},... | collective-permute-start | bytes 884744 | tf_op jit(solution)/shard_map/ppermute | solution.py:1161
  699.1 9.7 %collective-permute-start.41 = (bf16[2,48,1536]{2,1,0:T(8,128)(2,1)S(1)}, bf16[2,48,1536]{2,1,0:T(8,128)(2,1)S(1)}, u32[]{:S(2)}, u32[]{:S(2)}) collective-permute-start(bf16[2,48,1536]{2,1,0:T(8,128)(2,1)S(1)} %dynamic-slice_bitcast_fusion.3), channel_id=1, source_target_pairs={{0,8},{2,10},{4,12},{6,14},{8,0},{10,2},{12,4},{14,6},{16,24},{18,... | collective-permute-start | bytes 884744 | tf_op jit(solution)/shard_map/ppermute | solution.py:1161
  (71 other events, 677.6 us)

commit v2 on v1

--- a/solution.py
+++ b/solution.py
@@ -381,14 +381,13 @@
 
 
 def compact_rows(frame_total):
-    chunks = -(-frame_total * FRAME_ROWS // CHUNK) + 1
+    chunks = -(-frame_total * FRAME_ROWS // CHUNK) + 2
     return chunks * CHUNK
 
 
-def compact_kernel(frames_here, info_ref, own_k, own_v, other_k, other_v, kc_ref, vc_ref, valid_ref, table_ref):
+def key_places(frames_here, info_ref):
     total = 2 * frames_here
     length = info_ref[total]
-    rank = info_ref[total + 1]
     count = [jnp.int32(0), jnp.int32(0)]
     places = []
     for f in range(total):
@@ -398,36 +397,54 @@
         count[0] = count[0] + kept * (1 - late)
         count[1] = count[1] + kept * late
     chunks = [(c * FRAME_ROWS + CHUNK - 1) // CHUNK for c in count]
-    base = [jnp.int32(0), chunks[0] * CHUNK]
-    table_ref[total] = chunks[0]
-    table_ref[total + 1] = chunks[0] + chunks[1]
+    start = chunks[0] * CHUNK
+    starts = [
+        (kept, pl.multiple_of(jnp.where(late == 1, start, 0) + place * FRAME_ROWS, 16))
+        for kept, late, place in places
+    ]
+    tails = [
+        pl.multiple_of(count[0] * FRAME_ROWS, 16),
+        pl.multiple_of(start + count[1] * FRAME_ROWS, 16),
+    ]
+    return starts, tails, chunks[0], chunks[0] + chunks[1]
+
+
+def chunk_range(frames_here, split, end, info_ref):
+    total = 2 * frames_here
+    length = info_ref[total]
+    first = info_ref[total + 1] * frames_here
+    low = jnp.where(first >= length, split, 0)
+    high = jnp.where(first + frames_here <= length, split, end)
+    edge = jnp.clip((length - first) * PIXELS, 0, frames_here * PIXELS)
+    return low, high, edge
+
+
+def gather_keys(frames_here, info_ref, starts, tails, own_k, own_v, far_k, far_v, kc, vc, valid):
+    total = 2 * frames_here
+    length = info_ref[total]
+    rank = info_ref[total + 1]
     width = own_k.shape[1]
-    zeros = jnp.zeros((CHUNK, width), jnp.bfloat16)
-    valid_ref[...] = jnp.zeros_like(valid_ref)
     row = lax.broadcasted_iota(jnp.int32, (FRAME_ROWS, width), 0)
 
     def first_row(f):
-        side = f // frames_here
         local = f % frames_here
         start = local * PIXELS // 16 * 16
-        a = own_k[start : start + 16, :].astype(jnp.float32)
-        b = other_k[start : start + 16, :].astype(jnp.float32)
-        block = jnp.where(rank == side, a, b)
         at = local * PIXELS - start
-        return block[at : at + 1, :]
+        a = own_k[start : start + 16, :].astype(jnp.float32)[at : at + 1, :]
+        b = far_k[start : start + 16, :].astype(jnp.float32)[at : at + 1, :]
+        return jnp.where(rank == f // frames_here, a, b)
 
     fills = [first_row(0), first_row(total // 2)]
     for f in range(total // 2 + 1, total):
         if (f * PIXELS) % 16 == 0:
             fills[1] = jnp.where(length == f, first_row(f), fills[1])
     for s in range(2):
-        at = pl.multiple_of(base[s] + count[s] * FRAME_ROWS, 16)
-        kc_ref[pl.ds(at, CHUNK), :] = jnp.broadcast_to(fills[s], (CHUNK, width)).astype(jnp.bfloat16)
-        vc_ref[pl.ds(at, CHUNK), :] = zeros
+        span = pl.ds(tails[s], CHUNK)
+        kc[span, :] = jnp.broadcast_to(fills[s], (CHUNK, width)).astype(jnp.bfloat16)
+        vc[span, :] = jnp.zeros((CHUNK, width), jnp.bfloat16)
+        valid[span, :] = jnp.zeros((CHUNK, 128), jnp.bfloat16)
     for f in range(total):
-        kept, late, place = places[f]
-        at = pl.multiple_of(jnp.where(late == 1, base[1], base[0]) + place * FRAME_ROWS, 16)
-        table_ref[f] = jnp.where(kept == 1, at, -1)
+        kept, at = starts[f]
         side = f // frames_here
         local = f % frames_here
         start = local * PIXELS // 16 * 16
@@ -437,9 +454,10 @@
         def put(k_ref, v_ref):
             k = k_ref[start : start + FRAME_ROWS, :].astype(jnp.float32)
             v = v_ref[start : start + FRAME_ROWS, :].astype(jnp.float32)
-            kc_ref[pl.ds(at, FRAME_ROWS), :] = jnp.where(inside, k, k[lo : lo + 1, :]).astype(jnp.bfloat16)
-            vc_ref[pl.ds(at, FRAME_ROWS), :] = jnp.where(inside, v, 0.0).astype(jnp.bfloat16)
-            valid_ref[pl.ds(at, FRAME_ROWS), :] = inside[:, :128].astype(jnp.bfloat16)
+            span = pl.ds(at, FRAME_ROWS)
+            kc[span, :] = jnp.where(inside, k, k[lo : lo + 1, :]).astype(jnp.bfloat16)
+            vc[span, :] = jnp.where(inside, v, 0.0).astype(jnp.bfloat16)
+            valid[span, :] = inside.astype(jnp.bfloat16)
 
         @pl.when((kept == 1) & (rank == side))
         def _():
@@ -447,27 +465,7 @@
 
         @pl.when((kept == 1) & (rank != side))
         def _():
-            put(other_k, other_v)
-
-
-def compact(info, own_k, own_v, other_k, other_v, frames_here):
-    rows, width = own_k.shape
-    length = compact_rows(2 * frames_here)
-    vm = pl.BlockSpec(memory_space=pltpu.VMEM)
-    sm = pl.BlockSpec(memory_space=pltpu.SMEM)
-    return pl.pallas_call(
-        functools.partial(compact_kernel, frames_here),
-        out_shape=(
-            jax.ShapeDtypeStruct((length + CHUNK, width), jnp.bfloat16),
-            jax.ShapeDtypeStruct((length + CHUNK, width), jnp.bfloat16),
-            jax.ShapeDtypeStruct((length + CHUNK, 128), jnp.bfloat16),
-            jax.ShapeDtypeStruct((2 * frames_here + 2,), jnp.int32),
-        ),
-        in_specs=[sm, vm, vm, vm, vm],
-        out_specs=(vm, vm, vm, sm),
-        compiler_params=pltpu.CompilerParams(vmem_limit_bytes=VMEM_LIMIT),
-        name="compact",
-    )(info, own_k, own_v, other_k, other_v)
+            put(far_k, far_v)
 
 
 def query_tiles(rows):
@@ -478,17 +476,6 @@
     return tiles
 
 
-def chunk_range(frames_here, table_ref, info_ref):
-    total = 2 * frames_here
-    length = info_ref[total]
-    rank = info_ref[total + 1]
-    first = rank * frames_here
-    low = jnp.where(first >= length, table_ref[total], 0)
-    high = jnp.where(first + frames_here <= length, table_ref[total], table_ref[total + 1])
-    edge = jnp.clip((length - first) * PIXELS, 0, frames_here * PIXELS)
-    return low, high, table_ref[total], edge
-
-
 def split_heads(rows):
     lane = lax.broadcasted_iota(jnp.int32, rows.shape, 1)
     zero = jnp.zeros_like(rows)
@@ -501,9 +488,16 @@
     return jnp.where(same, 0.0, FAR)
 
 
-def attn_fwd_kernel(frames_here, info_ref, table_ref, q_ref, k_ref, v_ref, valid_ref, o_ref, lse_ref, qm, vt, acc, top):
+def attn_fwd_kernel(
+    frames_here, info_ref, q_ref, own_k, own_v, far_k, far_v, o_ref, lse_ref, kc_ref, vc_ref,
+    valid_ref, qm, vt, acc, top,
+):
     rows = q_ref.shape[0]
-    low, high, split, edge = chunk_range(frames_here, table_ref, info_ref)
+    starts, tails, split, end = key_places(frames_here, info_ref)
+    low, high, edge = chunk_range(frames_here, split, end, info_ref)
+    gather_keys(
+        frames_here, info_ref, starts, tails, own_k, own_v, far_k, far_v, kc_ref, vc_ref, valid_ref
+    )
     qm[0], qm[1] = split_heads(q_ref[...])
     acc[...] = jnp.zeros_like(acc)
     top[...] = jnp.full_like(top, NEG)
@@ -512,7 +506,7 @@
 
     def prepare(c, carry):
         span = pl.ds(pl.multiple_of(c * CHUNK, CHUNK), CHUNK)
-        turned = v_ref[span, :].T
+        turned = vc_ref[span, :].T
         ones = valid_ref[span, :].T[:16]
         for h in range(2):
             vt[h, 0:64, span] = turned[64 * h : 64 * h + 64]
@@ -523,7 +517,7 @@
 
     def body(c, carry):
         span = pl.ds(pl.multiple_of(c * CHUNK, CHUNK), CHUNK)
-        keys = k_ref[span, :]
+        keys = kc_ref[span, :]
 
         def scores(item):
             h, at, size = item
@@ -554,28 +548,37 @@
         o_ref[at : at + size, :] = jnp.concatenate(halves, axis=0).T.astype(jnp.bfloat16)
 
 
-def attn_fwd(info, table, q, kc, vc, valid, frames_here):
+def attn_fwd(info, q, own_k, own_v, far_k, far_v, old, part, frames_here):
     rows, width = q.shape
-    length = kc.shape[0]
-    pairs = width // 128
+    pairs = width // 256
+    length = compact_rows(2 * frames_here)
+    block = pl.BlockSpec((rows, 128), lambda p, *_: (0, p))
+    column = pl.BlockSpec((rows, 128), lambda p, *_: (0, p + part * pairs))
+    keys = pl.BlockSpec((length, 128), lambda p, *_: (0, p))
+    olds = [] if old is None else [old]
+
+    def kernel(*refs):
+        return attn_fwd_kernel(frames_here, *refs[:6], *refs[6 + len(olds) :])
+
     return pl.pallas_call(
-        functools.partial(attn_fwd_kernel, frames_here),
+        kernel,
         out_shape=(
             jax.ShapeDtypeStruct((rows, width), jnp.bfloat16),
             jax.ShapeDtypeStruct((pairs, 8, rows), jnp.float32),
+            jax.ShapeDtypeStruct((length, width // 2), jnp.bfloat16),
+            jax.ShapeDtypeStruct((length, width // 2), jnp.bfloat16),
+            jax.ShapeDtypeStruct((length, 128), jnp.bfloat16),
         ),
         grid_spec=pltpu.PrefetchScalarGridSpec(
-            num_scalar_prefetch=2,
+            num_scalar_prefetch=1,
             grid=(pairs,),
-            in_specs=[
-                pl.BlockSpec((rows, 128), lambda p, *_: (0, p)),
-                pl.BlockSpec((length, 128), lambda p, *_: (0, p)),
-                pl.BlockSpec((length, 128), lambda p, *_: (0, p)),
+            in_specs=[column, block, block, block, block] + [pl.BlockSpec(memory_space=pl.ANY)] * len(olds),
+            out_specs=[
+                column,
+                pl.BlockSpec((1, 8, rows), lambda p, *_: (p, 0, 0)),
+                keys,
+                keys,
                 pl.BlockSpec((length, 128), lambda p, *_: (0, 0)),
-            ],
-            out_specs=[
-                pl.BlockSpec((rows, 128), lambda p, *_: (0, p)),
-                pl.BlockSpec((1, 8, rows), lambda p, *_: (p, 0, 0)),
             ],
             scratch_shapes=[
                 pltpu.VMEM((2, rows, 128), jnp.bfloat16),
@@ -584,20 +587,23 @@
                 pltpu.VMEM((8, rows), jnp.float32),
             ],
         ),
-        compiler_params=pltpu.CompilerParams(
-            vmem_limit_bytes=VMEM_LIMIT, dimension_semantics=("arbitrary",)
-        ),
-        cost_estimate=pl.CostEstimate(flops=int(8e10), bytes_accessed=int(2e7), transcendentals=0),
+        input_output_aliases={6: 0} if olds else {},
+        compiler_params=params(),
+        cost_estimate=cost(4e10, 1e7),
         name="attn_fwd",
-    )(info, table, q, kc, vc, valid)
+    )(info, q, own_k, own_v, far_k, far_v, *olds)
 
 
 def attn_bwd_kernel(
-    frames_here, info_ref, table_ref, q_ref, k_ref, v_ref, valid_ref, o_ref, do_ref, lse_ref,
-    dq_ref, dk_ref, dv_ref, qm, dom, kt, dqt, delta,
+    frames_here, info_ref, q_ref, k_ref, v_ref, valid_ref, o_ref, do_ref, lse_ref,
+    dq_ref, own_dk, own_dv, far_dk, far_dv, qm, dom, kt, dqt, delta, dk_all, dv_all,
 ):
     rows = q_ref.shape[0]
-    low, high, split, edge = chunk_range(frames_here, table_ref, info_ref)
+    total = 2 * frames_here
+    length = info_ref[total]
+    rank = info_ref[total + 1]
+    starts, _, split, end = key_places(frames_here, info_ref)
+    low, high, edge = chunk_range(frames_here, split, end, info_ref)
     qm[0], qm[1] = split_heads(q_ref[...])
     dom[0], dom[1] = split_heads(do_ref[...])
     dqt[...] = jnp.zeros_like(dqt)
@@ -643,8 +649,8 @@
             dv = dv + dot(p.astype(jnp.bfloat16), dom[h, at : at + size, :])
             dk = dk + dot(ds, qm[h, at : at + size, :])
             dqt[h, :, at : at + size] += dot(kt[h, :, span], ds)
-        dk_ref[span, :] = (dk * LN2).astype(jnp.bfloat16)
-        dv_ref[span, :] = dv.astype(jnp.bfloat16)
+        dk_all[span, :] = (dk * LN2).astype(jnp.bfloat16)
+        dv_all[span, :] = dv.astype(jnp.bfloat16)
         return carry
 
     lax.fori_loop(low, high, body, 0)
@@ -652,25 +658,52 @@
         both = jnp.concatenate([dqt[0, :, at : at + size], dqt[1, :, at : at + size]], axis=0)
         dq_ref[at : at + size, :] = (both * 0.125).T.astype(jnp.bfloat16)
 
-
-def attn_bwd(info, table, q, kc, vc, valid, o, do, lse, frames_here, group):
+    first = rank * frames_here
+    early = first < length
+    late = first + frames_here > length
+    quad = 4
+    for f0 in range(0, total, quad):
+        at0 = f0 % frames_here * PIXELS
+
+        def put(k_out, v_out):
+            for src, dst in ((dk_all, k_out), (dv_all, v_out)):
+                parts = []
+                for f in range(f0, f0 + quad):
+                    kept, at = starts[f]
+                    lo = f % frames_here * PIXELS % 16
+                    use = (kept == 1) & jnp.where(f >= length, late, early)
+                    block = src[pl.ds(at, FRAME_ROWS), :].astype(jnp.float32)
+                    parts.append(jnp.where(use, block[lo : lo + PIXELS, :], 0.0))
+                dst[at0 : at0 + quad * PIXELS, :] = jnp.concatenate(parts, axis=0).astype(
+                    jnp.bfloat16
+                )
+
+        @pl.when(rank == f0 // frames_here)
+        def _():
+            put(own_dk, own_dv)
+
+        @pl.when(rank != f0 // frames_here)
+        def _():
+            put(far_dk, far_dv)
+
+
+def attn_bwd(info, q, kc, vc, valid, o, do, lse, pair, frames_here, after):
     rows, width = q.shape
     length = kc.shape[0]
-    apart = width // 256
-    rowspec = pl.BlockSpec((rows, 128), lambda p, *_: (0, group + apart * p))
-    keyspec = pl.BlockSpec((length, 128), lambda p, *_: (0, group + apart * p))
-    rowout = pl.BlockSpec((rows, 128), lambda p, *_: (0, p))
-    keyout = pl.BlockSpec((length, 128), lambda p, *_: (0, p))
+    local = pair % (width // 256)
+    rowspec = pl.BlockSpec((rows, 128), lambda p, *_: (0, pair))
+    keyspec = pl.BlockSpec((length, 128), lambda p, *_: (0, local))
+    whole = pl.BlockSpec((rows, 128), lambda p, *_: (0, 0))
+
+    def kernel(*refs):
+        return attn_bwd_kernel(frames_here, *refs[:8], *refs[8 + len(after) :])
+
     return pl.pallas_call(
-        functools.partial(attn_bwd_kernel, frames_here),
-        out_shape=(
-            jax.ShapeDtypeStruct((rows, 256), jnp.bfloat16),
-            jax.ShapeDtypeStruct((length, 256), jnp.bfloat16),
-            jax.ShapeDtypeStruct((length, 256), jnp.bfloat16),
-        ),
+        kernel,
+        out_shape=(jax.ShapeDtypeStruct((rows, 128), jnp.bfloat16),) * 5,
         grid_spec=pltpu.PrefetchScalarGridSpec(
-            num_scalar_prefetch=2,
-            grid=(2,),
+            num_scalar_prefetch=1,
+            grid=(1,),
             in_specs=[
                 rowspec,
                 keyspec,
@@ -678,72 +711,24 @@
                 pl.BlockSpec((length, 128), lambda p, *_: (0, 0)),
                 rowspec,
                 rowspec,
-                pl.BlockSpec((1, 8, rows), lambda p, *_: (group + apart * p, 0, 0)),
-            ],
-            out_specs=[rowout, keyout, keyout],
+                pl.BlockSpec((1, 8, rows), lambda p, *_: (local, 0, 0)),
+            ]
+            + [pl.BlockSpec(memory_space=pl.ANY)] * len(after),
+            out_specs=[whole] * 5,
             scratch_shapes=[
                 pltpu.VMEM((2, rows, 128), jnp.bfloat16),
                 pltpu.VMEM((2, rows, 128), jnp.bfloat16),
                 pltpu.VMEM((2, 64, length), jnp.bfloat16),
                 pltpu.VMEM((2, 64, rows), jnp.float32),
                 pltpu.VMEM((8, rows), jnp.float32),
+                pltpu.VMEM((length, 128), jnp.bfloat16),
+                pltpu.VMEM((length, 128), jnp.bfloat16),
             ],
         ),
-        compiler_params=pltpu.CompilerParams(
-            vmem_limit_bytes=VMEM_LIMIT, dimension_semantics=("arbitrary",)
-        ),
-        cost_estimate=pl.CostEstimate(flops=int(5e10), bytes_accessed=int(1e7), transcendentals=0),
+        compiler_params=params(),
+        cost_estimate=cost(3e10, 1e7),
         name="attn_bwd",
-    )(info, table, q, kc, vc, valid, o, do, lse)
-
-
-def spread_kernel(frames_here, info_ref, table_ref, dk_ref, dv_ref, ok_ref, ov_ref, xk_ref, xv_ref):
-    total = 2 * frames_here
-    length = info_ref[total]
-    rank = info_ref[total + 1]
-    first = rank * frames_here
-    early = first < length
-    late = first + frames_here > length
-    quad = 4
-    for f0 in range(0, total, quad):
-        side = f0 // frames_here
-        start = f0 % frames_here * PIXELS
-
-        def put(k_out, v_out):
-            for src, dst in ((dk_ref, k_out), (dv_ref, v_out)):
-                parts = []
-                for f in range(f0, f0 + quad):
-                    lo = f % frames_here * PIXELS % 16
-                    at = table_ref[f]
-                    met = jnp.where(f >= length, late, early)
-                    use = (at >= 0) & met
-                    block = src[pl.ds(pl.multiple_of(jnp.maximum(at, 0), 16), FRAME_ROWS), :].astype(jnp.float32)
-                    parts.append(jnp.where(use, block[lo : lo + PIXELS, :], 0.0))
-                dst[start : start + quad * PIXELS, :] = jnp.concatenate(parts, axis=0).astype(jnp.bfloat16)
-
-        @pl.when(rank == side)
-        def _():
-            put(ok_ref, ov_ref)
-
-        @pl.when(rank != side)
-        def _():
-            put(xk_ref, xv_ref)
-
-
-def spread(info, table, dk, dv, frames_here):
-    rows = frames_here * PIXELS
-    width = dk.shape[1]
-    vm = pl.BlockSpec(memory_space=pltpu.VMEM)
-    sm = pl.BlockSpec(memory_space=pltpu.SMEM)
-    one = jax.ShapeDtypeStruct((rows, 256), jnp.bfloat16)
-    return pl.pallas_call(
-        functools.partial(spread_kernel, frames_here),
-        out_shape=(one, one, one, one),
-        in_specs=[sm, sm, vm, vm],
-        out_specs=(vm, vm, vm, vm),
-        compiler_params=pltpu.CompilerParams(vmem_limit_bytes=VMEM_LIMIT),
-        name="spread",
-    )(info, table, dk, dv)
+    )(info, q, kc, vc, valid, o, do, lse, *after)
 
 
 TILE = 224
@@ -790,35 +775,67 @@
     return jnp.sum(x, axis=0, keepdims=True)
 
 
-def project_kernel(x_ref, gain_ref, shift_ref, w_ref, bias_ref, n_ref, q_ref, k_ref, v_ref):
-    width = x_ref.shape[1]
+def project_kernel(x_ref, gain_ref, shift_ref, wk, wv, bias_ref, n_ref, k_ref, v_ref):
     xhat, _ = ln_parts(x_ref[...].astype(jnp.float32))
     normed = (xhat * gain_ref[...] + shift_ref[...]).astype(jnp.bfloat16)
     n_ref[...] = normed
-    for i, (out, scale) in enumerate(((q_ref, QUERY_SCALE), (k_ref, None), (v_ref, None))):
-        span = slice(i * width, (i + 1) * width)
-        got = dot(normed, w_ref[:, span]) + bias_ref[:, span]
-        out[...] = (got if scale is None else got * scale).astype(jnp.bfloat16)
-
-
-def project(x, gain, shift, w, bias):
+    k_ref[...] = dot(normed, wk[...]).astype(jnp.bfloat16)
+    v_ref[...] = (dot(normed, wv[...]) + bias_ref[...]).astype(jnp.bfloat16)
+
+
+def weight_spec(width, size, column):
+    return pl.BlockSpec((width, size), lambda i: (0, column), pipeline_mode=pl.Buffered(1))
+
+
+def project(x, gain, shift, w, v_bias):
     rows, width = x.shape
+    half = width // 2
     return pl.pallas_call(
         project_kernel,
-        out_shape=(low_shape(rows, width),) * 4,
+        out_shape=(low_shape(rows, width), low_shape(rows, half), low_shape(rows, half)),
         grid=(rows // TILE,),
         in_specs=[
             tile_spec(width),
             whole_spec((1, width)),
             whole_spec((1, width)),
-            whole_spec(w.shape),
-            whole_spec((1, 3 * width)),
+            weight_spec(width, half, 2),
+            weight_spec(width, half, 4),
+            weight_spec(1, half, 0),
         ],
-        out_specs=[tile_spec(width)] * 4,
+        out_specs=[tile_spec(width), tile_spec(half), tile_spec(half)],
         compiler_params=params(),
-        cost_estimate=cost(6 * rows * width * width, 10 * rows * width + 6 * width * width),
+        cost_estimate=cost(2 * rows * width * width, 10 * rows * width),
         name="project",
-    )(x, gain, shift, w, bias)
+    )(x, gain, shift, w, w, v_bias)
+
+
+def project_more_kernel(n_ref, wq, wk, wv, q_bias, v_bias, q_ref, k_ref, v_ref):
+    normed = n_ref[...]
+    k_ref[...] = dot(normed, wk[...]).astype(jnp.bfloat16)
+    v_ref[...] = (dot(normed, wv[...]) + v_bias[...]).astype(jnp.bfloat16)
+    q_ref[...] = ((dot(normed, wq[...]) + q_bias[...]) * QUERY_SCALE).astype(jnp.bfloat16)
+
+
+def project_more(normed, w, q_bias, v_bias):
+    rows, width = normed.shape
+    half = width // 2
+    return pl.pallas_call(
+        project_more_kernel,
+        out_shape=(low_shape(rows, width), low_shape(rows, half), low_shape(rows, half)),
+        grid=(rows // TILE,),
+        in_specs=[
+            tile_spec(width),
+            weight_spec(width, width, 0),
+            weight_spec(width, half, 3),
+            weight_spec(width, half, 5),
+            whole_spec((1, width)),
+            weight_spec(1, half, 1),
+        ],
+        out_specs=[tile_spec(width), tile_spec(half), tile_spec(half)],
+        compiler_params=params(),
+        cost_estimate=cost(4 * rows * width * width, 10 * rows * width),
+        name="project_more",
+    )(normed, w, w, w, q_bias, v_bias)
 
 
 def mlp_fwd_kernel(
@@ -962,7 +979,9 @@
     )(cot, out, side, pool, w_first, gain3, w_down, slope, w_up, mid, gain2, w_out)
 
 
-def final_bwd_kernel(dq_ref, dk_ref, dv_ref, x_ref, branch_ref, gain, w_ref, grad_ref, sums_ref):
+def final_bwd_kernel(pairs, *refs):
+    pieces = [refs[i * pairs : (i + 1) * pairs] for i in range(5)]
+    x_ref, branch_ref, gain, w_ref, grad_ref, sums_ref = refs[5 * pairs :]
     width = x_ref.shape[1]
 
     @pl.when(pl.program_id(0) == 0)
@@ -972,33 +991,46 @@
     def add(row, value):
         sums_ref[row : row + 1, :] += rows_sum(value)
 
+    def join(part):
+        return jnp.concatenate([r[...] for r in part], axis=1)
+
+    def total(part, other):
+        both = [a[...].astype(jnp.float32) + b[...].astype(jnp.float32) for a, b in zip(part, other)]
+        return jnp.concatenate(both, axis=1).astype(jnp.bfloat16)
+
+    dq = join(pieces[0])
+    dk = total(pieces[1], pieces[2])
+    dv = total(pieces[3], pieces[4])
     dn = (
-        dot(dq_ref[...], w_ref[:, :width], NT)
-        + dot(dk_ref[...], w_ref[:, width : 2 * width], NT)
-        + dot(dv_ref[...], w_ref[:, 2 * width :], NT)
+        dot(dq, w_ref[:, :width], NT)
+        + dot(dk, w_ref[:, width : 2 * width], NT)
+        + dot(dv, w_ref[:, 2 * width :], NT)
     )
     xhat, rstd = ln_parts(x_ref[...].astype(jnp.float32))
     add(0, dn * xhat)
     add(1, dn)
-    add(2, dq_ref[...].astype(jnp.float32))
-    add(3, dv_ref[...].astype(jnp.float32))
+    add(2, dq.astype(jnp.float32))
+    add(3, dv.astype(jnp.float32))
     grad_ref[...] = (
         branch_ref[...].astype(jnp.float32) + ln_back(dn, gain[...], xhat, rstd)
     ).astype(jnp.bfloat16)
 
 
-def final_bwd(dq, dk, dv, x, branch, gain, w):
+def final_bwd(pieces, x, branch, gain, w):
     rows, width = x.shape
+    pairs = width // 128
     return pl.pallas_call(
-        final_bwd_kernel,
+        functools.partial(final_bwd_kernel, pairs),
         out_shape=(low_shape(rows, width), jax.ShapeDtypeStruct((8, width), jnp.float32)),
         grid=(rows // TILE,),
-        in_specs=[tile_spec(width)] * 5 + [whole_spec((1, width)), whole_spec(w.shape)],
+        in_specs=[tile_spec(128)] * (5 * pairs)
+        + [tile_spec(width)] * 2
+        + [whole_spec((1, width)), whole_spec(w.shape)],
         out_specs=[tile_spec(width), pl.BlockSpec((8, width), lambda i: (0, 0))],
         compiler_params=params(),
-        cost_estimate=cost(6 * rows * width * width, 12 * rows * width),
+        cost_estimate=cost(6 * rows * width * width, 16 * rows * width),
         name="final_bwd",
-    )(dq, dk, dv, x, branch, gain, w)
+    )(*pieces, x, branch, gain, w)
 
 
 def grid_masks(frames, lanes):
@@ -1138,48 +1170,280 @@
     return [(i, i ^ bit) for i in range(count)]
 
 
-def halve_frame(parts, rank):
-    first, second = parts
-    keep = jnp.where(rank == 0, first, second)
-    send = jnp.where(rank == 0, second, first)
-    got = lax.ppermute(send, "frame", flip(2, 1))
-    return (keep.astype(jnp.float32) + got.astype(jnp.float32)).astype(jnp.bfloat16)
-
-
-def halve_seq(x, order):
-    count = lax.axis_size("seq")
-    index = lax.axis_index("seq")
-    bits = count.bit_length() - 1
-    left = list(range(bits))[::-1]
-    x = x.reshape((2,) * bits + x.shape[1:])
-    for bit in order:
-        axis = left.index(bit)
-        left.remove(bit)
-        mine = (index >> bit) & 1
-        keep = lax.dynamic_index_in_dim(x, mine, axis, keepdims=False)
-        send = lax.dynamic_index_in_dim(x, 1 - mine, axis, keepdims=False)
-        got = lax.ppermute(send, "seq", flip(count, 1 << bit))
-        x = (keep.astype(jnp.float32) + got.astype(jnp.float32)).astype(jnp.bfloat16)
-    return x
-
-
-def everywhere(x):
-    count = lax.axis_size("seq")
-    x = x + lax.ppermute(x, "frame", flip(2, 1))
-    bit = 1
-    while bit < count:
-        x = x + lax.ppermute(x, "seq", flip(count, bit))
-        bit *= 2
-    return x
-
-
-def weight_grad(a, b):
-    return dot(a, b, TN).astype(jnp.bfloat16)
-
-
-def orders(bits):
+def low_sum(a, b):
+    return (a.astype(jnp.float32) + b.astype(jnp.float32)).astype(jnp.bfloat16)
+
+
+def block_place(owner, rounds):
+    place = 0
+    for bits in rounds:
+        for bit in bits:
+            place = place * 2 + ((owner >> bit) & 1)
+    return place
+
+
+def put_blocks(ref, value, first_owner, owners, rounds):
+    size = value.shape[0] // owners
+    for o in range(owners):
+        place = block_place(first_owner + o, rounds)
+        at = place * size
+        if not isinstance(at, int):
+            at = pl.multiple_of(at, 16)
+        ref[pl.ds(at, size), :] = value[o * size : (o + 1) * size, :]
+
+
+def grad_by_columns_kernel(rounds, seqs, info_ref, a_ref, b_ref, keep_ref, send_ref, turned):
+    step = pl.program_id(0)
+
+    @pl.when(step == 0)
+    def _():
+        turned[...] = a_ref[...].T
+
+    got = dot(turned[...], b_ref[...]).astype(jnp.bfloat16)
+
+    @pl.when(step < pl.num_programs(0) // 2)
+    def _():
+        put_blocks(keep_ref, got, 0, seqs, rounds)
+
+    @pl.when(step >= pl.num_programs(0) // 2)
+    def _():
+        put_blocks(send_ref, got, 0, seqs, rounds)
+
+
+def grad_by_columns(info, a, b, rounds, seqs, at):
+    rows, tall = a.shape
+    wide = b.shape[1]
+    block = min(768, wide // 2)
+    half = wide // 2 // block
+    out = jax.ShapeDtypeStruct((tall, wide // 2), jnp.bfloat16)
+    return pl.pallas_call(
+        functools.partial(grad_by_columns_kernel, rounds, seqs),
+        out_shape=(out, out),
+        grid_spec=pltpu.PrefetchScalarGridSpec(
+            num_scalar_prefetch=1,
+            grid=(2 * half,),
+            in_specs=[
+                pl.BlockSpec((rows, tall), lambda j, info: (0, 0)),
+                pl.BlockSpec(
+                    (rows, block),
+                    lambda j, info: (0, jnp.where(j < half, info[at], 1 - info[at]) * half + j % half),
+                ),
+            ],
+            out_specs=[
+                pl.BlockSpec((tall, block), lambda j, info: (0, jnp.minimum(j, half - 1))),
+                pl.BlockSpec((tall, block), lambda j, info: (0, jnp.maximum(j - half, 0))),
+            ],
+            scratch_shapes=[pltpu.VMEM((tall, rows), jnp.bfloat16)],
+        ),
+        compiler_params=params(),
+        cost_estimate=cost(2 * rows * tall * wide, 2 * rows * (tall + wide)),
+        name="grad_columns",
+    )(info, a, b)
+
+
+def pick_half(rank, value):
+    middle = value.shape[1] // 2
+    first, second = value[:, :middle], value[:, middle:]
+    return jnp.where(rank == 0, first, second), jnp.where(rank == 0, second, first)
+
+
+def grad_by_rows_kernel(rounds, seqs, at, info_ref, a_ref, b_ref, keep_ref, send_ref):
+    steps = pl.num_programs(0)
+    step = pl.program_id(0)
+    got = dot(a_ref[...], b_ref[...], TN).astype(jnp.bfloat16)
+    keep, send = pick_half(info_ref[at], got)
+    owners = seqs // (keep_ref.shape[0] // a_ref.shape[1])
+    put_blocks(keep_ref, keep, step * owners, owners, rounds)
+    put_blocks(send_ref, send, step * owners, owners, rounds)
+
+
+def grad_by_rows(info, a, b, rounds, seqs, at):
+    rows, tall = a.shape
+    wide = b.shape[1]
+    out = jax.ShapeDtypeStruct((tall, wide // 2), jnp.bfloat16)
+    return pl.pallas_call(
+        functools.partial(grad_by_rows_kernel, rounds, seqs, at),
+        out_shape=(out, out),
+        grid_spec=pltpu.PrefetchScalarGridSpec(
+            num_scalar_prefetch=1,
+            grid=(tall // 768,),
+            in_specs=[
+                pl.BlockSpec((rows, 768), lambda j, info: (0, j)),
+                pl.BlockSpec((rows, wide), lambda j, info: (0, 0)),
+            ],
+            out_specs=[pl.BlockSpec((tall, wide // 2), lambda j, info: (0, 0))] * 2,
+        ),
+        compiler_params=params(),
+        cost_estimate=cost(2 * rows * tall * wide, 2 * rows * (tall + wide)),
+        name="grad_rows",
+    )(info, a, b)
+
+
+def grad_pieces_kernel(
+    rounds, seqs, at, info_ref, n_ref, q0, q1, k0, x0, k1, x1, v0, y0, v1, y1, keep_ref, send_ref
+):
+    first = jnp.concatenate([q0[...], q1[...], low_sum(k0[...], x0[...])], axis=1)
+    second = jnp.concatenate(
+        [low_sum(k1[...], x1[...]), low_sum(v0[...], y0[...]), low_sum(v1[...], y1[...])], axis=1
+    )
+    both = jnp.concatenate([first, second], axis=1)
+    got = dot(n_ref[...], both, TN).astype(jnp.bfloat16)
+    keep, send = pick_half(info_ref[at], got)
+    put_blocks(keep_ref, keep, 0, seqs, rounds)
+    put_blocks(send_ref, send, 0, seqs, rounds)
+
+
+def grad_pieces(info, n1, pieces, rounds, seqs, at):
+    (q0, k0, x0, v0, y0), (q1, k1, x1, v1, y1) = pieces
+    rows, tall = n1.shape
+    out = jax.ShapeDtypeStruct((tall, 384), jnp.bfloat16)
+    vm = pl.BlockSpec(memory_space=pltpu.VMEM)
+    sm = pl.BlockSpec(memory_space=pltpu.SMEM)
+    return pl.pallas_call(
+        functools.partial(grad_pieces_kernel, rounds, seqs, at),
+        out_shape=(out, out),
+        in_specs=[sm] + [vm] * 11,
+        out_specs=(vm, vm),
+        compiler_params=pltpu.CompilerParams(vmem_limit_bytes=VMEM_LIMIT),
+        cost_estimate=cost(2 * rows * tall * 768, 4 * rows * tall),
+        name="grad_pieces",
+    )(info, n1, q0, q1, k0, x0, k1, x1, v0, y0, v1, y1)
+
+
+class Stream:
+    def __init__(self, rounds, keep, send):
+        self.rounds = [None] + rounds
+        self.at = 0
+        self.keep = keep
+        self.sends = [send]
+        self.gots = None
+        self.done = False
+
+    def start(self):
+        bits = self.rounds[self.at]
+        if bits is None:
+            self.gots = [lax.ppermute(self.sends[0], "frame", flip(2, 1))]
+            return
+        count = lax.axis_size("seq")
+        self.gots = []
+        for m in range(1, 1 << len(bits)):
+            mask = 0
+            for i, bit in enumerate(bits):
+                mask |= ((m >> (len(bits) - 1 - i)) & 1) << bit
+            self.gots.append(lax.ppermute(self.sends[m - 1], "seq", flip(count, mask)))
+
+
+class Total:
+    def __init__(self, rounds, value):
+        self.rounds = rounds
+        self.at = 0
+        self.value = value
+        self.done = False
+
+    def start(self):
+        bits = self.rounds[self.at]
+        if bits is None:
+            self.gots = [lax.ppermute(self.value, "frame", flip(2, 1))]
+            return
+        count = lax.axis_size("seq")
+        self.gots = []
+        for m in range(1, 1 << len(bits)):
+            mask = 0
+            for i, bit in enumerate(bits):
+                mask |= ((m >> i) & 1) << bit
+            self.gots.append(lax.ppermute(self.value, "seq", flip(count, mask)))
+
+
+def fold(info, at, streams, after=()):
+    streams = [s for s in streams if not s.done]
+    ins, outs, plan = [], [], []
+    for s in streams:
+        last = s.at + 1 == len(s.rounds)
+        if isinstance(s, Total):
+            parts = [s.value] + s.gots
+            plan.append((len(parts), None, None))
+            outs.append(jax.ShapeDtypeStruct(s.value.shape, jnp.float32))
+        else:
+            parts = [s.keep] + s.gots
+            rows, wide = s.keep.shape
+            if last:
+                plan.append((len(parts), (), 1))
+                outs.append(jax.ShapeDtypeStruct((rows, wide), jnp.float32))
+            else:
+                bits = s.rounds[s.at + 1]
+                ways = 1 << len(bits)
+                plan.append((len(parts), tuple(bits), ways))
+                outs += [jax.ShapeDtypeStruct((rows // ways, wide), jnp.bfloat16)] * ways
+        ins += parts
+
+    def kernel(info_ref, *refs):
+        sources, targets = list(refs[: len(ins)]), list(refs[len(ins) + len(after) :])
+        index = info_ref[at]
+        for count, bits, ways in plan:
+            parts = [sources.pop(0) for _ in range(count)]
+
+            def total(span):
+                value = parts[0][span].astype(jnp.float32)
+                for p in parts[1:]:
+                    value = value + p[span].astype(jnp.float32)
+                return value
+
+            if not bits:
+                targets.pop(0)[...] = total(...)
+                continue
+            mine = 0
+            for bit in bits:
+                mine = mine * 2 + ((index >> bit) & 1)
+            size = parts[0].shape[0] // ways
+            for m in range(ways):
+                start = pl.multiple_of((mine ^ m) * size, 16)
+                targets.pop(0)[...] = total((pl.ds(start, size), slice(None))).astype(jnp.bfloat16)
+
+    vm = pl.BlockSpec(memory_space=pltpu.VMEM)
+    sm = pl.BlockSpec(memory_space=pltpu.SMEM)
+    moved = sum(x.size * x.dtype.itemsize for x in ins) * 2
+    results = list(
+        pl.pallas_call(
+            kernel,
+            out_shape=tuple(outs),
+            in_specs=[sm] + [vm] * len(ins) + [pl.BlockSpec(memory_space=pl.ANY)] * len(after),
+            out_specs=(vm,) * len(outs),
+            compiler_params=pltpu.CompilerParams(vmem_limit_bytes=VMEM_LIMIT),
+            cost_estimate=cost(0, moved),
+            name="fold",
+        )(info, *ins, *after)
+    )
+    sent = []
+    for s, (_, bits, ways) in zip(streams, plan):
+        s.at += 1
+        s.done = s.at == len(s.rounds)
+        if isinstance(s, Total):
+            s.value = results.pop(0)
+            sent.append(s.value)
+        elif s.done:
+            s.keep = results.pop(0)
+            sent.append(s.keep)
+        else:
+            got = [results.pop(0) for _ in range(ways)]
+            s.keep, s.sends = got[0], got[1:]
+            sent.append(s.sends[0])
+        if not s.done:
+            s.start()
+    return sent[:1]
+
+
+def single(bits):
+    return [[b] for b in bits]
+
+
+def turned_orders(bits):
     low = list(range(bits))
     return [low[i:] + low[:i] for i in range(3)]
+
+
+def doubles(bits):
+    low = list(range(bits))
+    return [low[i : i + 2] for i in range(0, bits, 2)]
 
 
 def quick_device(
@@ -1192,26 +1456,33 @@
     inner = w_up.shape[1]
     seqs = lax.axis_size("seq")
     rank = lax.axis_index("frame")
-    share = width // seqs
-    half = width // 2
-    axis_orders = orders(seqs.bit_length() - 1)
+    bits = seqs.bit_length() - 1
+    orders = turned_orders(bits)
+    rank_at, seq_at = 2 * frames + 1, 2 * frames + 2
 
     def row(x):
         return x.reshape(1, -1)
 
-    all_masks = lax.all_gather(frame_mask, "seq", axis=0, tiled=True)
-    count = jnp.sum(all_masks).astype(jnp.float32)
+    def swap(x):
+        return lax.ppermute(x, "frame", flip(2, 1))
+
+    place = jnp.stack([rank, lax.axis_index("seq")]).astype(jnp.int32)
+    info = jnp.concatenate([frame_mask[0], clip_lengths[0, 0:1], place])
+    x = tokens[0]
+    count = Total(doubles(bits), jnp.sum(frame_mask).astype(jnp.float32) * jnp.ones((1, 128)))
+    count.start()
+    n1, k0, v0 = project(x, row(ln_gain_first), row(ln_bias_first), w_qkv, row(v_bias))
+    far_k0, far_v0 = swap(k0), swap(v0)
+    fold(info, seq_at, [count], (n1,))
+    q, k1, v1 = project_more(n1, w_qkv, row(q_bias), row(v_bias))
+    far_k1, far_v1 = swap(k1), swap(v1)
+    attended, *kept0 = attn_fwd(info, q, k0, v0, far_k0, far_v0, None, 0, frames)
+    fold(info, seq_at, [count], (kept0[0],))
+    attended, *kept1 = attn_fwd(info, q, k1, v1, far_k1, far_v1, attended, 1, frames)
+    while not count.done:
+        fold(info, seq_at, [count], (attended,))
+    count = count.value[0, 0]
     weight = (penalty_scale / count).reshape(1)
-    info = jnp.concatenate(
-        [frame_mask[0], clip_lengths[0, 0:1], rank.reshape(1).astype(jnp.int32)]
-    )
-    x = tokens[0]
-    qkv_bias = jnp.concatenate([q_bias, jnp.zeros_like(q_bias), v_bias])
-    n1, q, k, v = project(x, row(ln_gain_first), row(ln_bias_first), w_qkv, row(qkv_bias))
-    far_k = lax.ppermute(k, "frame", flip(2, 1))
-    far_v = lax.ppermute(v, "frame", flip(2, 1))
-    kc, vc, valid, table = compact(info, k, v, far_k, far_v, frames)
-    attended, lse = attn_fwd(info, table, q, kc, vc, valid, frames)
     mid, n2, hidden, slope, out, n3 = mlp_fwd(
         x, attended, w_out, row(out_bias), row(ln_gain_second), row(ln_bias_second), w_up,
         row(up_bias), w_down, row(down_bias), row(ln_gain_third), row(ln_bias_third),
@@ -1226,57 +1497,78 @@
         out_cot[0], out, side, pool_cot[0], first_pad, row(ln_gain_third), w_down, slope, w_up,
         mid, row(ln_gain_second), w_out,
     )
-    def halves(a, b):
-        middle = b.shape[1] // 2
-        return weight_grad(a, b[:, :middle]), weight_grad(a, b[:, middle:])
-
-    up_sum = halve_frame(halves(n2, d_up), rank).reshape(seqs, share, inner // 2)
-    down_sum = halve_frame(halves(hidden, d_down), rank).reshape(seqs, inner // seqs, half)
-    wout_sum = halve_frame(halves(attended, d_branch), rank).reshape(seqs, share, half)
-    grad_first = grad_first.astype(jnp.bfloat16).T
-    columns = grad_first.shape[1] // 2
-    first_sum = halve_frame((grad_first[:, :columns], grad_first[:, columns:]), rank)
-    grad_up = halve_seq(up_sum, axis_orders[0])
-    grad_down = halve_seq(down_sum, axis_orders[1])
-    grad_out = halve_seq(wout_sum, axis_orders[2])
-    grad_first = halve_seq(first_sum.reshape(seqs, share, columns), axis_orders[2])
-    early = everywhere(jnp.concatenate([sums.reshape(-1), small.reshape(-1)]))
-
-    groups = width // 128 // 2
-    parts_q, parts_k, parts_v, parts_w = [], [], [], []
-    for g in range(groups):
-        dq, dkc, dvc = attn_bwd(info, table, q, kc, vc, valid, attended, d_att, lse, frames, g)
-        own_k, own_v, other_k, other_v = spread(info, table, dkc, dvc, frames)
-
-        def joined(own, other):
-            got = lax.ppermute(other, "frame", flip(2, 1))
-            return (own.astype(jnp.float32) + got.astype(jnp.float32)).astype(jnp.bfloat16)
-
-        dk, dv = joined(own_k, other_k), joined(own_v, other_v)
-        parts_q.append(dq)
-        parts_k.append(dk)
-        parts_v.append(dv)
-        pair = (
-            weight_grad(n1, jnp.concatenate([dq, dk[:, :128]], axis=1)),
-            weight_grad(n1, jnp.concatenate([dk[:, 128:], dv], axis=1)),
+
+    def both(x):
+        middle = x.shape[1] // 2
+        first, second = x[:, :middle], x[:, middle:]
+        return jnp.where(rank == 0, first, second), jnp.where(rank == 0, second, first)
+
+    plain = single(range(bits)[::-1])
+    up = Stream(
+        single(orders[0]), *grad_by_columns(info, n2, d_up, single(orders[0]), seqs, rank_at)
+    )
+    up.start()
+    down = Stream(
+        single(orders[1]), *grad_by_rows(info, hidden, d_down, single(orders[1]), seqs, rank_at)
+    )
+    down.start()
+    branch = Stream(
+        single(orders[2]), *grad_by_rows(info, attended, d_branch, single(orders[2]), seqs, rank_at)
+    )
+    branch.start()
+    first = Stream(plain, *both(grad_first.astype(jnp.bfloat16).T))
+    first.start()
+    early = Total(
+        [None] + single(range(bits)), jnp.concatenate([sums.reshape(-1, 128), small.reshape(-1, 128)])
+    )
+    early.start()
+    streams = [up, down, branch, first, early]
+    after = fold(info, seq_at, streams)
+
+    pairs = width // 128
+    groups = pairs // 2
+    pieces = {}
+    group_streams = []
+
+    def group_stream(g):
+        stream = Stream(
+            doubles(bits),
+            *grad_pieces(
+                info, n1, (pieces[g], pieces[g + groups]), doubles(bits), seqs, rank_at
+            ),
         )
-        summed = halve_frame(pair, rank).reshape(seqs, share, 384)
-        parts_w.append(halve_seq(summed, axis_orders[g % 3]))
-
-    def heads(parts):
-        return jnp.concatenate([p[:, :128] for p in parts] + [p[:, 128:] for p in parts], axis=1)
-
+        stream.start()
+        group_streams.append(stream)
+        return stream
+
+    for turn, pair in enumerate(p for g in range(groups) for p in (g, g + groups)):
+        lse, kc, vc, valid = (kept0, kept1)[pair // groups]
+        dq, own_k, own_v, far_k, far_v = attn_bwd(
+            info, q, kc, vc, valid, attended, d_att, lse, pair, frames, after
+        )
+        pieces[pair] = (dq, own_k, swap(far_k), own_v, swap(far_v))
+        after = fold(info, seq_at, streams, (dq,))
+        if turn % 2 == 0 and turn > 0:
+            stream = group_stream(turn // 2 - 1)
+            streams.append(stream)
+            after = after + [stream.sends[0]]
+    streams.append(group_stream(groups - 1))
     tokens_grad, late = final_bwd(
-        heads(parts_q), heads(parts_k), heads(parts_v), x, d_branch, row(ln_gain_first), w_qkv
-    )
+        [pieces[p][i] for i in range(5) for p in range(pairs)],
+        x, d_branch, row(ln_gain_first), w_qkv,
+    )
+    late = Total([None] + doubles(bits), late)
+    late.start()
+    streams.append(late)
+    while not all(s.done for s in streams):
+        fold(info, seq_at, streams)
     grad_qkv = jnp.concatenate(
-        [p[:, 128 * i : 128 * i + 128] for i in range(3) for p in parts_w], axis=1
-    )
-    late = everywhere(late)
-    sums = early[: 16 * width].reshape(16, width)
-    small = early[16 * width :].reshape(8, 8, 128)
+        [s.keep[:, 128 * i : 128 * i + 128] for i in range(3) for s in group_streams], axis=1
+    )
+    late = late.value
+    sums = early.value[: 16 * width // 128].reshape(16, width)
+    small = early.value[16 * width // 128 :].reshape(8, 8, 128)
     penalty = small[3, 0, 0] / count
-    f32 = jnp.float32
     return (
         out[None],
         pooled[None],
@@ -1284,20 +1576,20 @@
         tokens_grad[None],
         late[0],
         late[1],
-        grad_qkv.astype(f32),
+        grad_qkv,
         late[2],
         late[3],
-        grad_out.astype(f32),
+        branch.keep,
         sums[5],
         sums[0],
         sums[1],
-        grad_up.astype(f32),
+        up.keep,
         sums[6 : 6 + inner // width].reshape(-1),
-        grad_down.astype(f32),
+        down.keep,
         sums[4],
         sums[2],
         sums[3],
-        grad_first.astype(f32),
+        first.keep,
         small[:3, :, : 9 * MAPS],
         small[4:8, :, 0],
     )

time: 723 us -> 676 us (0.935)
  Pallas kernels: 200 us -> 289 us
  waiting for transfers between devices: 89 us -> 21.6 us
  matrix products: 45.6 us -> 0 us
  blocking collectives: 42.2 us -> 0 us
  starting transfers between devices: 290 us -> 313 us
  other arithmetic: 18 us -> 3.02 us
    pallas_call x10 -> x29, Pallas kernels: 121 us -> 210 us  [the longest x6 60.4 us: attn_bwd(): pl.pallas_call(kernel, out_shape=(jax.ShapeDtypeStruct((rows, 128), jnp.b...]
    ppermute x53 -> x75, waiting for transfers between devices: 89 us -> 21.6 us  [the longest x34 20.4 us: start(): self.gots.append(lax.ppermute(self.sends[m - 1], 'seq', flip(count, mask)))]
    dot_general x12 -> x0, matrix products: 45.6 us -> none  [dot(): return lax.dot_general(a, b, dims, preferred_element_type=jnp.float32)]
    all_gather x1 -> x0, blocking collectives: 42.2 us -> none  [quick_device(): all_masks = lax.all_gather(frame_mask, 'seq', axis=0, tiled=True)]
    ppermute x53 -> x75, starting transfers between devices: 290 us -> 313 us  [the longest x34 260 us: start(): self.gots.append(lax.ppermute(self.sends[m - 1], 'seq', flip(count, mask)))]
    convert_element_type x42 -> x1, other arithmetic: 15.9 us -> 0.95 us  [quick_device(): first = Stream(plain, *both(grad_first.astype(jnp.bfloat16).T))]
    unnamed x122 -> x217, local copies, waits for them, and re-layouts: 10.3 us -> 19.6 us
  transfers between devices with their start and end apart: 53 -> 75, of which waited for: 29 -> 10; matrix products, arithmetic and copies ran while one was open for 12% -> 2% of each run, Pallas kernels for 4% -> 22%
where the time goes in v2:
time: 676 us; the launch traced here: 666 us
  starting transfers between devices  313 us (46%)
  Pallas kernels  289 us (43%)
  local copies, waits for them, and re-layouts  33.6 us (5%)
  waiting for transfers between devices  21.6 us (3%)
    ppermute x34, starting transfers between devices, start(): self.gots.append(lax.ppermute(self.sends[m - 1], 'seq', flip(count, mask)))  260 us
    pallas_call x6, Pallas kernels, attn_bwd(): pl.pallas_call(kernel, out_shape=(jax.ShapeDtypeStruct((rows, 128), jnp.b...  60.4 us
    pallas_call x1, Pallas kernels, mlp_bwd(): pl.pallas_call(mlp_bwd_kernel, out_shape=(low_shape(rows, width), low_sha...  36.9 us
    pallas_call x12, Pallas kernels, fold(): pl.pallas_call(kernel, out_shape=tuple(outs), in_specs=[sm] + [vm] * len(...  32.4 us
    pallas_call x1, Pallas kernels, mlp_fwd(): pl.pallas_call(mlp_fwd_kernel, out_shape=(low_shape(rows, width), low_sha...  32.1 us
    pallas_call x2, Pallas kernels, attn_fwd(): pl.pallas_call(kernel, out_shape=(jax.ShapeDtypeStruct((rows, width), jnp...  28.7 us
    pallas_call x2, Pallas kernels, grad_by_rows(): pl.pallas_call(functools.partial(grad_by_rows_kernel, rounds, seqs, at),...  21.8 us
    ppermute x34, waiting for transfers between devices, start(): self.gots.append(lax.ppermute(self.sends[m - 1], 'seq', flip(count, mask)))  20.4 us
  transfers between devices with their start and end apart: 75, of which 10 were waited for; matrix products, arithmetic and copies ran while one was open for 2% of the time, Pallas kernels for 22%

profile of v2, /device:TPU:0, one launch (start us, length us, event | category | flops | bytes accessed | tf_op | source)
XLA Modules:
  0.0 665.8 jit_solution(1179964510531240930)
XLA Ops:
  4.5 8.3 %project.1 = (bf16[1568,768]{1,0:T(8,128)(2,1)}, bf16[1568,384]{1,0:T(8,128)(2,1)}, bf16[1568,384]{1,0:T(8,128)(2,1)}) custom-call(bf16[1568,768]{1,0:T(8,128)(2,1)} %bitcast.37, f32[1,768]{1,0:T(1,128)} %reshape.111.gain_ref.refs_32_, f32[1,768]{1,0:T(1,128)} %reshape.112.shift_ref, bf16[768,2304]{1,0:T(8,128)(2,1)} %refs_33_.1, ...), custom_call_target="tpu_custom_call" | custom-call | flops 1849688064 | bytes 12042240 | tf_op jit(solution)/shard_map/project/pallas_call | solution.py:793
  24.0 9.1 %project_more.1 = (bf16[1568,768]{1,0:T(8,128)(2,1)}, bf16[1568,384]{1,0:T(8,128)(2,1)}, bf16[1568,384]{1,0:T(8,128)(2,1)}) custom-call(bf16[1568,768]{1,0:T(8,128)(2,1)} %get-tuple-element.168.n_ref.refs_4_, bf16[768,2304]{1,0:T(8,128)(2,1)} %refs_33_.1, bf16[768,2304]{1,0:T(8,128)(2,1)} %refs_33_.1, bf16[768,2304]{1,0:T(8,128)(2,1)} %refs_33_.1, ...), custom_call_target="tpu_custom_call" | custom-call | flops 3699376128 | bytes 12042240 | tf_op jit(solution)/shard_map/project_more/pallas_call | solution.py:822
  43.9 14.3 %attn_fwd.2 = (bf16[1568,768]{1,0:T(8,128)(2,1)}, f32[3,8,1568]{2,1,0:T(8,128)}, bf16[4608,384]{1,0:T(8,128)(2,1)}, bf16[4608,384]{1,0:T(8,128)(2,1)}, bf16[4608,128]{1,0:T(8,128)(2,1)}) custom-call(s32[19]{0:T(128)} %pad_add_fusion.refs_0_.info_ref, bf16[1568,768]{1,0:T(8,128)(2,1)} %get-tuple-element.169.refs_1_, ...), custom_call_target="tpu_custom_call" | custom-call | flops 40000000000 | bytes 10000000 | tf_op jit(solution)/shard_map/attn_fwd/pallas_call | solution.py:563
  60.7 14.4 %attn_fwd.3 = (bf16[1568,768]{1,0:T(8,128)(2,1)}, f32[3,8,1568]{2,1,0:T(8,128)}, bf16[4608,384]{1,0:T(8,128)(2,1)}, bf16[4608,384]{1,0:T(8,128)(2,1)}, bf16[4608,128]{1,0:T(8,128)(2,1)}) custom-call(s32[19]{0:T(128)} %pad_add_fusion.refs_0_.info_ref, bf16[1568,768]{1,0:T(8,128)(2,1)} %get-tuple-element.169.refs_1_, ...), custom_call_target="tpu_custom_call", output_to_operand_aliasing={{0}: (6, {})} | custom-call | flops 40000000000 | bytes 10000000 | tf_op jit(solution)/shard_map/attn_fwd/pallas_call | solution.py:563
  75.1 32.1 %mlp_fwd.1 = (bf16[1568,768]{1,0:T(8,128)(2,1)}, bf16[1568,768]{1,0:T(8,128)(2,1)}, bf16[1568,3072]{1,0:T(8,128)(2,1)}, bf16[1568,3072]{1,0:T(8,128)(2,1)}, bf16...) custom-call(bf16[1568,768]{1,0:T(8,128)(2,1)} %bitcast.38, bf16[1568,768]{1,0:T(8,128)(2,1)} %get-tuple-element.175.a_ref.refs_5_, ...), custom_call_target="tpu_custom_call" | custom-call | flops 16647192576 | bytes 33718272 | tf_op jit(solution)/shard_map/mlp_fwd/pallas_call | solution.py:880
  107.2 10.0 %learner.1 = (bf16[1568,256]{1,0:T(8,128)(2,1)}, bf16[64,768]{1,0:T(8,128)(2,1)}, f32[8,8,128]{2,1,0:T(8,128)}, f32[72,768]{1,0:T(8,128)}) custom-call(s32[19]{0:T(128)} %pad_add_fusion.refs_0_.info_ref, f32[1]{0:T(128)} %bitcast.8.weight_ref, bf16[1568,768]{1,0:T(8,128)(2,1)} %get-tuple-element.178.n3_ref, bf16[1568,768]{1,0:T(8,128)(2,1)} %get-tuple-element.176.out_ref, ...), custom_call_target="tpu_custom_call" | custom-call | flops 20000000000 | bytes 4816896 | tf_op jit(solution)/shard_map/learner/pallas_call | solution.py:1150
  117.3 36.9 %mlp_bwd.1 = (bf16[1568,768]{1,0:T(8,128)(2,1)}, bf16[1568,3072]{1,0:T(8,128)(2,1)}, bf16[1568,768]{1,0:T(8,128)(2,1)}, bf16[1568,768]{1,0:T(8,128)(2,1)}, f32[16,768]{1,0:T(8,128)}) custom-call(bf16[1568,768]{1,0:T(8,128)(2,1)} %bitcast.50, bf16[1568,768]{1,0:T(8,128)(2,1)} %get-tuple-element.176.out_ref, bf16[1568,256]{1,0:T(8,128)(2,1)} %get-tuple-element.181.side_ref, ...), custom_call_target="tpu_custom_call" | custom-call | flops 16647192576 | bytes 33718272 | tf_op jit(solution)/shard_map/mlp_bwd/pallas_call | solution.py:958
  154.2 15.1 %grad_rows.2 = (bf16[3072,384]{1,0:T(8,128)(2,1)}, bf16[3072,384]{1,0:T(8,128)(2,1)}) custom-call(s32[19]{0:T(128)} %pad_add_fusion.refs_0_.info_ref, bf16[1568,3072]{1,0:T(8,128)(2,1)} %get-tuple-element.187.a_ref, bf16[1568,768]{1,0:T(8,128)(2,1)} %get-tuple-element.188.b_ref), custom_call_target="tpu_custom_call" | custom-call | flops 7398752256 | bytes 12042240 | tf_op jit(solution)/shard_map/grad_rows/pallas_call | solution.py:1264
  169.3 15.2 %collective-permute-start.11 = (bf16[3072,384]{1,0:T(8,128)(2,1)}, bf16[3072,384]{1,0:T(8,128)(2,1)S(1)}, u32[]{:S(2)}, u32[]{:S(2)}) collective-permute-start(bf16[3072,384]{1,0:T(8,128)(2,1)} %get-tuple-element.190), channel_id=1, source_target_pairs={{0,1},{1,0},{2,3},{3,2},{4,5},{5,4},{6,7},{7,6},{8,9},{9,8},{10,11... | collective-permute-start | bytes 7077896 | tf_op jit(solution)/shard_map/ppermute | solution.py:1325
  184.5 15.3 %grad_columns.1 = (bf16[768,1536]{1,0:T(8,128)(2,1)}, bf16[768,1536]{1,0:T(8,128)(2,1)}) custom-call(s32[19]{0:T(128)} %pad_add_fusion.refs_0_.info_ref, bf16[1568,768]{1,0:T(8,128)(2,1)} %get-tuple-element.180.a_ref, bf16[1568,3072]{1,0:T(8,128)(2,1)} %get-tuple-element.184.b_ref), custom_call_target="tpu_custom_call" | custom-call | flops 7398752256 | bytes 12042240 | tf_op jit(solution)/shard_map/grad_columns/pallas_call | solution.py:1219
  199.8 6.7 %grad_rows.3 = (bf16[768,384]{1,0:T(8,128)(2,1)}, bf16[768,384]{1,0:T(8,128)(2,1)}) custom-call(s32[19]{0:T(128)} %pad_add_fusion.refs_0_.info_ref, bf16[1568,768]{1,0:T(8,128)(2,1)} %get-tuple-element.175.a_ref.refs_5_, bf16[1568,768]{1,0:T(8,128)(2,1)} %get-tuple-element.191.b_ref.refs_31_), custom_call_target="tpu_custom_call" | custom-call | flops 1849688064 | bytes 4816896 | tf_op jit(solution)/shard_map/grad_rows/pallas_call | solution.py:1264
  212.3 7.2 %fold.14 = (bf16[384,1536]{1,0:T(8,128)(2,1)}, bf16[384,1536]{1,0:T(8,128)(2,1)}, bf16[1536,384]{1,0:T(8,128)(2,1)}, bf16[1536,384]{1,0:T(8,128)(2,1)}, bf16[384...) custom-call(s32[19]{0:T(128)} %pad_add_fusion.refs_0_.info_ref, ...), custom_call_target="tpu_custom_call" | custom-call | bytes 21782528 | tf_op jit(solution)/shard_map/fold/pallas_call | solution.py:1406
  219.5 17.6 %collective-permute-start.16 = (bf16[1536,384]{1,0:T(8,128)(2,1)}, bf16[1536,384]{1,0:T(8,128)(2,1)S(1)}, u32[]{:S(2)}, u32[]{:S(2)}) collective-permute-start(bf16[1536,384]{1,0:T(8,128)(2,1)} %get-tuple-element.200), channel_id=1, source_target_pairs={{0,4},{2,6},{4,0},{6,2},{8,12},{10,14},{12,8},{14,10},{16,20},{18,... | collective-permute-start | bytes 3538952 | tf_op jit(solution)/shard_map/ppermute | solution.py:1333
  237.1 17.0 %collective-permute-start.17 = (bf16[384,384]{1,0:T(8,128)(2,1)}, bf16[384,384]{1,0:T(8,128)(2,1)S(1)}, u32[]{:S(2)}, u32[]{:S(2)}) collective-permute-start(bf16[384,384]{1,0:T(8,128)(2,1)} %get-tuple-element.202), channel_id=1, source_target_pairs={{0,8},{2,10},{4,12},{6,14},{8,0},{10,2},{12,4},{14,6},{16,24},{18,... | collective-permute-start | bytes 884744 | tf_op jit(solution)/shard_map/ppermute | solution.py:1333
  254.1 48.8 %collective-permute-start.18 = (bf16[384,36]{1,0:T(8,128)(2,1)}, bf16[384,36]{1,0:T(8,128)(2,1)S(1)}, u32[]{:S(2)}, u32[]{:S(2)}) collective-permute-start(bf16[384,36]{1,0:T(8,128)(2,1)} %get-tuple-element.204), channel_id=1, source_target_pairs={{0,16},{2,18},{4,20},{6,22},{8,24},{10,26},{12,28},{14,30},{16,0},... | collective-permute-start | bytes 82952 | tf_op jit(solution)/shard_map/ppermute | solution.py:1333
  303.0 10.0 %attn_bwd.6 = (bf16[1568,128]{1,0:T(8,128)(2,1)}, bf16[1568,128]{1,0:T(8,128)(2,1)}, bf16[1568,128]{1,0:T(8,128)(2,1)}, bf16[1568,128]{1,0:T(8,128)(2,1)}, bf16[1568,128]{1,0:T(8,128)(2,1)}) custom-call(s32[19]{0:T(128)} %pad_add_fusion.refs_0_.info_ref, bf16[1568,768]{1,0:T(8,128)(2,1)} %get-tuple-element.169.refs_1_, ...), custom_call_target="tpu_custom_call" | custom-call | flops 30000001024 | bytes 10000000 | tf_op jit(solution)/shard_map/attn_bwd/pallas_call | solution.py:701
  319.0 10.7 %collective-permute-start.20 = (bf16[192,1536]{1,0:T(8,128)(2,1)}, bf16[192,1536]{1,0:T(8,128)(2,1)S(1)}, u32[]{:S(2)}, u32[]{:S(2)}) collective-permute-start(bf16[192,1536]{1,0:T(8,128)(2,1)} %get-tuple-element.212.refs_8_), channel_id=1, source_target_pairs={{0,4},{2,6},{4,0},{6,2},{8,12},{10,14},{12,8},{14,10},{16,20},{18,... | collective-permute-start | bytes 1769480 | tf_op jit(solution)/shard_map/ppermute | solution.py:1333
  329.7 8.7 %collective-permute-start.22 = (bf16[192,384]{1,0:T(8,128)(2,1)}, bf16[192,384]{1,0:T(8,128)(2,1)S(1)}, u32[]{:S(2)}, u32[]{:S(2)}) collective-permute-start(bf16[192,384]{1,0:T(8,128)(2,1)} %get-tuple-element.216), channel_id=1, source_target_pairs={{0,16},{2,18},{4,20},{6,22},{8,24},{10,26},{12,28},{14,30},{16,0},... | collective-permute-start | bytes 442376 | tf_op jit(solution)/shard_map/ppermute | solution.py:1333
  339.1 9.8 %attn_bwd.7 = (bf16[1568,128]{1,0:T(8,128)(2,1)}, bf16[1568,128]{1,0:T(8,128)(2,1)}, bf16[1568,128]{1,0:T(8,128)(2,1)}, bf16[1568,128]{1,0:T(8,128)(2,1)}, bf16[1568,128]{1,0:T(8,128)(2,1)}) custom-call(s32[19]{0:T(128)} %pad_add_fusion.refs_0_.info_ref, bf16[1568,768]{1,0:T(8,128)(2,1)} %get-tuple-element.169.refs_1_, ...), custom_call_target="tpu_custom_call" | custom-call | flops 30000001024 | bytes 10000000 | tf_op jit(solution)/shard_map/attn_bwd/pallas_call | solution.py:701
  353.0 10.8 %collective-permute-start.25 = (bf16[96,1536]{1,0:T(8,128)(2,1)}, bf16[96,1536]{1,0:T(8,128)(2,1)S(1)}, u32[]{:S(2)}, u32[]{:S(2)}) collective-permute-start(bf16[96,1536]{1,0:T(8,128)(2,1)} %get-tuple-element.226.refs_8_), channel_id=1, source_target_pairs={{0,8},{2,10},{4,12},{6,14},{8,0},{10,2},{12,4},{14,6},{16,24},{18,... | collective-permute-start | bytes 884744 | tf_op jit(solution)/shard_map/ppermute | solution.py:1333
  377.9 18.1 %collective-permute-start.26 = (bf16[384,384]{1,0:T(8,128)(2,1)}, bf16[384,384]{1,0:T(8,128)(2,1)S(1)}, u32[]{:S(2)}, u32[]{:S(2)}) collective-permute-start(bf16[384,384]{1,0:T(8,128)(2,1)} %get-tuple-element.228), channel_id=1, source_target_pairs={{0,16},{2,18},{4,20},{6,22},{8,24},{10,26},{12,28},{14,30},{16,0},... | collective-permute-start | bytes 884744 | tf_op jit(solution)/shard_map/ppermute | solution.py:1333
  396.0 10.1 %attn_bwd.8 = (bf16[1568,128]{1,0:T(8,128)(2,1)}, bf16[1568,128]{1,0:T(8,128)(2,1)}, bf16[1568,128]{1,0:T(8,128)(2,1)}, bf16[1568,128]{1,0:T(8,128)(2,1)}, bf16[1568,128]{1,0:T(8,128)(2,1)}) custom-call(s32[19]{0:T(128)} %pad_add_fusion.refs_0_.info_ref, bf16[1568,768]{1,0:T(8,128)(2,1)} %get-tuple-element.169.refs_1_, ...), custom_call_target="tpu_custom_call" | custom-call | flops 30000001024 | bytes 10000000 | tf_op jit(solution)/shard_map/attn_bwd/pallas_call | solution.py:701
  423.5 9.2 %collective-permute-start.30 = (bf16[48,1536]{1,0:T(8,128)(2,1)}, bf16[48,1536]{1,0:T(8,128)(2,1)S(1)}, u32[]{:S(2)}, u32[]{:S(2)}) collective-permute-start(bf16[48,1536]{1,0:T(8,128)(2,1)} %get-tuple-element.236.refs_8_), channel_id=1, source_target_pairs={{0,16},{2,18},{4,20},{6,22},{8,24},{10,26},{12,28},{14,30},{16,0},... | collective-permute-start | bytes 442376 | tf_op jit(solution)/shard_map/ppermute | solution.py:1333
  438.9 10.2 %attn_bwd.9 = (bf16[1568,128]{1,0:T(8,128)(2,1)}, bf16[1568,128]{1,0:T(8,128)(2,1)}, bf16[1568,128]{1,0:T(8,128)(2,1)}, bf16[1568,128]{1,0:T(8,128)(2,1)}, bf16[1568,128]{1,0:T(8,128)(2,1)}) custom-call(s32[19]{0:T(128)} %pad_add_fusion.refs_0_.info_ref, bf16[1568,768]{1,0:T(8,128)(2,1)} %get-tuple-element.169.refs_1_, ...), custom_call_target="tpu_custom_call" | custom-call | flops 30000001024 | bytes 10000000 | tf_op jit(solution)/shard_map/attn_bwd/pallas_call | solution.py:701
  452.8 8.7 %collective-permute-start.40 = (bf16[192,384]{1,0:T(8,128)(2,1)}, bf16[192,384]{1,0:T(8,128)(2,1)S(1)}, u32[]{:S(2)}, u32[]{:S(2)}) collective-permute-start(bf16[192,384]{1,0:T(8,128)(2,1)} %get-tuple-element.259), channel_id=1, source_target_pairs={{0,4},{2,6},{4,0},{6,2},{8,12},{10,14},{12,8},{14,10},{16,20},{18,... | collective-permute-start | bytes 442376 | tf_op jit(solution)/shard_map/ppermute | solution.py:1333
  466.9 10.0 %attn_bwd.10 = (bf16[1568,128]{1,0:T(8,128)(2,1)}, bf16[1568,128]{1,0:T(8,128)(2,1)}, bf16[1568,128]{1,0:T(8,128)(2,1)}, bf16[1568,128]{1,0:T(8,128)(2,1)}, bf16[1568,128]{1,0:T(8,128)(2,1)}) custom-call(s32[19]{0:T(128)} %pad_add_fusion.refs_0_.info_ref, bf16[1568,768]{1,0:T(8,128)(2,1)} %get-tuple-element.169.refs_1_, ...), custom_call_target="tpu_custom_call" | custom-call | flops 30000001024 | bytes 10000000 | tf_op jit(solution)/shard_map/attn_bwd/pallas_call | solution.py:701
  490.1 10.2 %attn_bwd.11 = (bf16[1568,128]{1,0:T(8,128)(2,1)}, bf16[1568,128]{1,0:T(8,128)(2,1)}, bf16[1568,128]{1,0:T(8,128)(2,1)}, bf16[1568,128]{1,0:T(8,128)(2,1)}, bf16[1568,128]{1,0:T(8,128)(2,1)}) custom-call(s32[19]{0:T(128)} %pad_add_fusion.refs_0_.info_ref, bf16[1568,768]{1,0:T(8,128)(2,1)} %get-tuple-element.169.refs_1_, ...), custom_call_target="tpu_custom_call" | custom-call | flops 30000001024 | bytes 10000000 | tf_op jit(solution)/shard_map/attn_bwd/pallas_call | solution.py:701
  504.8 34.1 %collective-permute-start.51 = (bf16[48,384]{1,0:T(8,128)(2,1)S(1)}, bf16[48,384]{1,0:T(8,128)(2,1)S(1)}, u32[]{:S(2)}, u32[]{:S(2)}) collective-permute-start(bf16[48,384]{1,0:T(8,128)(2,1)S(1)} %copy-done.101), channel_id=1, source_target_pairs={{0,16},{2,18},{4,20},{6,22},{8,24},{10,26},{12,28},{14,30},{16,0},... | collective-permute-start | bytes 110600 | tf_op jit(solution)/shard_map/ppermute | solution.py:1333
  538.9 26.2 %collective-permute-start.52 = (bf16[48,384]{1,0:T(8,128)(2,1)S(1)}, bf16[48,384]{1,0:T(8,128)(2,1)S(1)}, u32[]{:S(2)}, u32[]{:S(2)}) collective-permute-start(bf16[48,384]{1,0:T(8,128)(2,1)S(1)} %copy-done.100), channel_id=1, source_target_pairs={{0,8},{2,10},{4,12},{6,14},{8,0},{10,2},{12,4},{14,6},{16,24},{18,... | collective-permute-start | bytes 110600 | tf_op jit(solution)/shard_map/ppermute | solution.py:1333
  566.0 6.2 grad_pieces.5
  572.6 15.2 %final_bwd.1 = (bf16[1568,768]{1,0:T(8,128)(2,1)}, f32[8,768]{1,0:T(8,128)}) custom-call(bf16[1568,128]{1,0:T(8,128)(2,1)} %get-tuple-element.210.refs_10_.q0.refs_0_, bf16[1568,128]{1,0:T(8,128)(2,1)} %get-tuple-element.234.refs_10_.q0.refs_1_, bf16[1568,128]{1,0:T(8,128)(2,1)} %get-tuple-element.257.refs_4_.refs_2_.q0, ...), custom_call_target="tpu_custom_call" | custom-call | flops 5549064192 | bytes 19267584 | tf_op jit(solution)/shard_map/final_bwd/pallas_call | solution.py:1022
  591.3 17.4 %collective-permute-start.56 = (bf16[192,384]{1,0:T(8,128)(2,1)}, bf16[192,384]{1,0:T(8,128)(2,1)S(1)}, u32[]{:S(2)}, u32[]{:S(2)}) collective-permute-start(bf16[192,384]{1,0:T(8,128)(2,1)} %get-tuple-element.288), channel_id=1, source_target_pairs={{0,2},{2,0},{4,6},{6,4},{8,10},{10,8},{12,14},{14,12},{16,18},{18,... | collective-permute-start | bytes 442376 | tf_op jit(solution)/shard_map/ppermute | solution.py:1333
  (394 shorter events, 166.4 us)
Async XLA Ops:
  12.9 27.4 %collective-permute-start.2 = (bf16[1568,384]{1,0:T(8,128)(2,1)}, bf16[1568,384]{1,0:T(8,128)(2,1)S(1)}, u32[]{:S(2)}, u32[]{:S(2)}) collective-permute-start(bf16[1568,384]{1,0:T(8,128)(2,1)} %get-tuple-element.172.refs_2_), channel_id=1, source_target_pairs={{0,1},{1,0},{2,3},{3,2},{4,5},{5,4},{6,7},{7,6},{8,9},{9,8},{10,11... | collective-permute-start | bytes 3612680 | tf_op jit(solution)/shard_map/ppermute | solution.py:1467
  13.3 29.5 %collective-permute-start.3 = (bf16[1568,384]{1,0:T(8,128)(2,1)}, bf16[1568,384]{1,0:T(8,128)(2,1)S(1)}, u32[]{:S(2)}, u32[]{:S(2)}) collective-permute-start(bf16[1568,384]{1,0:T(8,128)(2,1)} %get-tuple-element.173.refs_3_), channel_id=1, source_target_pairs={{0,1},{1,0},{2,3},{3,2},{4,5},{5,4},{6,7},{7,6},{8,9},{9,8},{10,11... | collective-permute-start | bytes 3612680 | tf_op jit(solution)/shard_map/ppermute | solution.py:1467
  14.7 21.2 %collective-permute-start.4 = (f32[1,128]{1,0:T(1,128)S(1)}, f32[1,128]{1,0:T(1,128)S(1)}, u32[]{:S(2)}, u32[]{:S(2)}) collective-permute-start(f32[1,128]{1,0:T(1,128)S(1)} %mul.3.refs_0_), channel_id=1, source_target_pairs={{0,2},{2,0},{4,6},{6,4},{8,10},{10,8},{12,14},{14,12},{16,18},{18,... | collective-permute-start | bytes 1544 | tf_op jit(solution)/shard_map/ppermute | solution.py:1354
  35.8 24.8 %collective-permute-start = (bf16[1568,384]{1,0:T(8,128)(2,1)}, bf16[1568,384]{1,0:T(8,128)(2,1)}, u32[]{:S(2)}, u32[]{:S(2)}) collective-permute-start(bf16[1568,384]{1,0:T(8,128)(2,1)} %get-tuple-element.170.refs_2_), channel_id=1, source_target_pairs={{0,1},{1,0},{2,3},{3,2},{4,5},{5,4},{6,7},{7,6},{8,9},{9,8},{10,11... | collective-permute-start | bytes 3612680 | tf_op jit(solution)/shard_map/ppermute | solution.py:1467
  35.9 24.8 %collective-permute-start.1 = (bf16[1568,384]{1,0:T(8,128)(2,1)}, bf16[1568,384]{1,0:T(8,128)(2,1)}, u32[]{:S(2)}, u32[]{:S(2)}) collective-permute-start(bf16[1568,384]{1,0:T(8,128)(2,1)} %get-tuple-element.171.refs_3_), channel_id=1, source_target_pairs={{0,1},{1,0},{2,3},{3,2},{4,5},{5,4},{6,7},{7,6},{8,9},{9,8},{10,11... | collective-permute-start | bytes 3612680 | tf_op jit(solution)/shard_map/ppermute | solution.py:1467
  169.3 41.3 %collective-permute-start.11 = (bf16[3072,384]{1,0:T(8,128)(2,1)}, bf16[3072,384]{1,0:T(8,128)(2,1)S(1)}, u32[]{:S(2)}, u32[]{:S(2)}) collective-permute-start(bf16[3072,384]{1,0:T(8,128)(2,1)} %get-tuple-element.190), channel_id=1, source_target_pairs={{0,1},{1,0},{2,3},{3,2},{4,5},{5,4},{6,7},{7,6},{8,9},{9,8},{10,11... | collective-permute-start | bytes 7077896 | tf_op jit(solution)/shard_map/ppermute | solution.py:1325
  219.5 93.6 %collective-permute-start.15 = (bf16[384,1536]{1,0:T(8,128)(2,1)}, bf16[384,1536]{1,0:T(8,128)(2,1)S(1)}, u32[]{:S(2)}, u32[]{:S(2)}) collective-permute-start(bf16[384,1536]{1,0:T(8,128)(2,1)} %get-tuple-element.198.refs_8_), channel_id=1, source_target_pairs={{0,2},{2,0},{4,6},{6,4},{8,10},{10,8},{12,14},{14,12},{16,18},{18,... | collective-permute-start | bytes 3538952 | tf_op jit(solution)/shard_map/ppermute | solution.py:1333
  219.5 93.6 %collective-permute-start.16 = (bf16[1536,384]{1,0:T(8,128)(2,1)}, bf16[1536,384]{1,0:T(8,128)(2,1)S(1)}, u32[]{:S(2)}, u32[]{:S(2)}) collective-permute-start(bf16[1536,384]{1,0:T(8,128)(2,1)} %get-tuple-element.200), channel_id=1, source_target_pairs={{0,4},{2,6},{4,0},{6,2},{8,12},{10,14},{12,8},{14,10},{16,20},{18,... | collective-permute-start | bytes 3538952 | tf_op jit(solution)/shard_map/ppermute | solution.py:1333
  237.1 76.0 %collective-permute-start.17 = (bf16[384,384]{1,0:T(8,128)(2,1)}, bf16[384,384]{1,0:T(8,128)(2,1)S(1)}, u32[]{:S(2)}, u32[]{:S(2)}) collective-permute-start(bf16[384,384]{1,0:T(8,128)(2,1)} %get-tuple-element.202), channel_id=1, source_target_pairs={{0,8},{2,10},{4,12},{6,14},{8,0},{10,2},{12,4},{14,6},{16,24},{18,... | collective-permute-start | bytes 884744 | tf_op jit(solution)/shard_map/ppermute | solution.py:1333
  254.1 58.9 %collective-permute-start.18 = (bf16[384,36]{1,0:T(8,128)(2,1)}, bf16[384,36]{1,0:T(8,128)(2,1)S(1)}, u32[]{:S(2)}, u32[]{:S(2)}) collective-permute-start(bf16[384,36]{1,0:T(8,128)(2,1)} %get-tuple-element.204), channel_id=1, source_target_pairs={{0,16},{2,18},{4,20},{6,22},{8,24},{10,26},{12,28},{14,30},{16,0},... | collective-permute-start | bytes 82952 | tf_op jit(solution)/shard_map/ppermute | solution.py:1333
  319.0 29.9 %collective-permute-start.20 = (bf16[192,1536]{1,0:T(8,128)(2,1)}, bf16[192,1536]{1,0:T(8,128)(2,1)S(1)}, u32[]{:S(2)}, u32[]{:S(2)}) collective-permute-start(bf16[192,1536]{1,0:T(8,128)(2,1)} %get-tuple-element.212.refs_8_), channel_id=1, source_target_pairs={{0,4},{2,6},{4,0},{6,2},{8,12},{10,14},{12,8},{14,10},{16,20},{18,... | collective-permute-start | bytes 1769480 | tf_op jit(solution)/shard_map/ppermute | solution.py:1333
  353.0 24.9 %collective-permute-start.25 = (bf16[96,1536]{1,0:T(8,128)(2,1)}, bf16[96,1536]{1,0:T(8,128)(2,1)S(1)}, u32[]{:S(2)}, u32[]{:S(2)}) collective-permute-start(bf16[96,1536]{1,0:T(8,128)(2,1)} %get-tuple-element.226.refs_8_), channel_id=1, source_target_pairs={{0,8},{2,10},{4,12},{6,14},{8,0},{10,2},{12,4},{14,6},{16,24},{18,... | collective-permute-start | bytes 884744 | tf_op jit(solution)/shard_map/ppermute | solution.py:1333
  370.1 46.1 %collective-permute-start.35 = (bf16[1568,128]{1,0:T(8,128)(2,1)S(1)}, bf16[1568,128]{1,0:T(8,128)(2,1)S(1)}, u32[]{:S(2)}, u32[]{:S(2)}) collective-permute-start(bf16[1568,128]{1,0:T(8,128)(2,1)S(1)} %copy-done.89), channel_id=1, source_target_pairs={{0,1},{1,0},{2,3},{3,2},{4,5},{5,4},{6,7},{7,6},{8,9},{9,8},{10,11... | collective-permute-start | bytes 1204232 | tf_op jit(solution)/shard_map/ppermute | solution.py:1467
  376.0 40.1 %collective-permute-start.37 = (bf16[1568,128]{1,0:T(8,128)(2,1)S(1)}, bf16[1568,128]{1,0:T(8,128)(2,1)S(1)}, u32[]{:S(2)}, u32[]{:S(2)}) collective-permute-start(bf16[1568,128]{1,0:T(8,128)(2,1)S(1)} %copy-done.87), channel_id=1, source_target_pairs={{0,1},{1,0},{2,3},{3,2},{4,5},{5,4},{6,7},{7,6},{8,9},{9,8},{10,11... | collective-permute-start | bytes 1204232 | tf_op jit(solution)/shard_map/ppermute | solution.py:1467
  377.4 38.7 %collective-permute-start.36 = (bf16[1568,128]{1,0:T(8,128)(2,1)}, bf16[1568,128]{1,0:T(8,128)(2,1)S(1)}, u32[]{:S(2)}, u32[]{:S(2)}) collective-permute-start(bf16[1568,128]{1,0:T(8,128)(2,1)} %get-tuple-element.247), channel_id=1, source_target_pairs={{0,1},{1,0},{2,3},{3,2},{4,5},{5,4},{6,7},{7,6},{8,9},{9,8},{10,11... | collective-permute-start | bytes 1204232 | tf_op jit(solution)/shard_map/ppermute | solution.py:1467
  377.5 38.7 %collective-permute-start.38 = (bf16[1568,128]{1,0:T(8,128)(2,1)}, bf16[1568,128]{1,0:T(8,128)(2,1)S(1)}, u32[]{:S(2)}, u32[]{:S(2)}) collective-permute-start(bf16[1568,128]{1,0:T(8,128)(2,1)} %get-tuple-element.251), channel_id=1, source_target_pairs={{0,1},{1,0},{2,3},{3,2},{4,5},{5,4},{6,7},{7,6},{8,9},{9,8},{10,11... | collective-permute-start | bytes 1204232 | tf_op jit(solution)/shard_map/ppermute | solution.py:1467
  377.9 32.2 %collective-permute-start.26 = (bf16[384,384]{1,0:T(8,128)(2,1)}, bf16[384,384]{1,0:T(8,128)(2,1)S(1)}, u32[]{:S(2)}, u32[]{:S(2)}) collective-permute-start(bf16[384,384]{1,0:T(8,128)(2,1)} %get-tuple-element.228), channel_id=1, source_target_pairs={{0,16},{2,18},{4,20},{6,22},{8,24},{10,26},{12,28},{14,30},{16,0},... | collective-permute-start | bytes 884744 | tf_op jit(solution)/shard_map/ppermute | solution.py:1333
  423.5 25.7 %collective-permute-start.39 = (bf16[768,384]{1,0:T(8,128)(2,1)}, bf16[768,384]{1,0:T(8,128)(2,1)S(1)}, u32[]{:S(2)}, u32[]{:S(2)}) collective-permute-start(bf16[768,384]{1,0:T(8,128)(2,1)} %get-tuple-element.253.refs_9_), channel_id=1, source_target_pairs={{0,1},{1,0},{2,3},{3,2},{4,5},{5,4},{6,7},{7,6},{8,9},{9,8},{10,11... | collective-permute-start | bytes 1769480 | tf_op jit(solution)/shard_map/ppermute | solution.py:1325
  423.5 25.7 %collective-permute-start.30 = (bf16[48,1536]{1,0:T(8,128)(2,1)}, bf16[48,1536]{1,0:T(8,128)(2,1)S(1)}, u32[]{:S(2)}, u32[]{:S(2)}) collective-permute-start(bf16[48,1536]{1,0:T(8,128)(2,1)} %get-tuple-element.236.refs_8_), channel_id=1, source_target_pairs={{0,16},{2,18},{4,20},{6,22},{8,24},{10,26},{12,28},{14,30},{16,0},... | collective-permute-start | bytes 442376 | tf_op jit(solution)/shard_map/ppermute | solution.py:1333
  461.6 21.3 %collective-permute-start.45 = (bf16[1568,128]{1,0:T(8,128)(2,1)S(1)}, bf16[1568,128]{1,0:T(8,128)(2,1)S(1)}, u32[]{:S(2)}, u32[]{:S(2)}) collective-permute-start(bf16[1568,128]{1,0:T(8,128)(2,1)S(1)} %copy-done.88), channel_id=1, source_target_pairs={{0,1},{1,0},{2,3},{3,2},{4,5},{5,4},{6,7},{7,6},{8,9},{9,8},{10,11... | collective-permute-start | bytes 1204232 | tf_op jit(solution)/shard_map/ppermute | solution.py:1467
  462.1 20.8 %collective-permute-start.44 = (bf16[1568,128]{1,0:T(8,128)(2,1)}, bf16[1568,128]{1,0:T(8,128)(2,1)S(1)}, u32[]{:S(2)}, u32[]{:S(2)}) collective-permute-start(bf16[1568,128]{1,0:T(8,128)(2,1)} %get-tuple-element.266), channel_id=1, source_target_pairs={{0,1},{1,0},{2,3},{3,2},{4,5},{5,4},{6,7},{7,6},{8,9},{9,8},{10,11... | collective-permute-start | bytes 1204232 | tf_op jit(solution)/shard_map/ppermute | solution.py:1467
  477.0 61.9 %collective-permute-start.47 = (bf16[1568,128]{1,0:T(8,128)(2,1)}, bf16[1568,128]{1,0:T(8,128)(2,1)S(1)}, u32[]{:S(2)}, u32[]{:S(2)}) collective-permute-start(bf16[1568,128]{1,0:T(8,128)(2,1)} %get-tuple-element.275), channel_id=1, source_target_pairs={{0,1},{1,0},{2,3},{3,2},{4,5},{5,4},{6,7},{7,6},{8,9},{9,8},{10,11... | collective-permute-start | bytes 1204232 | tf_op jit(solution)/shard_map/ppermute | solution.py:1467
  482.2 82.8 %collective-permute-start.49 = (bf16[1568,128]{1,0:T(8,128)(2,1)}, bf16[1568,128]{1,0:T(8,128)(2,1)}, u32[]{:S(2)}, u32[]{:S(2)}) collective-permute-start(bf16[1568,128]{1,0:T(8,128)(2,1)} %get-tuple-element.279), channel_id=1, source_target_pairs={{0,1},{1,0},{2,3},{3,2},{4,5},{5,4},{6,7},{7,6},{8,9},{9,8},{10,11... | collective-permute-start | bytes 1204232 | tf_op jit(solution)/shard_map/ppermute | solution.py:1467
  500.4 64.7 %collective-permute-start.48 = (bf16[1568,128]{1,0:T(8,128)(2,1)}, bf16[1568,128]{1,0:T(8,128)(2,1)S(1)}, u32[]{:S(2)}, u32[]{:S(2)}) collective-permute-start(bf16[1568,128]{1,0:T(8,128)(2,1)} %get-tuple-element.276), channel_id=1, source_target_pairs={{0,1},{1,0},{2,3},{3,2},{4,5},{5,4},{6,7},{7,6},{8,9},{9,8},{10,11... | collective-permute-start | bytes 1204232 | tf_op jit(solution)/shard_map/ppermute | solution.py:1467
  504.8 60.4 %collective-permute-start.50 = (bf16[1568,128]{1,0:T(8,128)(2,1)}, bf16[1568,128]{1,0:T(8,128)(2,1)S(1)}, u32[]{:S(2)}, u32[]{:S(2)}) collective-permute-start(bf16[1568,128]{1,0:T(8,128)(2,1)} %get-tuple-element.280), channel_id=1, source_target_pairs={{0,1},{1,0},{2,3},{3,2},{4,5},{5,4},{6,7},{7,6},{8,9},{9,8},{10,11... | collective-permute-start | bytes 1204232 | tf_op jit(solution)/shard_map/ppermute | solution.py:1467
  504.8 83.0 %collective-permute-start.51 = (bf16[48,384]{1,0:T(8,128)(2,1)S(1)}, bf16[48,384]{1,0:T(8,128)(2,1)S(1)}, u32[]{:S(2)}, u32[]{:S(2)}) collective-permute-start(bf16[48,384]{1,0:T(8,128)(2,1)S(1)} %copy-done.101), channel_id=1, source_target_pairs={{0,16},{2,18},{4,20},{6,22},{8,24},{10,26},{12,28},{14,30},{16,0},... | collective-permute-start | bytes 110600 | tf_op jit(solution)/shard_map/ppermute | solution.py:1333
  538.9 49.0 %collective-permute-start.52 = (bf16[48,384]{1,0:T(8,128)(2,1)S(1)}, bf16[48,384]{1,0:T(8,128)(2,1)S(1)}, u32[]{:S(2)}, u32[]{:S(2)}) collective-permute-start(bf16[48,384]{1,0:T(8,128)(2,1)S(1)} %copy-done.100), channel_id=1, source_target_pairs={{0,8},{2,10},{4,12},{6,14},{8,0},{10,2},{12,4},{14,6},{16,24},{18,... | collective-permute-start | bytes 110600 | tf_op jit(solution)/shard_map/ppermute | solution.py:1333
  565.1 22.9 %collective-permute-start.53 = (bf16[48,384]{1,0:T(8,128)(2,1)S(1)}, bf16[48,384]{1,0:T(8,128)(2,1)S(1)}, u32[]{:S(2)}, u32[]{:S(2)}) collective-permute-start(bf16[48,384]{1,0:T(8,128)(2,1)S(1)} %copy-done.99), channel_id=1, source_target_pairs={{0,24},{2,26},{4,28},{6,30},{8,16},{10,18},{12,20},{14,22},{16,8},... | collective-permute-start | bytes 110600 | tf_op jit(solution)/shard_map/ppermute | solution.py:1333
  565.1 22.9 %collective-permute-start.54 = (bf16[768,384]{1,0:T(8,128)(2,1)S(1)}, bf16[768,384]{1,0:T(8,128)(2,1)S(1)}, u32[]{:S(2)}, u32[]{:S(2)}) collective-permute-start(bf16[768,384]{1,0:T(8,128)(2,1)S(1)} %copy-done.82), channel_id=1, source_target_pairs={{0,1},{1,0},{2,3},{3,2},{4,5},{5,4},{6,7},{7,6},{8,9},{9,8},{10,11... | collective-permute-start | bytes 1769480 | tf_op jit(solution)/shard_map/ppermute | solution.py:1325
  572.2 45.3 %collective-permute-start.58 = (bf16[768,384]{1,0:T(8,128)(2,1)}, bf16[768,384]{1,0:T(8,128)(2,1)S(1)}, u32[]{:S(2)}, u32[]{:S(2)}) collective-permute-start(bf16[768,384]{1,0:T(8,128)(2,1)} %get-tuple-element.291), channel_id=1, source_target_pairs={{0,1},{1,0},{2,3},{3,2},{4,5},{5,4},{6,7},{7,6},{8,9},{9,8},{10,11... | collective-permute-start | bytes 1769480 | tf_op jit(solution)/shard_map/ppermute | solution.py:1325
  587.8 22.3 %collective-permute-start.59 = (f32[8,768]{1,0:T(8,128)}, f32[8,768]{1,0:T(8,128)S(1)}, u32[]{:S(2)}, u32[]{:S(2)}) collective-permute-start(f32[8,768]{1,0:T(8,128)} %get-tuple-element.292.refs_6_), channel_id=1, source_target_pairs={{0,1},{1,0},{2,3},{3,2},{4,5},{5,4},{6,7},{7,6},{8,9},{9,8},{10,11... | collective-permute-start | bytes 73736 | tf_op jit(solution)/shard_map/ppermute | solution.py:1346
  591.3 22.2 %collective-permute-start.56 = (bf16[192,384]{1,0:T(8,128)(2,1)}, bf16[192,384]{1,0:T(8,128)(2,1)S(1)}, u32[]{:S(2)}, u32[]{:S(2)}) collective-permute-start(bf16[192,384]{1,0:T(8,128)(2,1)} %get-tuple-element.288), channel_id=1, source_target_pairs={{0,2},{2,0},{4,6},{6,4},{8,10},{10,8},{12,14},{14,12},{16,18},{18,... | collective-permute-start | bytes 442376 | tf_op jit(solution)/shard_map/ppermute | solution.py:1333
  (146 other events, 1542.2 us)

commit v3 on v2

--- a/solution.py
+++ b/solution.py
@@ -371,8 +371,7 @@
 NT = (((1,), (1,)), ((), ()))
 TN = (((0,), (0,)), ((), ()))
 PIXELS = 196
-FRAME_ROWS = 208
-CHUNK = 512
+UNIT = 256
 VMEM_LIMIT = 60 * 1024 * 1024
 
 
@@ -381,8 +380,7 @@
 
 
 def compact_rows(frame_total):
-    chunks = -(-frame_total * FRAME_ROWS // CHUNK) + 2
-    return chunks * CHUNK
+    return (-(-frame_total * PIXELS // UNIT) + 3) * UNIT
 
 
 def key_places(frames_here, info_ref):
@@ -396,68 +394,39 @@
         places.append((kept, late, jnp.where(late == 1, count[1], count[0])))
         count[0] = count[0] + kept * (1 - late)
         count[1] = count[1] + kept * late
-    chunks = [(c * FRAME_ROWS + CHUNK - 1) // CHUNK for c in count]
-    start = chunks[0] * CHUNK
+    units = [(c * PIXELS + UNIT - 1) // UNIT for c in count]
+    start = units[0] * UNIT
     starts = [
-        (kept, pl.multiple_of(jnp.where(late == 1, start, 0) + place * FRAME_ROWS, 16))
+        (kept, pl.multiple_of(jnp.where(late == 1, start, 0) + place * PIXELS, 4))
         for kept, late, place in places
     ]
-    tails = [
-        pl.multiple_of(count[0] * FRAME_ROWS, 16),
-        pl.multiple_of(start + count[1] * FRAME_ROWS, 16),
-    ]
-    return starts, tails, chunks[0], chunks[0] + chunks[1]
-
-
-def chunk_range(frames_here, split, end, info_ref):
+    tails = [pl.multiple_of(count[0] * PIXELS, 4), pl.multiple_of(start + count[1] * PIXELS, 4)]
+    return starts, tails, units[0], units[0] + units[1]
+
+
+def clip_edge(frames_here, info_ref):
     total = 2 * frames_here
-    length = info_ref[total]
     first = info_ref[total + 1] * frames_here
-    low = jnp.where(first >= length, split, 0)
-    high = jnp.where(first + frames_here <= length, split, end)
-    edge = jnp.clip((length - first) * PIXELS, 0, frames_here * PIXELS)
-    return low, high, edge
-
-
-def gather_keys(frames_here, info_ref, starts, tails, own_k, own_v, far_k, far_v, kc, vc, valid):
+    return jnp.clip((info_ref[total] - first) * PIXELS, 0, frames_here * PIXELS)
+
+
+def gather_keys(frames_here, info_ref, starts, tails, own_k, own_v, far_k, far_v, kf, vf):
     total = 2 * frames_here
-    length = info_ref[total]
     rank = info_ref[total + 1]
     width = own_k.shape[1]
-    row = lax.broadcasted_iota(jnp.int32, (FRAME_ROWS, width), 0)
-
-    def first_row(f):
-        local = f % frames_here
-        start = local * PIXELS // 16 * 16
-        at = local * PIXELS - start
-        a = own_k[start : start + 16, :].astype(jnp.float32)[at : at + 1, :]
-        b = far_k[start : start + 16, :].astype(jnp.float32)[at : at + 1, :]
-        return jnp.where(rank == f // frames_here, a, b)
-
-    fills = [first_row(0), first_row(total // 2)]
-    for f in range(total // 2 + 1, total):
-        if (f * PIXELS) % 16 == 0:
-            fills[1] = jnp.where(length == f, first_row(f), fills[1])
-    for s in range(2):
-        span = pl.ds(tails[s], CHUNK)
-        kc[span, :] = jnp.broadcast_to(fills[s], (CHUNK, width)).astype(jnp.bfloat16)
-        vc[span, :] = jnp.zeros((CHUNK, width), jnp.bfloat16)
-        valid[span, :] = jnp.zeros((CHUNK, 128), jnp.bfloat16)
+    for tail in tails:
+        for ref in (kf, vf):
+            ref[pl.ds(tail, UNIT), :] = jnp.zeros((UNIT, width), jnp.float32)
     for f in range(total):
-        kept, at = starts[f]
+        kept, place = starts[f]
         side = f // frames_here
-        local = f % frames_here
-        start = local * PIXELS // 16 * 16
-        lo = local * PIXELS - start
-        inside = (row >= lo) & (row < lo + PIXELS)
+        at = f % frames_here * PIXELS
+        base = at // 16 * 16
 
         def put(k_ref, v_ref):
-            k = k_ref[start : start + FRAME_ROWS, :].astype(jnp.float32)
-            v = v_ref[start : start + FRAME_ROWS, :].astype(jnp.float32)
-            span = pl.ds(at, FRAME_ROWS)
-            kc[span, :] = jnp.where(inside, k, k[lo : lo + 1, :]).astype(jnp.bfloat16)
-            vc[span, :] = jnp.where(inside, v, 0.0).astype(jnp.bfloat16)
-            valid[span, :] = inside.astype(jnp.bfloat16)
+            for src, dst in ((k_ref, kf), (v_ref, vf)):
+                block = src[base : base + 208, :].astype(jnp.float32)
+                dst[pl.ds(place, PIXELS), :] = block[at - base : at - base + PIXELS, :]
 
         @pl.when((kept == 1) & (rank == side))
         def _():
@@ -468,12 +437,14 @@
             put(far_k, far_v)
 
 
+def real_keys(start, size, split, tails, axis, shape):
+    at = lax.broadcasted_iota(jnp.int32, shape, axis) + start
+    return at < jnp.where(at >= split * UNIT, tails[1], tails[0])
+
+
 def query_tiles(rows):
-    parts = max(1, rows // 512)
-    tiles = [(i * 512, 512) for i in range(parts)]
-    last = tiles[-1][0]
-    tiles[-1] = (last, rows - last)
-    return tiles
+    parts = rows // 512
+    return [(i * 512, 512) for i in range(parts)], (parts * 512, rows - parts * 512)
 
 
 def split_heads(rows):
@@ -482,256 +453,376 @@
     return jnp.where(lane < 64, rows, zero), jnp.where(lane < 64, zero, rows)
 
 
-def bias_row(c, split, edge, at, size):
+def clip_bias(late, edge, at, size):
     column = lax.broadcasted_iota(jnp.int32, (1, size), 1) + at
-    same = (column >= edge) == (c >= split)
-    return jnp.where(same, 0.0, FAR)
+    return jnp.where((column >= edge) == late, 0.0, FAR)
+
+
+def sweep(first, end, sizes, body):
+    count = end - first
+    big = sizes[0]
+    main = count // big
+
+    def step(c, carry):
+        body(pl.multiple_of((first + c * big) * UNIT, UNIT), big * UNIT)
+        return carry
+
+    lax.fori_loop(0, main, step, 0)
+    at = first + main * big
+    left = count - main * big
+    for size in sizes[1:]:
+
+        @pl.when((left & size) != 0)
+        def _():
+            body(pl.multiple_of(at * UNIT, UNIT), size * UNIT)
+
+        at = at + (left & size)
 
 
 def attn_fwd_kernel(
     frames_here, info_ref, q_ref, own_k, own_v, far_k, far_v, o_ref, lse_ref, kc_ref, vc_ref,
-    valid_ref, qm, vt, acc, top,
+    qm, qr, vt, acc, accr, top, kf, vf,
 ):
     rows = q_ref.shape[0]
     starts, tails, split, end = key_places(frames_here, info_ref)
-    low, high, edge = chunk_range(frames_here, split, end, info_ref)
-    gather_keys(
-        frames_here, info_ref, starts, tails, own_k, own_v, far_k, far_v, kc_ref, vc_ref, valid_ref
-    )
+    edge = clip_edge(frames_here, info_ref)
+    crossing = (edge > 0) & (edge < rows)
+    low = jnp.where(edge > 0, 0, split)
+    high = jnp.where(edge < rows, end, split)
+    gather_keys(frames_here, info_ref, starts, tails, own_k, own_v, far_k, far_v, kf, vf)
+    tiles, (rest_at, rest) = query_tiles(rows)
     qm[0], qm[1] = split_heads(q_ref[...])
+    for h in range(2):
+        qr[h * rest : h * rest + rest, :] = qm[h, rest_at:rows, :]
     acc[...] = jnp.zeros_like(acc)
-    top[...] = jnp.full_like(top, NEG)
-    tiles = query_tiles(rows)
-    work = [(h, at, size) for h in range(2) for at, size in tiles]
-
-    def prepare(c, carry):
-        span = pl.ds(pl.multiple_of(c * CHUNK, CHUNK), CHUNK)
-        turned = vc_ref[span, :].T
-        ones = valid_ref[span, :].T[:16]
-        for h in range(2):
-            vt[h, 0:64, span] = turned[64 * h : 64 * h + 64]
-            vt[h, 64:80, span] = ones
-        return carry
-
-    lax.fori_loop(low, high, prepare, 0)
-
-    def body(c, carry):
-        span = pl.ds(pl.multiple_of(c * CHUNK, CHUNK), CHUNK)
+    accr[...] = jnp.zeros_like(accr)
+    top[...] = jnp.zeros_like(top)
+
+    def prepare(start, size):
+        span = pl.ds(start, size)
+        kc_ref[span, :] = kf[span, :].astype(jnp.bfloat16)
+        values = vf[span, :].astype(jnp.bfloat16)
+        vc_ref[span, :] = values
+        vt[0:128, span] = values.T
+        real = real_keys(start, size, split, tails, 1, (16, size))
+        vt[128:144, span] = real.astype(jnp.float32).astype(jnp.bfloat16)
+
+    sweep(low, high, (2, 1), prepare)
+
+    def value_rows(h, span):
+        return jnp.concatenate([vt[64 * h : 64 * h + 64, span], vt[128:144, span]], axis=0)
+
+    def plain(work, start, size):
+        span = pl.ds(start, size)
         keys = kc_ref[span, :]
 
         def scores(item):
-            h, at, size = item
-            return dot(keys, qm[h, at : at + size, :], NT)
+            h, at, wide, _ = item
+            return dot(keys, qr[...] if h is None else qm[h, at : at + wide, :], NT)
 
         ahead = scores(work[0])
-        for i, (h, at, size) in enumerate(work):
+        for i, (h, at, wide, bias) in enumerate(work):
             s = ahead
             if i + 1 < len(work):
                 ahead = scores(work[i + 1])
-            bias = bias_row(c, split, edge, at, size)
-            old = top[h : h + 1, at : at + size]
-            new = jnp.maximum(old, jnp.max(s, axis=0, keepdims=True) + bias)
-            p = jnp.exp2(s - (new - bias)).astype(jnp.bfloat16)
-            top[h : h + 1, at : at + size] = new
-            acc[h, :, at : at + size] = acc[h, :, at : at + size] * jnp.exp2(old - new) + dot(
-                vt[h, :, span], p
-            )
-        return carry
-
-    lax.fori_loop(low, high, body, 0)
-    for at, size in tiles:
+            if bias is not None:
+                s = s + bias
+            p = jnp.exp2(s * QUERY_SCALE).astype(jnp.bfloat16)
+            if h is None:
+                accr[:, : 2 * rest] += dot(vt[:, span], p)
+            else:
+                acc[h, :, at : at + wide] += dot(value_rows(h, span), p)
+
+    every = [(h, at, wide, None) for h in range(2) for at, wide in tiles]
+
+    @pl.when(jnp.logical_not(crossing))
+    def _():
+        sweep(low, high, (4, 2, 1), functools.partial(plain, every + [(None, 0, 2 * rest, None)]))
+
+    @pl.when(crossing)
+    def _():
+        for late in (False, True):
+            work = []
+            for at, wide in tiles + [(rest_at, rest)]:
+                if late and at == 0 or not late and at == rest_at:
+                    continue
+                bias = clip_bias(late, edge, at, wide)
+                work += [(h, at, wide, bias) for h in range(2)]
+            body = functools.partial(plain, work)
+            sweep(split if late else 0, end if late else split, (4, 2, 1), body)
+
+    for h in range(2):
+        lanes = slice(h * rest, h * rest + rest)
+        acc[h, 0:64, rest_at:rows] += accr[64 * h : 64 * h + 64, lanes]
+        acc[h, 64:80, rest_at:rows] += accr[128:144, lanes]
+    mass = jnp.concatenate([acc[0, 64:72, :], acc[1, 64:72, :]], axis=0)
+    safe = (jnp.min(mass) >= 2.0**-60) & (jnp.max(mass) <= 2.0**60)
+
+    @pl.when(jnp.logical_not(safe))
+    def _():
+        acc[...] = jnp.zeros_like(acc)
+        top[...] = jnp.full_like(top, NEG)
+
+        def careful(start, size):
+            span = pl.ds(start, size)
+            keys = kc_ref[span, :]
+            real = real_keys(start, size, split, tails, 0, (size, 1))
+            drop = jnp.where(real, 0.0, FAR)
+            late = start >= split * UNIT
+            for h in range(2):
+                for at, wide in tiles + [(rest_at, rest)]:
+                    lanes = slice(at, at + wide)
+                    s = dot(keys, qm[h, lanes, :], NT) * QUERY_SCALE + drop
+                    bias = jnp.where(crossing, clip_bias(late, edge, at, wide), 0.0)
+                    old = top[h : h + 1, lanes]
+                    new = jnp.maximum(old, jnp.max(s, axis=0, keepdims=True) + bias)
+                    p = jnp.exp2(s - (new - bias)).astype(jnp.bfloat16)
+                    top[h : h + 1, lanes] = new
+                    acc[h, :, lanes] = acc[h, :, lanes] * jnp.exp2(old - new) + dot(
+                        value_rows(h, span), p
+                    )
+
+        sweep(low, high, (1,), careful)
+
+    for at, wide in tiles + [(rest_at, rest)]:
+        lanes = slice(at, at + wide)
         halves = []
         for h in range(2):
-            mass = acc[h, 64:65, at : at + size]
-            halves.append(acc[h, 0:64, at : at + size] / mass)
-            lse_ref[0, h : h + 1, at : at + size] = top[h : h + 1, at : at + size] + jnp.log2(mass)
-        o_ref[at : at + size, :] = jnp.concatenate(halves, axis=0).T.astype(jnp.bfloat16)
+            sums = acc[h, 64:65, lanes]
+            halves.append(acc[h, 0:64, lanes] / sums)
+            lse_ref[0, h : h + 1, lanes] = top[h : h + 1, lanes] + jnp.log2(sums)
+        o_ref[lanes, :] = jnp.concatenate(halves, axis=0).T.astype(jnp.bfloat16)
 
 
 def attn_fwd(info, q, own_k, own_v, far_k, far_v, old, part, frames_here):
     rows, width = q.shape
     pairs = width // 256
     length = compact_rows(2 * frames_here)
+    rest = rows % 512
     block = pl.BlockSpec((rows, 128), lambda p, *_: (0, p))
     column = pl.BlockSpec((rows, 128), lambda p, *_: (0, p + part * pairs))
-    keys = pl.BlockSpec((length, 128), lambda p, *_: (0, p))
-    olds = [] if old is None else [old]
+    keys = pl.BlockSpec((length, 128), lambda p, *_: (0, p + part * pairs))
 
     def kernel(*refs):
-        return attn_fwd_kernel(frames_here, *refs[:6], *refs[6 + len(olds) :])
+        return attn_fwd_kernel(frames_here, *refs[:6], *refs[6 + len(old) :])
 
     return pl.pallas_call(
         kernel,
         out_shape=(
             jax.ShapeDtypeStruct((rows, width), jnp.bfloat16),
-            jax.ShapeDtypeStruct((pairs, 8, rows), jnp.float32),
-            jax.ShapeDtypeStruct((length, width // 2), jnp.bfloat16),
-            jax.ShapeDtypeStruct((length, width // 2), jnp.bfloat16),
-            jax.ShapeDtypeStruct((length, 128), jnp.bfloat16),
+            jax.ShapeDtypeStruct((2 * pairs, 8, rows), jnp.float32),
+            jax.ShapeDtypeStruct((length, width), jnp.bfloat16),
+            jax.ShapeDtypeStruct((length, width), jnp.bfloat16),
         ),
         grid_spec=pltpu.PrefetchScalarGridSpec(
             num_scalar_prefetch=1,
             grid=(pairs,),
-            in_specs=[column, block, block, block, block] + [pl.BlockSpec(memory_space=pl.ANY)] * len(olds),
+            in_specs=[column, block, block, block, block]
+            + [pl.BlockSpec(memory_space=pl.ANY)] * len(old),
             out_specs=[
                 column,
-                pl.BlockSpec((1, 8, rows), lambda p, *_: (p, 0, 0)),
+                pl.BlockSpec((1, 8, rows), lambda p, *_: (p + part * pairs, 0, 0)),
                 keys,
                 keys,
-                pl.BlockSpec((length, 128), lambda p, *_: (0, 0)),
             ],
             scratch_shapes=[
                 pltpu.VMEM((2, rows, 128), jnp.bfloat16),
-                pltpu.VMEM((2, 80, length), jnp.bfloat16),
+                pltpu.VMEM((2 * rest, 128), jnp.bfloat16),
+                pltpu.VMEM((144, length), jnp.bfloat16),
                 pltpu.VMEM((2, 80, rows), jnp.float32),
+                pltpu.VMEM((144, 128), jnp.float32),
                 pltpu.VMEM((8, rows), jnp.float32),
+                pltpu.VMEM((length, 128), jnp.float32),
+                pltpu.VMEM((length, 128), jnp.float32),
             ],
         ),
-        input_output_aliases={6: 0} if olds else {},
+        input_output_aliases={6 + i: i for i in range(len(old))},
         compiler_params=params(),
         cost_estimate=cost(4e10, 1e7),
         name="attn_fwd",
-    )(info, q, own_k, own_v, far_k, far_v, *olds)
+    )(info, q, own_k, own_v, far_k, far_v, *old)
 
 
 def attn_bwd_kernel(
-    frames_here, info_ref, q_ref, k_ref, v_ref, valid_ref, o_ref, do_ref, lse_ref,
-    dq_ref, own_dk, own_dv, far_dk, far_dv, qm, dom, kt, dqt, delta, dk_all, dv_all,
+    frames_here, info_ref, q_ref, k_ref, v_ref, o_ref, do_ref, lse_ref,
+    dq_ref, own_dk, own_dv, away, qm, qr, dom, dor, dqt, dqr, delta, dk_all, dv_all, back,
 ):
     rows = q_ref.shape[0]
     total = 2 * frames_here
     length = info_ref[total]
     rank = info_ref[total + 1]
     starts, _, split, end = key_places(frames_here, info_ref)
-    low, high, edge = chunk_range(frames_here, split, end, info_ref)
+    edge = clip_edge(frames_here, info_ref)
+    crossing = (edge > 0) & (edge < rows)
+    low = jnp.where(edge > 0, 0, split)
+    high = jnp.where(edge < rows, end, split)
+    tiles, (rest_at, rest) = query_tiles(rows)
     qm[0], qm[1] = split_heads(q_ref[...])
     dom[0], dom[1] = split_heads(do_ref[...])
+    for h in range(2):
+        qr[h * rest : h * rest + rest, :] = qm[h, rest_at:rows, :]
+        dor[h * rest : h * rest + rest, :] = dom[h, rest_at:rows, :]
     dqt[...] = jnp.zeros_like(dqt)
-    tiles = query_tiles(rows)
-    work = [(h, at, size) for h in range(2) for at, size in tiles]
-    for at, size in tiles:
-        span = slice(at, at + size)
+    dqr[...] = jnp.zeros_like(dqr)
+    for at, wide in tiles + [(rest_at, rest)]:
+        span = slice(at, at + wide)
         prod = (o_ref[span, :].astype(jnp.float32) * do_ref[span, :].astype(jnp.float32)).T
         for h in range(2):
             delta[h : h + 1, span] = jnp.sum(prod[64 * h : 64 * h + 64], axis=0, keepdims=True)
 
-    def prepare(c, carry):
-        span = pl.ds(pl.multiple_of(c * CHUNK, CHUNK), CHUNK)
-        turned = (k_ref[span, :] * valid_ref[span, :]).T
-        for h in range(2):
-            kt[h, :, span] = turned[64 * h : 64 * h + 64]
-        return carry
-
-    lax.fori_loop(low, high, prepare, 0)
-
-    def body(c, carry):
-        span = pl.ds(pl.multiple_of(c * CHUNK, CHUNK), CHUNK)
+    def both_rows(ref, lead):
+        pieces = [ref[(*lead, slice(h, h + 1), slice(rest_at, rows))] for h in range(2)]
+        return jnp.concatenate(pieces, axis=1)
+
+    def visit(work, start, size):
+        span = pl.ds(start, size)
         keys = k_ref[span, :]
         values = v_ref[span, :]
+        turned = keys.T
+
+        def rows_of(item):
+            h, at, wide, _ = item
+            if h is None:
+                return qr[...], dor[...]
+            return qm[h, at : at + wide, :], dom[h, at : at + wide, :]
 
         def scores(item):
-            h, at, size = item
-            return (
-                dot(keys, qm[h, at : at + size, :], NT),
-                dot(values, dom[h, at : at + size, :], NT),
-            )
-
-        dk = jnp.zeros((CHUNK, 128), jnp.float32)
-        dv = jnp.zeros((CHUNK, 128), jnp.float32)
+            queries, douts = rows_of(item)
+            return dot(keys, queries, NT), dot(values, douts, NT)
+
+        dk = jnp.zeros((size, 128), jnp.float32)
+        dv = jnp.zeros((size, 128), jnp.float32)
         ahead = scores(work[0])
-        for i, (h, at, size) in enumerate(work):
+        for i, item in enumerate(work):
+            h, at, wide, bias = item
             s, dp = ahead
             if i + 1 < len(work):
                 ahead = scores(work[i + 1])
-            bias = bias_row(c, split, edge, at, size)
-            p = jnp.exp2(s - (lse_ref[0, h : h + 1, at : at + size] - bias))
-            ds = (p * (dp - delta[h : h + 1, at : at + size])).astype(jnp.bfloat16)
-            dv = dv + dot(p.astype(jnp.bfloat16), dom[h, at : at + size, :])
-            dk = dk + dot(ds, qm[h, at : at + size, :])
-            dqt[h, :, at : at + size] += dot(kt[h, :, span], ds)
-        dk_all[span, :] = (dk * LN2).astype(jnp.bfloat16)
-        dv_all[span, :] = dv.astype(jnp.bfloat16)
-        return carry
-
-    lax.fori_loop(low, high, body, 0)
-    for at, size in tiles:
-        both = jnp.concatenate([dqt[0, :, at : at + size], dqt[1, :, at : at + size]], axis=0)
-        dq_ref[at : at + size, :] = (both * 0.125).T.astype(jnp.bfloat16)
-
-    first = rank * frames_here
-    early = first < length
-    late = first + frames_here > length
-    quad = 4
-    for f0 in range(0, total, quad):
-        at0 = f0 % frames_here * PIXELS
+            queries, douts = rows_of(item)
+            if h is None:
+                lse, inner = both_rows(lse_ref, (0,)), both_rows(delta, ())
+            else:
+                lse = lse_ref[0, h : h + 1, at : at + wide]
+                inner = delta[h : h + 1, at : at + wide]
+            if bias is not None:
+                lse = lse - bias
+            p = jnp.exp2(jnp.minimum(s * QUERY_SCALE - lse, 0.0))
+            ds = (p * (dp - inner)).astype(jnp.bfloat16)
+            dv = dv + dot(p.astype(jnp.bfloat16), douts)
+            dk = dk + dot(ds, queries)
+            if h is None:
+                dqr[:, : 2 * rest] += dot(turned, ds)
+            else:
+                dqt[h, :, at : at + wide] += dot(turned[64 * h : 64 * h + 64], ds)
+        return dk, dv
+
+    def fresh(work, start, size):
+        dk, dv = visit(work, start, size)
+        dk_all[pl.ds(start, size), :] = dk * 0.125
+        dv_all[pl.ds(start, size), :] = dv
+
+    every = [(h, at, wide, None) for h in range(2) for at, wide in tiles]
+
+    @pl.when(jnp.logical_not(crossing))
+    def _():
+        sweep(low, high, (2, 1), functools.partial(fresh, every + [(None, 0, 2 * rest, None)]))
+
+    @pl.when(crossing)
+    def _():
+        for late in (False, True):
+            work = []
+            for at, wide in tiles + [(rest_at, rest)]:
+                if late and at == 0 or not late and at == rest_at:
+                    continue
+                bias = clip_bias(late, edge, at, wide)
+                work += [(h, at, wide, bias) for h in range(2)]
+            body = functools.partial(fresh, work)
+            sweep(split if late else 0, end if late else split, (1,), body)
+
+    for h in range(2):
+        lanes = slice(h * rest, h * rest + rest)
+        dqt[h, :, rest_at:rows] += dqr[64 * h : 64 * h + 64, lanes]
+    for at, wide in tiles + [(rest_at, rest)]:
+        both = jnp.concatenate([dqt[0, :, at : at + wide], dqt[1, :, at : at + wide]], axis=0)
+        dq_ref[at : at + wide, :] = (both * 0.125).T.astype(jnp.bfloat16)
+
+    for side in range(2):
 
         def put(k_out, v_out):
-            for src, dst in ((dk_all, k_out), (dv_all, v_out)):
-                parts = []
-                for f in range(f0, f0 + quad):
-                    kept, at = starts[f]
-                    lo = f % frames_here * PIXELS % 16
-                    use = (kept == 1) & jnp.where(f >= length, late, early)
-                    block = src[pl.ds(at, FRAME_ROWS), :].astype(jnp.float32)
-                    parts.append(jnp.where(use, block[lo : lo + PIXELS, :], 0.0))
-                dst[at0 : at0 + quad * PIXELS, :] = jnp.concatenate(parts, axis=0).astype(
-                    jnp.bfloat16
-                )
-
-        @pl.when(rank == f0 // frames_here)
+            for src, out in ((dk_all, k_out), (dv_all, v_out)):
+                for f in range(side * frames_here, side * frames_here + frames_here):
+                    kept, place = starts[f]
+                    use = (kept == 1) & jnp.where(f >= length, edge < rows, edge > 0)
+                    at = f % frames_here * PIXELS
+                    back[at : at + PIXELS, :] = jnp.where(use, src[pl.ds(place, PIXELS), :], 0.0)
+                out(back[...].astype(jnp.bfloat16))
+
+        def write(ref, lanes):
+            def store(value):
+                ref[:, lanes] = value
+
+            return store
+
+        @pl.when(rank == side)
         def _():
-            put(own_dk, own_dv)
-
-        @pl.when(rank != f0 // frames_here)
+            put(write(own_dk, slice(0, 128)), write(own_dv, slice(0, 128)))
+
+        @pl.when(rank != side)
         def _():
-            put(far_dk, far_dv)
-
-
-def attn_bwd(info, q, kc, vc, valid, o, do, lse, pair, frames_here, after):
-    rows, width = q.shape
+            put(write(away, slice(0, 128)), write(away, slice(128, 256)))
+
+
+def attn_bwd(info, q, kc, vc, o, do, lse, pairs, frames_here, after):
+    rows = q.shape[0]
     length = kc.shape[0]
-    local = pair % (width // 256)
-    rowspec = pl.BlockSpec((rows, 128), lambda p, *_: (0, pair))
-    keyspec = pl.BlockSpec((length, 128), lambda p, *_: (0, local))
-    whole = pl.BlockSpec((rows, 128), lambda p, *_: (0, 0))
+    rest = rows % 512
+    first = pairs[0]
+    apart = pairs[-1] - first
+    rowspec = pl.BlockSpec((rows, 128), lambda p, *_: (0, first + apart * p))
+    keyspec = pl.BlockSpec((length, 128), lambda p, *_: (0, first + apart * p))
+    out = pl.BlockSpec((rows, 128), lambda p, *_: (0, p))
 
     def kernel(*refs):
-        return attn_bwd_kernel(frames_here, *refs[:8], *refs[8 + len(after) :])
+        return attn_bwd_kernel(frames_here, *refs[:7], *refs[7 + len(after) :])
 
     return pl.pallas_call(
         kernel,
-        out_shape=(jax.ShapeDtypeStruct((rows, 128), jnp.bfloat16),) * 5,
+        out_shape=(jax.ShapeDtypeStruct((rows, 128 * len(pairs)), jnp.bfloat16),) * 3
+        + (jax.ShapeDtypeStruct((rows, 256 * len(pairs)), jnp.bfloat16),),
         grid_spec=pltpu.PrefetchScalarGridSpec(
             num_scalar_prefetch=1,
-            grid=(1,),
+            grid=(len(pairs),),
             in_specs=[
                 rowspec,
                 keyspec,
                 keyspec,
-                pl.BlockSpec((length, 128), lambda p, *_: (0, 0)),
                 rowspec,
                 rowspec,
-                pl.BlockSpec((1, 8, rows), lambda p, *_: (local, 0, 0)),
+                pl.BlockSpec((1, 8, rows), lambda p, *_: (first + apart * p, 0, 0)),
             ]
             + [pl.BlockSpec(memory_space=pl.ANY)] * len(after),
-            out_specs=[whole] * 5,
+            out_specs=[out] * 3 + [pl.BlockSpec((rows, 256), lambda p, *_: (0, p))],
             scratch_shapes=[
                 pltpu.VMEM((2, rows, 128), jnp.bfloat16),
+                pltpu.VMEM((2 * rest, 128), jnp.bfloat16),
                 pltpu.VMEM((2, rows, 128), jnp.bfloat16),
-                pltpu.VMEM((2, 64, length), jnp.bfloat16),
+                pltpu.VMEM((2 * rest, 128), jnp.bfloat16),
                 pltpu.VMEM((2, 64, rows), jnp.float32),
+                pltpu.VMEM((128, 128), jnp.float32),
                 pltpu.VMEM((8, rows), jnp.float32),
-                pltpu.VMEM((length, 128), jnp.bfloat16),
-                pltpu.VMEM((length, 128), jnp.bfloat16),
+                pltpu.VMEM((length, 128), jnp.float32),
+                pltpu.VMEM((length, 128), jnp.float32),
+                pltpu.VMEM((rows, 128), jnp.float32),
             ],
         ),
         compiler_params=params(),
-        cost_estimate=cost(3e10, 1e7),
+        cost_estimate=cost(3e10 * len(pairs), 1e7),
         name="attn_bwd",
-    )(info, q, kc, vc, valid, o, do, lse, *after)
+    )(info, q, kc, vc, o, do, lse, *after)
 
 
 TILE = 224
+PART = 384
 INV_SQRT2 = 0.7071067811865476
 INV_SQRT_2PI = 0.3989422804014327
 QUERY_SCALE = 0.125 * LOG2E
@@ -771,16 +862,25 @@
     return rstd * (dxhat - jnp.mean(dxhat, axis=-1, keepdims=True) - xhat * along)
 
 
+def line(ref):
+    return ref[...].reshape(1, -1)
+
+
+def vector_spec(size):
+    return pl.BlockSpec((size,), lambda i: (0,))
+
+
 def rows_sum(x):
     return jnp.sum(x, axis=0, keepdims=True)
 
 
 def project_kernel(x_ref, gain_ref, shift_ref, wk, wv, bias_ref, n_ref, k_ref, v_ref):
     xhat, _ = ln_parts(x_ref[...].astype(jnp.float32))
-    normed = (xhat * gain_ref[...] + shift_ref[...]).astype(jnp.bfloat16)
+    normed = (xhat * line(gain_ref) + line(shift_ref)).astype(jnp.bfloat16)
     n_ref[...] = normed
+    half = k_ref.shape[1]
     k_ref[...] = dot(normed, wk[...]).astype(jnp.bfloat16)
-    v_ref[...] = (dot(normed, wv[...]) + bias_ref[...]).astype(jnp.bfloat16)
+    v_ref[...] = (dot(normed, wv[...]) + line(bias_ref)[:, :half]).astype(jnp.bfloat16)
 
 
 def weight_spec(width, size, column):
@@ -796,11 +896,11 @@
         grid=(rows // TILE,),
         in_specs=[
             tile_spec(width),
-            whole_spec((1, width)),
-            whole_spec((1, width)),
+            vector_spec(width),
+            vector_spec(width),
             weight_spec(width, half, 2),
             weight_spec(width, half, 4),
-            weight_spec(1, half, 0),
+            vector_spec(width),
         ],
         out_specs=[tile_spec(width), tile_spec(half), tile_spec(half)],
         compiler_params=params(),
@@ -812,8 +912,9 @@
 def project_more_kernel(n_ref, wq, wk, wv, q_bias, v_bias, q_ref, k_ref, v_ref):
     normed = n_ref[...]
     k_ref[...] = dot(normed, wk[...]).astype(jnp.bfloat16)
-    v_ref[...] = (dot(normed, wv[...]) + v_bias[...]).astype(jnp.bfloat16)
-    q_ref[...] = ((dot(normed, wq[...]) + q_bias[...]) * QUERY_SCALE).astype(jnp.bfloat16)
+    half = v_ref.shape[1]
+    v_ref[...] = (dot(normed, wv[...]) + line(v_bias)[:, half:]).astype(jnp.bfloat16)
+    q_ref[...] = (dot(normed, wq[...]) + line(q_bias)).astype(jnp.bfloat16)
 
 
 def project_more(normed, w, q_bias, v_bias):
@@ -828,8 +929,8 @@
             weight_spec(width, width, 0),
             weight_spec(width, half, 3),
             weight_spec(width, half, 5),
-            whole_spec((1, width)),
-            weight_spec(1, half, 1),
+            vector_spec(width),
+            vector_spec(width),
         ],
         out_specs=[tile_spec(width), tile_spec(half), tile_spec(half)],
         compiler_params=params(),
@@ -845,16 +946,17 @@
     width = x_ref.shape[1]
     inner = w_up.shape[1]
     parts = inner // width
-    middle = x_ref[...].astype(jnp.float32) + dot(a_ref[...], w_out[...]) + b_out[...]
+    middle = x_ref[...].astype(jnp.float32) + dot(a_ref[...], w_out[...]) + line(b_out)
     mid_ref[...] = middle.astype(jnp.bfloat16)
     xhat, _ = ln_parts(middle)
-    n2 = (xhat * gain2[...] + shift2[...]).astype(jnp.bfloat16)
+    n2 = (xhat * line(gain2) + line(shift2)).astype(jnp.bfloat16)
     n2_ref[...] = n2
-    out = middle + b_down[...]
+    out = middle + line(b_down)
+    up_shift = line(b_up)
 
     def raise_part(j):
         span = slice(j * width, (j + 1) * width)
-        return dot(n2, w_up[:, span]) + b_up[:, span]
+        return dot(n2, w_up[:, span]) + up_shift[:, span]
 
     ahead = raise_part(0)
     for j in range(parts):
@@ -870,13 +972,13 @@
         out = out + dot(hid, w_down[span, :])
     out_ref[...] = out.astype(jnp.bfloat16)
     xhat, _ = ln_parts(out)
-    n3_ref[...] = (xhat * gain3[...] + shift3[...]).astype(jnp.bfloat16)
+    n3_ref[...] = (xhat * line(gain3) + line(shift3)).astype(jnp.bfloat16)
 
 
 def mlp_fwd(x, attended, w_out, b_out, gain2, shift2, w_up, b_up, w_down, b_down, gain3, shift3):
     rows, width = x.shape
     inner = w_up.shape[1]
-    vec = whole_spec((1, width))
+    vec = vector_spec(width)
     return pl.pallas_call(
         mlp_fwd_kernel,
         out_shape=(
@@ -886,7 +988,7 @@
         grid=(rows // TILE,),
         in_specs=[
             tile_spec(width), tile_spec(width), whole_spec(w_out.shape), vec, vec, vec,
-            whole_spec(w_up.shape), whole_spec((1, inner)), whole_spec(w_down.shape), vec, vec, vec,
+            whole_spec(w_up.shape), vector_spec(inner), whole_spec(w_down.shape), vec, vec, vec,
         ],
         out_specs=[
             tile_spec(width), tile_spec(width), tile_spec(inner),
@@ -913,7 +1015,11 @@
         sums_ref[...] = jnp.zeros_like(sums_ref)
 
     def add(row, value):
-        sums_ref[row : row + 1, :] += rows_sum(value)
+        total = rows_sum(value)
+        middle = total.shape[1] // 2
+        below = sums_ref.shape[0] // 2 + row
+        sums_ref[row : row + 1, :] += total[:, :middle]
+        sums_ref[below : below + 1, :] += total[:, middle:]
 
     dn3 = dot(side_ref[:, :128], w_first[...])
     xhat, rstd = ln_parts(out_ref[...].astype(jnp.float32))
@@ -921,7 +1027,7 @@
     add(3, dn3)
     d_out = (
         cot_ref[...].astype(jnp.float32)
-        + ln_back(dn3, gain3[...], xhat, rstd)
+        + ln_back(dn3, line(gain3), xhat, rstd)
         + dot(side_ref[:, 128:192], pool_ref[...])
     )
     d_down = d_out.astype(jnp.bfloat16)
@@ -945,7 +1051,7 @@
     xhat, rstd = ln_parts(mid_ref[...].astype(jnp.float32))
     add(0, dn2 * xhat)
     add(1, dn2)
-    d_branch = (d_out + ln_back(dn2, gain2[...], xhat, rstd)).astype(jnp.bfloat16)
+    d_branch = (d_out + ln_back(dn2, line(gain2), xhat, rstd)).astype(jnp.bfloat16)
     dbranch_ref[...] = d_branch
     add(5, d_branch.astype(jnp.float32))
     datt_ref[...] = dot(d_branch, w_out[...], NT).astype(jnp.bfloat16)
@@ -954,12 +1060,12 @@
 def mlp_bwd(cot, out, side, pool, w_first, gain3, w_down, slope, w_up, mid, gain2, w_out):
     rows, width = cot.shape
     inner = w_up.shape[1]
-    vec = whole_spec((1, width))
+    vec = vector_spec(width)
     return pl.pallas_call(
         mlp_bwd_kernel,
         out_shape=(
             low_shape(rows, width), low_shape(rows, inner), low_shape(rows, width),
-            low_shape(rows, width), jax.ShapeDtypeStruct((16, width), jnp.float32),
+            low_shape(rows, width), jax.ShapeDtypeStruct((32, width // 2), jnp.float32),
         ),
         grid=(rows // TILE,),
         in_specs=[
@@ -969,7 +1075,7 @@
         ],
         out_specs=[
             tile_spec(width), tile_spec(inner), tile_spec(width), tile_spec(width),
-            pl.BlockSpec((16, width), lambda i: (0, 0)),
+            pl.BlockSpec((32, width // 2), lambda i: (0, 0)),
         ],
         compiler_params=params(),
         cost_estimate=cost(
@@ -989,7 +1095,11 @@
         sums_ref[...] = jnp.zeros_like(sums_ref)
 
     def add(row, value):
-        sums_ref[row : row + 1, :] += rows_sum(value)
+        total = rows_sum(value)
+        middle = total.shape[1] // 2
+        below = sums_ref.shape[0] // 2 + row
+        sums_ref[row : row + 1, :] += total[:, :middle]
+        sums_ref[below : below + 1, :] += total[:, middle:]
 
     def join(part):
         return jnp.concatenate([r[...] for r in part], axis=1)
@@ -1012,7 +1122,7 @@
     add(2, dq.astype(jnp.float32))
     add(3, dv.astype(jnp.float32))
     grad_ref[...] = (
-        branch_ref[...].astype(jnp.float32) + ln_back(dn, gain[...], xhat, rstd)
+        branch_ref[...].astype(jnp.float32) + ln_back(dn, line(gain), xhat, rstd)
     ).astype(jnp.bfloat16)
 
 
@@ -1021,16 +1131,19 @@
     pairs = width // 128
     return pl.pallas_call(
         functools.partial(final_bwd_kernel, pairs),
-        out_shape=(low_shape(rows, width), jax.ShapeDtypeStruct((8, width), jnp.float32)),
+        out_shape=(low_shape(rows, width), jax.ShapeDtypeStruct((16, width // 2), jnp.float32)),
         grid=(rows // TILE,),
-        in_specs=[tile_spec(128)] * (5 * pairs)
+        in_specs=[
+            pl.BlockSpec((TILE, 128), functools.partial(lambda c, i: (i, c), column))
+            for _, column in pieces
+        ]
         + [tile_spec(width)] * 2
-        + [whole_spec((1, width)), whole_spec(w.shape)],
-        out_specs=[tile_spec(width), pl.BlockSpec((8, width), lambda i: (0, 0))],
+        + [vector_spec(width), whole_spec(w.shape)],
+        out_specs=[tile_spec(width), pl.BlockSpec((16, width // 2), lambda i: (0, 0))],
         compiler_params=params(),
         cost_estimate=cost(6 * rows * width * width, 16 * rows * width),
         name="final_bwd",
-    )(*pieces, x, branch, gain, w)
+    )(*[array for array, _ in pieces], x, branch, gain, w)
 
 
 def grid_masks(frames, lanes):
@@ -1049,7 +1162,7 @@
 
 def learner_kernel(
     frames, info_ref, weight_ref, n3_ref, out_ref, pool_ref, wt_ref, cw_ref, cwt_ref, cb_ref,
-    mask_ref, side_ref, pooled_ref, small_ref, gfirst_ref,
+    mask_ref, side_ref, pooled_ref, small_ref, keep_ref, send_ref, rounds, seqs,
 ):
     rows = n3_ref.shape[0]
     lanes = mask_ref.shape[1]
@@ -1099,7 +1212,10 @@
     maps = 1.0 / (1.0 + jnp.exp(-levels[3]))
     total = rows_sum(maps)
     meet = 0.5 * (total * total - rows_sum(maps * maps)) * live
-    small_ref[3] = jnp.zeros((8, 128), jnp.float32) + jnp.sum(meet)
+    small_ref[...] = jnp.zeros_like(small_ref)
+    small_ref[8:9, 128:256] = jnp.zeros((1, 128), jnp.float32) + jnp.sum(meet)
+    shifts = jnp.zeros((8, 128), jnp.float32)
+    lane = lax.broadcasted_iota(jnp.int32, (8, 128), 1)
 
     owner = lax.broadcasted_iota(jnp.int32, (8 * frames, lanes), 0) // 8
     mine = owner.astype(jnp.float32) == frame_of
@@ -1114,20 +1230,28 @@
     d_maps = d_maps * live + weight_ref[0] * live * (total - maps)
     d_level = d_maps * maps * (1.0 - maps)
     for n in (2, 1, 0):
-        small_ref[4 + n + 1] = jnp.broadcast_to(
-            jnp.sum(d_level, axis=1, keepdims=True), (8, 128)
-        )
+        shifts = jnp.where(lane == n + 1, jnp.sum(d_level, axis=1, keepdims=True), shifts)
         d_taps = spread_taps(d_level)
-        small_ref[n] = jnp.concatenate(
-            [exact(hiddens[n], d_taps, NT), jnp.zeros((8, 56), jnp.float32)], axis=1
-        )
+        small_ref[0:8, 128 * n : 128 * n + 72] = exact(hiddens[n], d_taps, NT)
         d_hidden = exact(cw_ref[n], d_taps)
         x = levels[n]
         bell = jnp.exp(-0.5 * x * x) * INV_SQRT_2PI
         d_level = d_hidden * (area_of(x) + x * bell) * inside
-    small_ref[4] = jnp.broadcast_to(jnp.sum(d_level, axis=1, keepdims=True), (8, 128))
+    shifts = jnp.where(lane == 0, jnp.sum(d_level, axis=1, keepdims=True), shifts)
+    small_ref[8:16, 0:8] = shifts.T[0:8, :]
     d_first = spread_taps(d_level)[:, :rows]
-    gfirst_ref[...] = dot(d_first.astype(jnp.bfloat16), n3_ref[...])
+    grad = dot(d_first.astype(jnp.bfloat16), n3_ref[...])
+    grad = jnp.concatenate([grad, jnp.zeros((56, grad.shape[1]), jnp.float32)], axis=0).T
+    columns = 9 * MAPS // 2
+    lane = lax.broadcasted_iota(jnp.int32, grad.shape, 1)
+    left = jnp.where(lane < columns, grad, 0.0).astype(jnp.bfloat16)
+    right = jnp.where(lane < columns, pltpu.roll(grad, 128 - columns, 1), 0.0).astype(jnp.bfloat16)
+    size = grad.shape[0] // seqs // 3
+    for ref, side in ((keep_ref, 0), (send_ref, 1)):
+        value = jnp.where(rank == side, left, right)
+        for o in range(seqs):
+            parts = [value[(3 * o + t) * size : (3 * o + t + 1) * size, :] for t in range(3)]
+            put_rows(ref, block_place(o, rounds) * size, jnp.concatenate(parts, axis=1))
     tall = jnp.concatenate(
         [
             d_first,
@@ -1140,7 +1264,7 @@
     side_ref[...] = tall.T.astype(jnp.bfloat16)
 
 
-def learner(info, weight, n3, out, pool, w_first, conv_weights, conv_biases):
+def learner(info, weight, n3, out, pool, w_first, conv_weights, conv_biases, rounds, seqs):
     rows, width = n3.shape
     frames = rows // PIXELS
     lanes = -(-rows // 128) * 128
@@ -1148,15 +1272,16 @@
     sm = pl.BlockSpec(memory_space=pltpu.SMEM)
     masks = jnp.asarray(grid_masks(frames, lanes))
     return pl.pallas_call(
-        functools.partial(learner_kernel, frames),
+        functools.partial(learner_kernel, frames, rounds=rounds, seqs=seqs),
         out_shape=(
             low_shape(rows, 256),
             low_shape(8 * frames, width),
-            jax.ShapeDtypeStruct((8, 8, 128), jnp.float32),
-            jax.ShapeDtypeStruct((9 * MAPS, width), jnp.float32),
+            jax.ShapeDtypeStruct((16, PART), jnp.float32),
+            low_shape(width // 3, PART),
+            low_shape(width // 3, PART),
         ),
         in_specs=[sm, sm] + [vm] * 8,
-        out_specs=(vm, vm, vm, vm),
+        out_specs=(vm,) * 5,
         compiler_params=pltpu.CompilerParams(vmem_limit_bytes=VMEM_LIMIT),
         cost_estimate=cost(2e10, 4 * rows * width),
         name="learner",
@@ -1182,32 +1307,45 @@
     return place
 
 
+def put_rows(ref, at, value):
+    if not isinstance(at, int):
+        at = pl.multiple_of(at, 16)
+    ref[pl.ds(at, value.shape[0]), :] = value
+
+
 def put_blocks(ref, value, first_owner, owners, rounds):
     size = value.shape[0] // owners
     for o in range(owners):
         place = block_place(first_owner + o, rounds)
-        at = place * size
-        if not isinstance(at, int):
-            at = pl.multiple_of(at, 16)
-        ref[pl.ds(at, size), :] = value[o * size : (o + 1) * size, :]
+        put_rows(ref, place * size, value[o * size : (o + 1) * size, :])
 
 
 def grad_by_columns_kernel(rounds, seqs, info_ref, a_ref, b_ref, keep_ref, send_ref, turned):
     step = pl.program_id(0)
+    half = pl.num_programs(0) // 2
 
     @pl.when(step == 0)
     def _():
         turned[...] = a_ref[...].T
 
     got = dot(turned[...], b_ref[...]).astype(jnp.bfloat16)
-
-    @pl.when(step < pl.num_programs(0) // 2)
+    parts = got.shape[1] // PART
+    size = got.shape[0] // seqs
+
+    def put(ref):
+        for o in range(seqs):
+            base = block_place(o, rounds) * size * parts * half
+            for i in range(parts):
+                at = base + (lax.rem(step, half) * parts + i) * size
+                put_rows(ref, at, got[o * size : o * size + size, i * PART : i * PART + PART])
+
+    @pl.when(step < half)
     def _():
-        put_blocks(keep_ref, got, 0, seqs, rounds)
-
-    @pl.when(step >= pl.num_programs(0) // 2)
+        put(keep_ref)
+
+    @pl.when(step >= half)
     def _():
-        put_blocks(send_ref, got, 0, seqs, rounds)
+        put(send_ref)
 
 
 def grad_by_columns(info, a, b, rounds, seqs, at):
@@ -1215,7 +1353,8 @@
     wide = b.shape[1]
     block = min(768, wide // 2)
     half = wide // 2 // block
-    out = jax.ShapeDtypeStruct((tall, wide // 2), jnp.bfloat16)
+    out = jax.ShapeDtypeStruct((tall * wide // 2 // PART, PART), jnp.bfloat16)
+    whole = pl.BlockSpec(out.shape, lambda j, info: (0, 0))
     return pl.pallas_call(
         functools.partial(grad_by_columns_kernel, rounds, seqs),
         out_shape=(out, out),
@@ -1229,10 +1368,7 @@
                     lambda j, info: (0, jnp.where(j < half, info[at], 1 - info[at]) * half + j % half),
                 ),
             ],
-            out_specs=[
-                pl.BlockSpec((tall, block), lambda j, info: (0, jnp.minimum(j, half - 1))),
-                pl.BlockSpec((tall, block), lambda j, info: (0, jnp.maximum(j - half, 0))),
-            ],
+            out_specs=[whole, whole],
             scratch_shapes=[pltpu.VMEM((tall, rows), jnp.bfloat16)],
         ),
         compiler_params=params(),
@@ -1248,7 +1384,6 @@
 
 
 def grad_by_rows_kernel(rounds, seqs, at, info_ref, a_ref, b_ref, keep_ref, send_ref):
-    steps = pl.num_programs(0)
     step = pl.program_id(0)
     got = dot(a_ref[...], b_ref[...], TN).astype(jnp.bfloat16)
     keep, send = pick_half(info_ref[at], got)
@@ -1279,9 +1414,9 @@
     )(info, a, b)
 
 
-def grad_pieces_kernel(
-    rounds, seqs, at, info_ref, n_ref, q0, q1, k0, x0, k1, x1, v0, y0, v1, y1, keep_ref, send_ref
-):
+def grad_pieces_kernel(rounds, seqs, at, info_ref, n_ref, *refs):
+    (q0, k0, x0, v0, y0), (q1, k1, x1, v1, y1) = refs[:5], refs[5:10]
+    keep_ref, send_ref = refs[-2:]
     first = jnp.concatenate([q0[...], q1[...], low_sum(k0[...], x0[...])], axis=1)
     second = jnp.concatenate(
         [low_sum(k1[...], x1[...]), low_sum(v0[...], y0[...]), low_sum(v1[...], y1[...])], axis=1
@@ -1293,157 +1428,256 @@
     put_blocks(send_ref, send, 0, seqs, rounds)
 
 
-def grad_pieces(info, n1, pieces, rounds, seqs, at):
-    (q0, k0, x0, v0, y0), (q1, k1, x1, v1, y1) = pieces
+def grad_pieces(info, n1, pieces, rounds, seqs, at, after):
     rows, tall = n1.shape
-    out = jax.ShapeDtypeStruct((tall, 384), jnp.bfloat16)
-    vm = pl.BlockSpec(memory_space=pltpu.VMEM)
-    sm = pl.BlockSpec(memory_space=pltpu.SMEM)
+    out = jax.ShapeDtypeStruct((tall, PART), jnp.bfloat16)
+    flat = [piece for pair in pieces for piece in pair]
+    whole = pl.BlockSpec((tall, PART), lambda i, info: (0, 0))
     return pl.pallas_call(
         functools.partial(grad_pieces_kernel, rounds, seqs, at),
         out_shape=(out, out),
-        in_specs=[sm] + [vm] * 11,
-        out_specs=(vm, vm),
-        compiler_params=pltpu.CompilerParams(vmem_limit_bytes=VMEM_LIMIT),
+        grid_spec=pltpu.PrefetchScalarGridSpec(
+            num_scalar_prefetch=1,
+            grid=(1,),
+            in_specs=[pl.BlockSpec((rows, tall), lambda i, info: (0, 0))]
+            + [
+                pl.BlockSpec((rows, 128), functools.partial(lambda c, i, info: (0, c), column))
+                for _, column in flat
+            ]
+            + [pl.BlockSpec(memory_space=pl.ANY)] * len(after),
+            out_specs=[whole, whole],
+        ),
+        compiler_params=params(),
         cost_estimate=cost(2 * rows * tall * 768, 4 * rows * tall),
         name="grad_pieces",
-    )(info, n1, q0, q1, k0, x0, k1, x1, v0, y0, v1, y1)
+    )(info, n1, *[array for array, _ in flat], *after)
 
 
 class Stream:
-    def __init__(self, rounds, keep, send):
-        self.rounds = [None] + rounds
-        self.at = 0
-        self.keep = keep
-        self.sends = [send]
-        self.gots = None
-        self.done = False
-
-    def start(self):
-        bits = self.rounds[self.at]
-        if bits is None:
-            self.gots = [lax.ppermute(self.sends[0], "frame", flip(2, 1))]
-            return
-        count = lax.axis_size("seq")
-        self.gots = []
-        for m in range(1, 1 << len(bits)):
-            mask = 0
-            for i, bit in enumerate(bits):
-                mask |= ((m >> (len(bits) - 1 - i)) & 1) << bit
-            self.gots.append(lax.ppermute(self.sends[m - 1], "seq", flip(count, mask)))
-
-
-class Total:
-    def __init__(self, rounds, value):
-        self.rounds = rounds
-        self.at = 0
-        self.value = value
-        self.done = False
-
-    def start(self):
-        bits = self.rounds[self.at]
-        if bits is None:
-            self.gots = [lax.ppermute(self.value, "frame", flip(2, 1))]
-            return
-        count = lax.axis_size("seq")
-        self.gots = []
-        for m in range(1, 1 << len(bits)):
-            mask = 0
-            for i, bit in enumerate(bits):
-                mask |= ((m >> i) & 1) << bit
-            self.gots.append(lax.ppermute(self.value, "seq", flip(count, mask)))
-
-
-def fold(info, at, streams, after=()):
-    streams = [s for s in streams if not s.done]
-    ins, outs, plan = [], [], []
-    for s in streams:
-        last = s.at + 1 == len(s.rounds)
-        if isinstance(s, Total):
-            parts = [s.value] + s.gots
-            plan.append((len(parts), None, None))
-            outs.append(jax.ShapeDtypeStruct(s.value.shape, jnp.float32))
-        else:
-            parts = [s.keep] + s.gots
-            rows, wide = s.keep.shape
-            if last:
-                plan.append((len(parts), (), 1))
-                outs.append(jax.ShapeDtypeStruct((rows, wide), jnp.float32))
+    def __init__(self, rounds, keep, send, emit=None):
+        self.rounds, self.at, self.keep, self.emit = rounds, 0, keep, emit
+        self.gots = [(lax.ppermute(send, "frame", flip(2, 1)), 0)]
+
+    def bits(self):
+        return self.rounds[self.at] if self.at < len(self.rounds) else None
+
+
+class Total(Stream):
+    def __init__(self, rounds, value, emit):
+        super().__init__(rounds, value, value, emit)
+
+
+def split_low(value):
+    high = value.astype(jnp.bfloat16)
+    return high, (value - high.astype(jnp.float32)).astype(jnp.bfloat16)
+
+
+def fold(info, at, bundles, after=(), emit=None):
+    arrays, plan, outs = [], [], []
+
+    def source(array):
+        for i, known in enumerate(arrays):
+            if known is array:
+                return i
+        arrays.append(array)
+        return len(arrays) - 1
+
+    for streams, sending in bundles:
+        entry = []
+        bits = streams[0].bits() if sending else None
+        ways = 1 << len(bits) if bits else 1
+        offset = 0
+        for s in streams:
+            parts = [(source(array), start) for array, start in s.gots]
+            rows = s.keep.shape[0]
+            entry.append((s, source(s.keep), parts, rows, offset))
+            if isinstance(s, Total):
+                kept = jax.ShapeDtypeStruct((rows, PART), jnp.float32)
+                offset += 2 * rows
             else:
-                bits = s.rounds[s.at + 1]
-                ways = 1 << len(bits)
-                plan.append((len(parts), tuple(bits), ways))
-                outs += [jax.ShapeDtypeStruct((rows // ways, wide), jnp.bfloat16)] * ways
-        ins += parts
+                kept = jax.ShapeDtypeStruct((rows // ways, PART), jnp.bfloat16)
+                offset += rows // ways
+            if sending:
+                outs.append(kept)
+            elif s.emit:
+                outs += s.emit[0]
+            elif not emit:
+                outs.append(kept)
+        outs += [jax.ShapeDtypeStruct((offset, PART), jnp.bfloat16)] * (ways - 1)
+        plan.append((entry, bits, ways))
+    if emit:
+        outs += emit[0]
 
     def kernel(info_ref, *refs):
-        sources, targets = list(refs[: len(ins)]), list(refs[len(ins) + len(after) :])
+        sources, targets = refs[: len(arrays)], list(refs[len(arrays) + len(after) :])
         index = info_ref[at]
-        for count, bits, ways in plan:
-            parts = [sources.pop(0) for _ in range(count)]
-
-            def total(span):
-                value = parts[0][span].astype(jnp.float32)
-                for p in parts[1:]:
-                    value = value + p[span].astype(jnp.float32)
-                return value
-
-            if not bits:
-                targets.pop(0)[...] = total(...)
-                continue
+        ready = []
+        for entry, bits, ways in plan:
             mine = 0
-            for bit in bits:
+            for bit in bits or ():
                 mine = mine * 2 + ((index >> bit) & 1)
-            size = parts[0].shape[0] // ways
-            for m in range(ways):
-                start = pl.multiple_of((mine ^ m) * size, 16)
-                targets.pop(0)[...] = total((pl.ds(start, size), slice(None))).astype(jnp.bfloat16)
+            kept = []
+            for s, own, parts, rows, offset in entry:
+                size = rows // ways
+                if bits:
+                    kept.append(targets.pop(0))
+                elif s.emit or not emit:
+                    count = len(s.emit[0]) if s.emit else 1
+                    kept.append([targets.pop(0) for _ in range(count)])
+                else:
+                    kept.append(None)
+            sends = [targets.pop(0) for _ in range(ways - 1)]
+            for (s, own, parts, rows, offset), keep in zip(entry, kept):
+
+                def total(start, size):
+                    value = sources[own][pl.ds(start, size), :].astype(jnp.float32)
+                    for i, begin in parts:
+                        if isinstance(s, Total):
+                            if sources[i].dtype == jnp.float32:
+                                value = value + sources[i][...]
+                            else:
+                                value = value + sources[i][begin : begin + rows, :].astype(jnp.float32)
+                                value = value + sources[i][
+                                    begin + rows : begin + 2 * rows, :
+                                ].astype(jnp.float32)
+                        else:
+                            value = value + sources[i][pl.ds(begin + start, size), :].astype(jnp.float32)
+                    return value
+
+                if bits and isinstance(s, Total):
+                    value = total(0, rows)
+                    keep[...] = value
+                    high, low = split_low(value)
+                    for send in sends:
+                        send[offset : offset + rows, :] = high
+                        send[offset + rows : offset + 2 * rows, :] = low
+                elif bits:
+                    size = rows // ways
+                    for m in range(ways):
+                        start = pl.multiple_of((mine ^ m) * size, 16)
+                        value = total(start, size).astype(jnp.bfloat16)
+                        if m == 0:
+                            keep[...] = value
+                        else:
+                            sends[m - 1][offset : offset + size, :] = value
+                elif keep is None:
+                    ready.append(total(0, rows))
+                elif s.emit:
+                    s.emit[1](total(0, rows), *keep)
+                else:
+                    keep[0][...] = total(0, rows).astype(keep[0].dtype)
+        if emit:
+            emit[1](ready, *targets)
 
     vm = pl.BlockSpec(memory_space=pltpu.VMEM)
     sm = pl.BlockSpec(memory_space=pltpu.SMEM)
-    moved = sum(x.size * x.dtype.itemsize for x in ins) * 2
+    moved = sum(x.size * x.dtype.itemsize for x in arrays) * 2
     results = list(
         pl.pallas_call(
             kernel,
             out_shape=tuple(outs),
-            in_specs=[sm] + [vm] * len(ins) + [pl.BlockSpec(memory_space=pl.ANY)] * len(after),
+            in_specs=[sm] + [vm] * len(arrays) + [pl.BlockSpec(memory_space=pl.ANY)] * len(after),
             out_specs=(vm,) * len(outs),
             compiler_params=pltpu.CompilerParams(vmem_limit_bytes=VMEM_LIMIT),
             cost_estimate=cost(0, moved),
             name="fold",
-        )(info, *ins, *after)
+        )(info, *arrays, *after)
     )
     sent = []
-    for s, (_, bits, ways) in zip(streams, plan):
-        s.at += 1
-        s.done = s.at == len(s.rounds)
-        if isinstance(s, Total):
-            s.value = results.pop(0)
-            sent.append(s.value)
-        elif s.done:
-            s.keep = results.pop(0)
-            sent.append(s.keep)
-        else:
-            got = [results.pop(0) for _ in range(ways)]
-            s.keep, s.sends = got[0], got[1:]
-            sent.append(s.sends[0])
-        if not s.done:
-            s.start()
-    return sent[:1]
-
-
-def single(bits):
-    return [[b] for b in bits]
-
-
-def turned_orders(bits):
-    low = list(range(bits))
-    return [low[i:] + low[:i] for i in range(3)]
+    count = lax.axis_size("seq")
+    for entry, bits, ways in plan:
+        for s, *_ in entry:
+            if bits:
+                s.keep = results.pop(0)
+            elif s.emit:
+                s.result = [results.pop(0) for _ in s.emit[0]]
+            elif not emit:
+                s.keep = results.pop(0)
+            s.gots = []
+        for m in range(1, ways):
+            mask = 0
+            for i, bit in enumerate(bits):
+                mask |= ((m >> (len(bits) - 1 - i)) & 1) << bit
+            send = results.pop(0)
+            sent.append(send)
+            got = lax.ppermute(send, "seq", flip(count, mask))
+            for s, _, _, _, offset in entry:
+                s.gots.append((got, offset))
+        if bits:
+            for s, *_ in entry:
+                s.at += 1
+    return sent[:1], results
+
+
+def add_all(value, bits, after):
+    count = lax.axis_size("seq")
+    gots = []
+    for m in range(1, 1 << len(bits)):
+        mask = sum(((m >> i) & 1) << bit for i, bit in enumerate(bits))
+        gots.append(lax.ppermute(value, "seq", flip(count, mask)))
+
+    def kernel(*refs):
+        total = refs[0][...]
+        for ref in refs[1 : 1 + len(gots)]:
+            total = total + ref[...]
+        refs[-1][...] = total
+
+    vm = pl.BlockSpec(memory_space=pltpu.VMEM)
+    return pl.pallas_call(
+        kernel,
+        out_shape=jax.ShapeDtypeStruct(value.shape, jnp.float32),
+        in_specs=[vm] * (1 + len(gots)) + [pl.BlockSpec(memory_space=pl.ANY)] * len(after),
+        out_specs=vm,
+        name="add_all",
+    )(value, *gots, *after)
 
 
 def doubles(bits):
     low = list(range(bits))
     return [low[i : i + 2] for i in range(0, bits, 2)]
+
+
+def f32_shape(*shape):
+    return jax.ShapeDtypeStruct(shape, jnp.float32)
+
+
+def write_plain(value, ref):
+    ref[...] = value
+
+
+def write_wide(value, ref):
+    size = ref.shape[0]
+    for i in range(value.shape[0] // size):
+        ref[:, i * PART : i * PART + PART] = value[i * size : i * size + size, :]
+
+
+def write_first(value, ref):
+    for i in range(3):
+        ref[16 * i : 16 * i + 16, :] = value[:, 128 * i : 128 * i + ref.shape[1]]
+
+
+def write_vectors(value, *refs):
+    row = 0
+    for ref in refs:
+        for i in range(ref.shape[0] // (2 * PART)):
+            ref[2 * PART * i : 2 * PART * i + PART] = value[row, :]
+            ref[2 * PART * i + PART : 2 * PART * (i + 1)] = value[value.shape[0] // 2 + row, :]
+            row += 1
+
+
+def write_small(value, weights_ref, biases_ref, meet_ref):
+    for n in range(3):
+        weights_ref[n] = value[0:8, 128 * n : 128 * n + 9 * MAPS]
+    biases_ref[...] = value[8:12, 0:MAPS]
+    meet_ref[...] = value[8:9, 128:129]
+
+
+def write_groups(values, ref):
+    count = len(values)
+    for i in range(3):
+        for g, value in enumerate(values):
+            at = 128 * (i * count + g)
+            ref[:, at : at + 128] = value[:, 128 * i : 128 * i + 128]
 
 
 def quick_device(
@@ -1457,11 +1691,9 @@
     seqs = lax.axis_size("seq")
     rank = lax.axis_index("frame")
     bits = seqs.bit_length() - 1
-    orders = turned_orders(bits)
+    near = doubles(bits)
+    far = [[bit] for pair in near[1:] for bit in pair] + near[:1]
     rank_at, seq_at = 2 * frames + 1, 2 * frames + 2
-
-    def row(x):
-        return x.reshape(1, -1)
 
     def swap(x):
         return lax.ppermute(x, "frame", flip(2, 1))
@@ -1469,129 +1701,132 @@
     place = jnp.stack([rank, lax.axis_index("seq")]).astype(jnp.int32)
     info = jnp.concatenate([frame_mask[0], clip_lengths[0, 0:1], place])
     x = tokens[0]
-    count = Total(doubles(bits), jnp.sum(frame_mask).astype(jnp.float32) * jnp.ones((1, 128)))
-    count.start()
-    n1, k0, v0 = project(x, row(ln_gain_first), row(ln_bias_first), w_qkv, row(v_bias))
+    n1, k0, v0 = project(x, ln_gain_first, ln_bias_first, w_qkv, v_bias)
     far_k0, far_v0 = swap(k0), swap(v0)
-    fold(info, seq_at, [count], (n1,))
-    q, k1, v1 = project_more(n1, w_qkv, row(q_bias), row(v_bias))
+    q, k1, v1 = project_more(n1, w_qkv, q_bias, v_bias)
     far_k1, far_v1 = swap(k1), swap(v1)
-    attended, *kept0 = attn_fwd(info, q, k0, v0, far_k0, far_v0, None, 0, frames)
-    fold(info, seq_at, [count], (kept0[0],))
-    attended, *kept1 = attn_fwd(info, q, k1, v1, far_k1, far_v1, attended, 1, frames)
-    while not count.done:
-        fold(info, seq_at, [count], (attended,))
-    count = count.value[0, 0]
+    count = jnp.sum(frame_mask).astype(jnp.float32) * jnp.ones((1, 128))
+    count = add_all(count, near[0], (n1,))
+    half = attn_fwd(info, q, k0, v0, far_k0, far_v0, (), 0, frames)
+    for pair in near[1:]:
+        count = add_all(count, pair, (half[0],))
+    attended, lse, kc, vc = attn_fwd(info, q, k1, v1, far_k1, far_v1, tuple(half), 1, frames)
+    count = count[0, 0]
     weight = (penalty_scale / count).reshape(1)
     mid, n2, hidden, slope, out, n3 = mlp_fwd(
-        x, attended, w_out, row(out_bias), row(ln_gain_second), row(ln_bias_second), w_up,
-        row(up_bias), w_down, row(down_bias), row(ln_gain_third), row(ln_bias_third),
-    )
-    side, pooled, small, grad_first = learner(
-        info, weight, n3, out, pool_cot[0], w_first, conv_weights, conv_biases
+        x, attended, w_out, out_bias, ln_gain_second, ln_bias_second, w_up, up_bias, w_down,
+        down_bias, ln_gain_third, ln_bias_third,
+    )
+    side, pooled, small, first_keep, first_send = learner(
+        info, weight, n3, out, pool_cot[0], w_first, conv_weights, conv_biases, near, seqs
     )
     first_pad = jnp.concatenate(
         [w_first.T, jnp.zeros((128 - 9 * MAPS, width), jnp.bfloat16)], axis=0
     )
     d_down, d_up, d_branch, d_att, sums = mlp_bwd(
-        out_cot[0], out, side, pool_cot[0], first_pad, row(ln_gain_third), w_down, slope, w_up,
-        mid, row(ln_gain_second), w_out,
-    )
-
-    def both(x):
-        middle = x.shape[1] // 2
-        first, second = x[:, :middle], x[:, middle:]
-        return jnp.where(rank == 0, first, second), jnp.where(rank == 0, second, first)
-
-    plain = single(range(bits)[::-1])
+        out_cot[0], out, side, pool_cot[0], first_pad, ln_gain_third, w_down, slope, w_up, mid,
+        ln_gain_second, w_out,
+    )
+    first = Stream(
+        near, first_keep, first_send, ([f32_shape(width // seqs, 9 * MAPS // 2)], write_first)
+    )
+    meet = Total(
+        near,
+        small,
+        ([f32_shape(3, MAPS, 9 * MAPS), f32_shape(4, MAPS), f32_shape(1, 1)], write_small),
+    )
+    vectors = Total(
+        near, sums, ([f32_shape(width)] * 6 + [f32_shape(inner)], write_vectors)
+    )
+    down = Stream(
+        far,
+        *grad_by_rows(info, hidden, d_down, far, seqs, rank_at),
+        ([f32_shape(inner // seqs, PART)], write_plain),
+    )
     up = Stream(
-        single(orders[0]), *grad_by_columns(info, n2, d_up, single(orders[0]), seqs, rank_at)
-    )
-    up.start()
-    down = Stream(
-        single(orders[1]), *grad_by_rows(info, hidden, d_down, single(orders[1]), seqs, rank_at)
-    )
-    down.start()
+        near,
+        *grad_by_columns(info, n2, d_up, near, seqs, rank_at),
+        ([f32_shape(width // seqs, inner // 2)], write_wide),
+    )
     branch = Stream(
-        single(orders[2]), *grad_by_rows(info, attended, d_branch, single(orders[2]), seqs, rank_at)
-    )
-    branch.start()
-    first = Stream(plain, *both(grad_first.astype(jnp.bfloat16).T))
-    first.start()
-    early = Total(
-        [None] + single(range(bits)), jnp.concatenate([sums.reshape(-1, 128), small.reshape(-1, 128)])
-    )
-    early.start()
-    streams = [up, down, branch, first, early]
-    after = fold(info, seq_at, streams)
-
+        near,
+        *grad_by_rows(info, attended, d_branch, near, seqs, rank_at),
+        ([f32_shape(width // seqs, PART)], write_plain),
+    )
+    early = [up, branch, first, vectors, meet]
     pairs = width // 128
     groups = pairs // 2
     pieces = {}
-    group_streams = []
-
-    def group_stream(g):
-        stream = Stream(
-            doubles(bits),
-            *grad_pieces(
-                info, n1, (pieces[g], pieces[g + groups]), doubles(bits), seqs, rank_at
-            ),
+
+    def attend_back(which, after):
+        dq, own_k, own_v, away = attn_bwd(
+            info, q, kc, vc, attended, d_att, lse, which, frames, after
         )
-        stream.start()
-        group_streams.append(stream)
-        return stream
-
-    for turn, pair in enumerate(p for g in range(groups) for p in (g, g + groups)):
-        lse, kc, vc, valid = (kept0, kept1)[pair // groups]
-        dq, own_k, own_v, far_k, far_v = attn_bwd(
-            info, q, kc, vc, valid, attended, d_att, lse, pair, frames, after
-        )
-        pieces[pair] = (dq, own_k, swap(far_k), own_v, swap(far_v))
-        after = fold(info, seq_at, streams, (dq,))
-        if turn % 2 == 0 and turn > 0:
-            stream = group_stream(turn // 2 - 1)
-            streams.append(stream)
-            after = after + [stream.sends[0]]
-    streams.append(group_stream(groups - 1))
+        away = swap(away)
+        for i, pair in enumerate(which):
+            pieces[pair] = [(dq, i), (own_k, i), (away, 2 * i), (own_v, i), (away, 2 * i + 1)]
+        return dq
+
+    def group_stream(g, after):
+        both = (pieces[g], pieces[g + groups])
+        grads = grad_pieces(info, n1, both, near, seqs, rank_at, after)
+        return Stream(near, *grads), list(grads[1:])
+
+    streams = []
+    after, _ = fold(info, seq_at, [(early, True), ([down], True)])
+    last = attend_back((0, groups), after)
+    after, _ = fold(info, seq_at, [(early, True), ([down], True)], (last,))
+    last = attend_back((1, 1 + groups), after)
+    after, _ = fold(info, seq_at, [(early, False), ([down], True)], (last,))
+    stream, sent = group_stream(0, after)
+    streams.append(stream)
+    last = attend_back((2,), after + sent)
+    stream, after = group_stream(1, (last,))
+    streams.append(stream)
+    last = attend_back((2 + groups,), after)
+    after, _ = fold(info, seq_at, [(streams[:2], True), ([down], False)], (last,))
+    stream, _ = group_stream(2, after)
+    streams.append(stream)
     tokens_grad, late = final_bwd(
-        [pieces[p][i] for i in range(5) for p in range(pairs)],
-        x, d_branch, row(ln_gain_first), w_qkv,
-    )
-    late = Total([None] + doubles(bits), late)
-    late.start()
-    streams.append(late)
-    while not all(s.done for s in streams):
-        fold(info, seq_at, streams)
-    grad_qkv = jnp.concatenate(
-        [s.keep[:, 128 * i : 128 * i + 128] for i in range(3) for s in group_streams], axis=1
-    )
-    late = late.value
-    sums = early.value[: 16 * width // 128].reshape(16, width)
-    small = early.value[16 * width // 128 :].reshape(8, 8, 128)
-    penalty = small[3, 0, 0] / count
+        [pieces[p][i] for i in range(5) for p in range(pairs)], x, d_branch, ln_gain_first, w_qkv
+    )
+    late = Total(near, late, ([f32_shape(width)] * 4, write_vectors))
+    while streams[2].at < streams[0].at:
+        bundles = [([streams[2], late], True)]
+        if streams[0].gots:
+            bundles.append((streams[:2], False))
+        fold(info, seq_at, bundles)
+    while late.bits():
+        fold(info, seq_at, [(streams + [late], True)])
+    results = fold(
+        info, seq_at, [(streams, False), ([late], False)],
+        emit=([f32_shape(width // seqs, 3 * width // 2)], write_groups),
+    )[1]
+    vectors, late = vectors.result, late.result
+    conv_w, conv_b, total = meet.result
     return (
         out[None],
         pooled[None],
-        penalty,
+        total[0, 0] / count,
         tokens_grad[None],
         late[0],
         late[1],
-        grad_qkv,
+        results[0],
         late[2],
         late[3],
-        branch.keep,
-        sums[5],
-        sums[0],
-        sums[1],
-        up.keep,
-        sums[6 : 6 + inner // width].reshape(-1),
-        down.keep,
-        sums[4],
-        sums[2],
-        sums[3],
-        first.keep,
-        small[:3, :, : 9 * MAPS],
-        small[4:8, :, 0],
+        branch.result[0],
+        vectors[5],
+        vectors[0],
+        vectors[1],
+        up.result[0],
+        vectors[6],
+        down.result[0],
+        vectors[4],
+        vectors[2],
+        vectors[3],
+        first.result[0],
+        conv_w,
+        conv_b,
     )
 
 
@@ -1605,7 +1840,7 @@
         and frames % 4 == 0
         and tokens.shape[1] % TILE == 0
         and tokens.shape[2] == HEADS * HEAD_DIM
-        and seqs & (seqs - 1) == 0
+        and seqs == 16
     )
     return (quick_device if fits else plain_device)(*arrays)
 

time: 676 us -> 572 us (0.85); the launches traced: 666 us -> 574 us
  starting transfers between devices: 313 us -> 203 us
  waiting for transfers between devices: 21.6 us -> 64.4 us
  local copies, waits for them, and re-layouts: 33.6 us -> 15.3 us
    ppermute x59 -> x36, starting transfers between devices: 295 us -> 201 us  [the longest x20 190 us: fold(): got = lax.ppermute(send, 'seq', flip(count, mask))]
    ppermute x59 -> x36, waiting for transfers between devices: 21.5 us -> 64.4 us  [the longest x20 60.6 us: fold(): got = lax.ppermute(send, 'seq', flip(count, mask))]
    ppermute x16 -> x8, starting transfers between devices: 17.9 us -> 1.51 us  [swap(): return lax.ppermute(x, 'frame', flip(2, 1))]
    pallas_call x2, Pallas kernels: 28.7 us -> 37.5 us  [attn_fwd(): pl.pallas_call(kernel, out_shape=(jax.ShapeDtypeStruct((rows, width), jnp...]
    reshape x13 -> x0, local copies, waits for them, and re-layouts: 8.47 us -> none  [the longest x10 7.87 us: row(): return x.reshape(1, -1)]
    pallas_call x12 -> x7, Pallas kernels: 32.4 us -> 24.3 us  [fold(): pl.pallas_call(kernel, out_shape=tuple(outs), in_specs=[sm] + [vm] * len(...]
    unnamed x217 -> x113, local copies, waits for them, and re-layouts: 19.6 us -> 14.6 us
  transfers between devices with their start and end apart: 75 -> 44, of which waited for: 10 -> 16; matrix products, arithmetic and copies ran while one was open for 2% -> 1% of each run, Pallas kernels for 22% -> 24%
where the time goes in v3:
time: 572 us; the launch traced here: 574 us
  Pallas kernels  285 us (50%)
  starting transfers between devices  203 us (35%)
  waiting for transfers between devices  64.4 us (11%)
  local copies, waits for them, and re-layouts  15.3 us (3%)
    ppermute x20, starting transfers between devices, fold(): got = lax.ppermute(send, 'seq', flip(count, mask))  190 us
    ppermute x20, waiting for transfers between devices, fold(): got = lax.ppermute(send, 'seq', flip(count, mask))  60.6 us
    pallas_call x4, Pallas kernels, attn_bwd(): pl.pallas_call(kernel, out_shape=(jax.ShapeDtypeStruct((rows, 128 * len(p...  51.2 us
    pallas_call x2, Pallas kernels, attn_fwd(): pl.pallas_call(kernel, out_shape=(jax.ShapeDtypeStruct((rows, width), jnp...  37.5 us
    pallas_call x1, Pallas kernels, mlp_bwd(): pl.pallas_call(mlp_bwd_kernel, out_shape=(low_shape(rows, width), low_sha...  36.8 us
    pallas_call x1, Pallas kernels, mlp_fwd(): pl.pallas_call(mlp_fwd_kernel, out_shape=(low_shape(rows, width), low_sha...  31.9 us
    pallas_call x7, Pallas kernels, fold(): pl.pallas_call(kernel, out_shape=tuple(outs), in_specs=[sm] + [vm] * len(...  24.3 us
    pallas_call x2, Pallas kernels, grad_by_rows(): pl.pallas_call(functools.partial(grad_by_rows_kernel, rounds, seqs, at),...  21.5 us
  transfers between devices with their start and end apart: 44, of which 16 were waited for; matrix products, arithmetic and copies ran while one was open for 1% of the time, Pallas kernels for 24%

profile of v3, /device:TPU:0, one launch (start us, length us, event | category | flops | bytes accessed | tf_op | source)
XLA Modules:
  0.0 574.3 jit_solution(4878426269704090190)
XLA Ops:
  0.7 8.3 %project.1 = (bf16[1568,768]{1,0:T(8,128)(2,1)}, bf16[1568,384]{1,0:T(8,128)(2,1)}, bf16[1568,384]{1,0:T(8,128)(2,1)}) custom-call(bf16[1568,768]{1,0:T(8,128)(2,1)} %bitcast.18, f32[768]{0:T(1024)} %refs_32_.1, f32[768]{0:T(1024)} %shift_ref.1, bf16[768,2304]{1,0:T(8,128)(2,1)} %refs_33_.1, bf16[768,2304]{1,0:T(8,128)(2,1)} %refs_33_.1, f32[768]{0:T(1024)} %v_bias.1), custom_call_target="tpu_custom_call" | custom-call | flops 1849688064 | bytes 12042240 | tf_op jit(solution)/shard_map/project/pallas_call | solution.py:893
  16.0 9.1 %project_more.1 = (bf16[1568,768]{1,0:T(8,128)(2,1)}, bf16[1568,384]{1,0:T(8,128)(2,1)}, bf16[1568,384]{1,0:T(8,128)(2,1)}) custom-call(bf16[1568,768]{1,0:T(8,128)(2,1)} %get-tuple-element.144.n_ref.refs_4_, bf16[768,2304]{1,0:T(8,128)(2,1)} %refs_33_.1, bf16[768,2304]{1,0:T(8,128)(2,1)} %refs_33_.1, bf16[768,2304]{1,0:T(8,128)(2,1)} %refs_33_.1, ...), custom_call_target="tpu_custom_call" | custom-call | flops 3699376128 | bytes 12042240 | tf_op jit(solution)/shard_map/project_more/pallas_call | solution.py:923
  35.9 12.7 %attn_fwd.2 = (bf16[1568,768]{1,0:T(8,128)(2,1)}, f32[6,8,1568]{2,1,0:T(8,128)}, bf16[4096,768]{1,0:T(8,128)(2,1)}, bf16[4096,768]{1,0:T(8,128)(2,1)}) custom-call(s32[19]{0:T(128)} %pad_add_fusion.refs_0_.info_ref, bf16[1568,768]{1,0:T(8,128)(2,1)} %get-tuple-element.145.refs_1_, bf16[1568,384]{1,0:T(8,128)(2,1)} %get-tuple-element.148.refs_2_, ...), custom_call_target="tpu_custom_call" | custom-call | flops 40000000000 | bytes 10000000 | tf_op jit(solution)/shard_map/attn_fwd/pallas_call | solution.py:609
  51.1 24.8 %attn_fwd.3 = (bf16[1568,768]{1,0:T(8,128)(2,1)}, f32[6,8,1568]{2,1,0:T(8,128)}, bf16[4096,768]{1,0:T(8,128)(2,1)}, bf16[4096,768]{1,0:T(8,128)(2,1)}) custom-call(s32[19]{0:T(128)} %pad_add_fusion.refs_0_.info_ref, bf16[1568,768]{1,0:T(8,128)(2,1)} %get-tuple-element.145.refs_1_, ...), custom_call_target="tpu_custom_call", output_to_operand_aliasing={{0}: (6, {}), {1}: (7, {}), {2}: (8, {}), {3}: (9, {})} | custom-call | flops 40000000000 | bytes 10000000 | tf_op jit(solution)/shard_map/attn_fwd/pallas_call | solution.py:609
  75.9 31.9 %mlp_fwd.1 = (bf16[1568,768]{1,0:T(8,128)(2,1)}, bf16[1568,768]{1,0:T(8,128)(2,1)}, bf16[1568,3072]{1,0:T(8,128)(2,1)}, bf16[1568,3072]{1,0:T(8,128)(2,1)}, bf16...) custom-call(bf16[1568,768]{1,0:T(8,128)(2,1)} %bitcast.19, bf16[1568,768]{1,0:T(8,128)(2,1)} %get-tuple-element.154.a_ref.refs_4_, ...), custom_call_target="tpu_custom_call" | custom-call | flops 16647192576 | bytes 33718272 | tf_op jit(solution)/shard_map/mlp_fwd/pallas_call | solution.py:982
  107.8 10.5 %learner.1 = (bf16[1568,256]{1,0:T(8,128)(2,1)}, bf16[64,768]{1,0:T(8,128)(2,1)}, f32[16,384]{1,0:T(8,128)}, bf16[256,384]{1,0:T(8,128)(2,1)}, bf16[256,384]{1,0:T(8,128)(2,1)}) custom-call(s32[19]{0:T(128)} %pad_add_fusion.refs_0_.info_ref, f32[1]{0:T(128)} %bitcast.7.weight_ref, bf16[1568,768]{1,0:T(8,128)(2,1)} %get-tuple-element.156.n3_ref, ...), custom_call_target="tpu_custom_call" | custom-call | flops 20000000000 | bytes 4816896 | tf_op jit(solution)/shard_map/learner/pallas_call | solution.py:1274
  118.3 36.8 %mlp_bwd.1 = (bf16[1568,768]{1,0:T(8,128)(2,1)}, bf16[1568,3072]{1,0:T(8,128)(2,1)}, bf16[1568,768]{1,0:T(8,128)(2,1)}, bf16[1568,768]{1,0:T(8,128)(2,1)}, f32[32,384]{1,0:T(8,128)}) custom-call(bf16[1568,768]{1,0:T(8,128)(2,1)} %bitcast.29, bf16[1568,768]{1,0:T(8,128)(2,1)} %get-tuple-element.155.out_ref, bf16[1568,256]{1,0:T(8,128)(2,1)} %get-tuple-element.159.side_ref, ...), custom_call_target="tpu_custom_call" | custom-call | flops 16647192576 | bytes 33718272 | tf_op jit(solution)/shard_map/mlp_bwd/pallas_call | solution.py:1064
  155.1 14.9 %grad_rows.3 = (bf16[3072,384]{1,0:T(8,128)(2,1)}, bf16[3072,384]{1,0:T(8,128)(2,1)}) custom-call(s32[19]{0:T(128)} %pad_add_fusion.refs_0_.info_ref, bf16[1568,3072]{1,0:T(8,128)(2,1)} %get-tuple-element.172.a_ref, bf16[1568,768]{1,0:T(8,128)(2,1)} %get-tuple-element.173.b_ref), custom_call_target="tpu_custom_call" | custom-call | flops 7398752256 | bytes 12042240 | tf_op jit(solution)/shard_map/grad_rows/pallas_call | solution.py:1399
  170.0 15.8 %grad_columns.1 = (bf16[3072,384]{1,0:T(8,128)(2,1)}, bf16[3072,384]{1,0:T(8,128)(2,1)}) custom-call(s32[19]{0:T(128)} %pad_add_fusion.refs_0_.info_ref, bf16[1568,768]{1,0:T(8,128)(2,1)} %get-tuple-element.158.a_ref, bf16[1568,3072]{1,0:T(8,128)(2,1)} %get-tuple-element.162.b_ref), custom_call_target="tpu_custom_call" | custom-call | flops 7398752256 | bytes 12042240 | tf_op jit(solution)/shard_map/grad_columns/pallas_call | solution.py:1358
  186.3 6.6 %grad_rows.2 = (bf16[768,384]{1,0:T(8,128)(2,1)}, bf16[768,384]{1,0:T(8,128)(2,1)}) custom-call(s32[19]{0:T(128)} %pad_add_fusion.refs_0_.info_ref, bf16[1568,768]{1,0:T(8,128)(2,1)} %get-tuple-element.154.a_ref.refs_4_, bf16[1568,768]{1,0:T(8,128)(2,1)} %get-tuple-element.165.b_ref.refs_31_), custom_call_target="tpu_custom_call" | custom-call | flops 1849688064 | bytes 4816896 | tf_op jit(solution)/shard_map/grad_rows/pallas_call | solution.py:1399
  197.9 7.5 %fold.7 = (bf16[768,384]{1,0:T(8,128)(2,1)}, bf16[192,384]{1,0:T(8,128)(2,1)}, bf16[64,384]{1,0:T(8,128)(2,1)}, f32[32,384]{1,0:T(8,128)}, f32[16,384]{1,0:T(8,1...) custom-call(s32[19]{0:T(128)} %pad_add_fusion.refs_0_.info_ref, ...), custom_call_target="tpu_custom_call" | custom-call | bytes 22315008 | tf_op jit(solution)/shard_map/fold/pallas_call | solution.py:1576
  205.4 9.5 %collective-permute-start.19 = (bf16[1536,384]{1,0:T(8,128)(2,1)}, bf16[1536,384]{1,0:T(8,128)(2,1)S(1)}, u32[]{:S(2)}, u32[]{:S(2)}) collective-permute-start(bf16[1536,384]{1,0:T(8,128)(2,1)} %get-tuple-element.184), channel_id=1, source_target_pairs={{0,8},{2,10},{4,12},{6,14},{8,0},{10,2},{12,4},{14,6},{16,24},{18,... | collective-permute-start | bytes 3538952 | tf_op jit(solution)/shard_map/ppermute | solution.py:1603
  214.9 21.7 %collective-permute-start.16 = (bf16[1120,384]{1,0:T(8,128)(2,1)}, bf16[1120,384]{1,0:T(8,128)(2,1)S(1)}, u32[]{:S(2)}, u32[]{:S(2)}) collective-permute-start(bf16[1120,384]{1,0:T(8,128)(2,1)} %get-tuple-element.176.refs_7_), channel_id=1, source_target_pairs={{0,4},{2,6},{4,0},{6,2},{8,12},{10,14},{12,8},{14,10},{16,20},{18,... | collective-permute-start | bytes 2580488 | tf_op jit(solution)/shard_map/ppermute | solution.py:1603
  238.1 15.7 %attn_bwd.4 = (bf16[1568,256]{1,0:T(8,128)(2,1)}, bf16[1568,256]{1,0:T(8,128)(2,1)}, bf16[1568,256]{1,0:T(8,128)(2,1)}, bf16[1568,512]{1,0:T(8,128)(2,1)}) custom-call(s32[19]{0:T(128)} %pad_add_fusion.refs_0_.info_ref, bf16[1568,768]{1,0:T(8,128)(2,1)} %get-tuple-element.145.refs_1_, bf16[4096,768]{1,0:T(8,128)(2,1)} %get-tuple-element.186.refs_2_, ...), custom_call_target="tpu_custom_call" | custom-call | flops 60000002048 | bytes 10000000 | tf_op jit(solution)/shard_map/attn_bwd/pallas_call | solution.py:788
  259.0 16.8 %collective-permute-done.18.refs_2_ = bf16[1120,384]{1,0:T(8,128)(2,1)} collective-permute-done((bf16[1120,384]{1,0:T(8,128)(2,1)}, bf16[1120,384]{1,0:T(8,128)(2,1)}, u32[]{:S(2)}, u32[]{:S(2)}) %collective-permute-start.18) | collective-permute-done | bytes 860192 | tf_op jit(solution)/shard_map/ppermute | solution.py:1603
  276.8 4.5 fold.8
  281.4 30.2 %collective-permute-start.23 = (bf16[768,384]{1,0:T(8,128)(2,1)}, bf16[768,384]{1,0:T(8,128)(2,1)S(1)}, u32[]{:S(2)}, u32[]{:S(2)}) collective-permute-start(bf16[768,384]{1,0:T(8,128)(2,1)} %get-tuple-element.199), channel_id=1, source_target_pairs={{0,16},{2,18},{4,20},{6,22},{8,24},{10,26},{12,28},{14,30},{16,0},... | collective-permute-start | bytes 1769480 | tf_op jit(solution)/shard_map/ppermute | solution.py:1603
  311.6 14.2 %collective-permute-start.21 = (bf16[352,384]{1,0:T(8,128)(2,1)}, bf16[352,384]{1,0:T(8,128)(2,1)}, u32[]{:S(2)}, u32[]{:S(2)}) collective-permute-start(bf16[352,384]{1,0:T(8,128)(2,1)} %get-tuple-element.192), channel_id=1, source_target_pairs={{0,8},{2,10},{4,12},{6,14},{8,0},{10,2},{12,4},{14,6},{16,24},{18,... | collective-permute-start | bytes 811016 | tf_op jit(solution)/shard_map/ppermute | solution.py:1603
  328.1 15.9 %attn_bwd.5 = (bf16[1568,256]{1,0:T(8,128)(2,1)}, bf16[1568,256]{1,0:T(8,128)(2,1)}, bf16[1568,256]{1,0:T(8,128)(2,1)}, bf16[1568,512]{1,0:T(8,128)(2,1)}) custom-call(s32[19]{0:T(128)} %pad_add_fusion.refs_0_.info_ref, bf16[1568,768]{1,0:T(8,128)(2,1)} %get-tuple-element.145.refs_1_, bf16[4096,768]{1,0:T(8,128)(2,1)} %get-tuple-element.186.refs_2_, ...), custom_call_target="tpu_custom_call" | custom-call | flops 60000002048 | bytes 10000000 | tf_op jit(solution)/shard_map/attn_bwd/pallas_call | solution.py:788
  344.0 6.4 %collective-permute-done.20.refs_0_ = bf16[352,384]{1,0:T(8,128)(2,1)S(1)} collective-permute-done((bf16[352,384]{1,0:T(8,128)(2,1)}, bf16[352,384]{1,0:T(8,128)(2,1)S(1)}, u32[]{:S(2)}, u32[]{:S(2)}) %collective-permute-start.20) | collective-permute-done | bytes 270368 | tf_op jit(solution)/shard_map/ppermute | solution.py:1603
  350.4 6.1 %collective-permute-done.22.refs_2_ = bf16[352,384]{1,0:T(8,128)(2,1)} collective-permute-done((bf16[352,384]{1,0:T(8,128)(2,1)}, bf16[352,384]{1,0:T(8,128)(2,1)}, u32[]{:S(2)}, u32[]{:S(2)}) %collective-permute-start.22) | collective-permute-done | bytes 270368 | tf_op jit(solution)/shard_map/ppermute | solution.py:1603
  361.2 6.9 %grad_pieces.3 = (bf16[768,384]{1,0:T(8,128)(2,1)}, bf16[768,384]{1,0:T(8,128)(2,1)}) custom-call(s32[19]{0:T(128)} %pad_add_fusion.refs_0_.info_ref, bf16[1568,768]{1,0:T(8,128)(2,1)} %get-tuple-element.144.n_ref.refs_4_, bf16[1568,256]{1,0:T(8,128)(2,1)} %get-tuple-element.190.refs_10_.refs_0_.refs_5_.refs_3_, ...), custom_call_target="tpu_custom_call" | custom-call | flops 1849688064 | bytes 4816896 | tf_op jit(solution)/shard_map/grad_pieces/pallas_call | solution.py:1436
  368.2 9.7 %attn_bwd.6 = (bf16[1568,128]{1,0:T(8,128)(2,1)}, bf16[1568,128]{1,0:T(8,128)(2,1)}, bf16[1568,128]{1,0:T(8,128)(2,1)}, bf16[1568,256]{1,0:T(8,128)(2,1)}) custom-call(s32[19]{0:T(128)} %pad_add_fusion.refs_0_.info_ref, bf16[1568,768]{1,0:T(8,128)(2,1)} %get-tuple-element.145.refs_1_, bf16[4096,768]{1,0:T(8,128)(2,1)} %get-tuple-element.186.refs_2_, ...), custom_call_target="tpu_custom_call" | custom-call | flops 30000001024 | bytes 10000000 | tf_op jit(solution)/shard_map/attn_bwd/pallas_call | solution.py:788
  379.1 6.9 %grad_pieces.4 = (bf16[768,384]{1,0:T(8,128)(2,1)}, bf16[768,384]{1,0:T(8,128)(2,1)}) custom-call(s32[19]{0:T(128)} %pad_add_fusion.refs_0_.info_ref, bf16[1568,768]{1,0:T(8,128)(2,1)} %get-tuple-element.144.n_ref.refs_4_, bf16[1568,256]{1,0:T(8,128)(2,1)} %get-tuple-element.201.refs_10_.refs_0_.refs_5_.refs_1_.refs_4_, ...), custom_call_target="tpu_custom_call" | custom-call | flops 1849688064 | bytes 4816896 | tf_op jit(solution)/shard_map/grad_pieces/pallas_call | solution.py:1436
  386.0 9.9 %attn_bwd.7 = (bf16[1568,128]{1,0:T(8,128)(2,1)}, bf16[1568,128]{1,0:T(8,128)(2,1)}, bf16[1568,128]{1,0:T(8,128)(2,1)}, bf16[1568,256]{1,0:T(8,128)(2,1)}) custom-call(s32[19]{0:T(128)} %pad_add_fusion.refs_0_.info_ref, bf16[1568,768]{1,0:T(8,128)(2,1)} %get-tuple-element.145.refs_1_, bf16[4096,768]{1,0:T(8,128)(2,1)} %get-tuple-element.186.refs_2_, ...), custom_call_target="tpu_custom_call" | custom-call | flops 30000001024 | bytes 10000000 | tf_op jit(solution)/shard_map/attn_bwd/pallas_call | solution.py:788
  396.9 15.8 %collective-permute-start.30 = (bf16[192,384]{1,0:T(8,128)(2,1)S(1)}, bf16[192,384]{1,0:T(8,128)(2,1)S(1)}, u32[]{:S(2)}, u32[]{:S(2)}) collective-permute-start(bf16[192,384]{1,0:T(8,128)(2,1)S(1)} %copy-done.24), channel_id=1, source_target_pairs={{0,4},{2,6},{4,0},{6,2},{8,12},{10,14},{12,8},{14,10},{16,20},{18,... | collective-permute-start | bytes 442376 | tf_op jit(solution)/shard_map/ppermute | solution.py:1603
  417.1 5.9 %collective-permute-start.31 = (bf16[192,384]{1,0:T(8,128)(2,1)S(1)}, bf16[192,384]{1,0:T(8,128)(2,1)S(1)}, u32[]{:S(2)}, u32[]{:S(2)}) collective-permute-start(bf16[192,384]{1,0:T(8,128)(2,1)S(1)} %copy-done.54), channel_id=1, source_target_pairs={{0,2},{2,0},{4,6},{6,4},{8,10},{10,8},{12,14},{14,12},{16,18},{18,... | collective-permute-start | bytes 442376 | tf_op jit(solution)/shard_map/ppermute | solution.py:1603
  437.8 7.0 %grad_pieces.5 = (bf16[768,384]{1,0:T(8,128)(2,1)}, bf16[768,384]{1,0:T(8,128)(2,1)}) custom-call(s32[19]{0:T(128)} %pad_add_fusion.refs_0_.info_ref, bf16[1568,768]{1,0:T(8,128)(2,1)} %get-tuple-element.144.n_ref.refs_4_, bf16[1568,128]{1,0:T(8,128)(2,1)} %get-tuple-element.208.refs_10_.refs_2_.refs_0_, ...), custom_call_target="tpu_custom_call" | custom-call | flops 1849688064 | bytes 4816896 | tf_op jit(solution)/shard_map/grad_pieces/pallas_call | solution.py:1436
  448.4 15.2 %final_bwd.1 = (bf16[1568,768]{1,0:T(8,128)(2,1)}, f32[16,384]{1,0:T(8,128)}) custom-call(bf16[1568,256]{1,0:T(8,128)(2,1)} %get-tuple-element.190.refs_10_.refs_0_.refs_5_.refs_3_, bf16[1568,256]{1,0:T(8,128)(2,1)} %get-tuple-element.201.refs_10_.refs_0_.refs_5_.refs_1_.refs_4_, bf16[1568,128]{1,0:T(8,128)(2,1)} %get-tuple-element.208.refs_10_.refs_2_.refs_0_, ...), custom_call_target="tpu_custom_call" | custom-call | flops 5549064192 | bytes 19267584 | tf_op jit(solution)/shard_map/final_bwd/pallas_call | solution.py:1132
  483.1 37.2 %collective-permute-start.41 = (bf16[176,384]{1,0:T(8,128)(2,1)}, bf16[176,384]{1,0:T(8,128)(2,1)S(1)}, u32[]{:S(2)}, u32[]{:S(2)}) collective-permute-start(bf16[176,384]{1,0:T(8,128)(2,1)} %get-tuple-element.241), channel_id=1, source_target_pairs={{0,16},{2,18},{4,20},{6,22},{8,24},{10,26},{12,28},{14,30},{16,0},... | collective-permute-start | bytes 405512 | tf_op jit(solution)/shard_map/ppermute | solution.py:1603
  520.3 42.0 %collective-permute-start.42 = (bf16[176,384]{1,0:T(8,128)(2,1)}, bf16[176,384]{1,0:T(8,128)(2,1)S(1)}, u32[]{:S(2)}, u32[]{:S(2)}) collective-permute-start(bf16[176,384]{1,0:T(8,128)(2,1)} %get-tuple-element.242), channel_id=1, source_target_pairs={{0,8},{2,10},{4,12},{6,14},{8,0},{10,2},{12,4},{14,6},{16,24},{18,... | collective-permute-start | bytes 405512 | tf_op jit(solution)/shard_map/ppermute | solution.py:1603
  565.7 4.7 collective-permute-done.43.refs_2_
  (200 shorter events, 88.0 us)
Async XLA Ops:
  9.0 23.3 %collective-permute-start.2 = (bf16[1568,384]{1,0:T(8,128)(2,1)}, bf16[1568,384]{1,0:T(8,128)(2,1)S(1)}, u32[]{:S(2)}, u32[]{:S(2)}) collective-permute-start(bf16[1568,384]{1,0:T(8,128)(2,1)} %get-tuple-element.148.refs_2_), channel_id=1, source_target_pairs={{0,1},{1,0},{2,3},{3,2},{4,5},{5,4},{6,7},{7,6},{8,9},{9,8},{10,11... | collective-permute-start | bytes 3612680 | tf_op jit(solution)/shard_map/ppermute | solution.py:1699
  9.4 25.4 %collective-permute-start.3 = (bf16[1568,384]{1,0:T(8,128)(2,1)}, bf16[1568,384]{1,0:T(8,128)(2,1)S(1)}, u32[]{:S(2)}, u32[]{:S(2)}) collective-permute-start(bf16[1568,384]{1,0:T(8,128)(2,1)} %get-tuple-element.149.refs_3_), channel_id=1, source_target_pairs={{0,1},{1,0},{2,3},{3,2},{4,5},{5,4},{6,7},{7,6},{8,9},{9,8},{10,11... | collective-permute-start | bytes 3612680 | tf_op jit(solution)/shard_map/ppermute | solution.py:1699
  10.8 17.2 %collective-permute-start.4 = (f32[1,128]{1,0:T(1,128)S(1)}, f32[1,128]{1,0:T(1,128)S(1)}, u32[]{:S(2)}, u32[]{:S(2)}) collective-permute-start(f32[1,128]{1,0:T(1,128)S(1)} %mul.3.refs_0_), channel_id=1, source_target_pairs={{0,2},{2,0},{4,6},{6,4},{8,10},{10,8},{12,14},{14,12},{16,18},{18,... | collective-permute-start | bytes 1544 | tf_op jit(solution)/shard_map/ppermute | solution.py:1617
  13.8 14.2 %collective-permute-start.5 = (f32[1,128]{1,0:T(1,128)S(1)}, f32[1,128]{1,0:T(1,128)S(1)}, u32[]{:S(2)}, u32[]{:S(2)}) collective-permute-start(f32[1,128]{1,0:T(1,128)S(1)} %mul.3.refs_0_), channel_id=1, source_target_pairs={{0,4},{2,6},{4,0},{6,2},{8,12},{10,14},{12,8},{14,10},{16,20},{18,... | collective-permute-start | bytes 1544 | tf_op jit(solution)/shard_map/ppermute | solution.py:1617
  15.3 13.2 %collective-permute-start.6 = (f32[1,128]{1,0:T(1,128)S(1)}, f32[1,128]{1,0:T(1,128)S(1)}, u32[]{:S(2)}, u32[]{:S(2)}) collective-permute-start(f32[1,128]{1,0:T(1,128)S(1)} %mul.3.refs_0_), channel_id=1, source_target_pairs={{0,6},{2,4},{4,2},{6,0},{8,14},{10,12},{12,10},{14,8},{16,22},{18,... | collective-permute-start | bytes 1544 | tf_op jit(solution)/shard_map/ppermute | solution.py:1617
  27.9 23.1 %collective-permute-start = (bf16[1568,384]{1,0:T(8,128)(2,1)}, bf16[1568,384]{1,0:T(8,128)(2,1)}, u32[]{:S(2)}, u32[]{:S(2)}) collective-permute-start(bf16[1568,384]{1,0:T(8,128)(2,1)} %get-tuple-element.146.refs_2_), channel_id=1, source_target_pairs={{0,1},{1,0},{2,3},{3,2},{4,5},{5,4},{6,7},{7,6},{8,9},{9,8},{10,11... | collective-permute-start | bytes 3612680 | tf_op jit(solution)/shard_map/ppermute | solution.py:1699
  28.0 23.1 %collective-permute-start.1 = (bf16[1568,384]{1,0:T(8,128)(2,1)}, bf16[1568,384]{1,0:T(8,128)(2,1)}, u32[]{:S(2)}, u32[]{:S(2)}) collective-permute-start(bf16[1568,384]{1,0:T(8,128)(2,1)} %get-tuple-element.147.refs_3_), channel_id=1, source_target_pairs={{0,1},{1,0},{2,3},{3,2},{4,5},{5,4},{6,7},{7,6},{8,9},{9,8},{10,11... | collective-permute-start | bytes 3612680 | tf_op jit(solution)/shard_map/ppermute | solution.py:1699
  30.2 18.4 %collective-permute-start.7 = (f32[1,128]{1,0:T(1,128)}, f32[1,128]{1,0:T(1,128)S(1)}, u32[]{:S(2)}, u32[]{:S(2)}) collective-permute-start(f32[1,128]{1,0:T(1,128)} %add_all.2.refs_0_), channel_id=1, source_target_pairs={{0,8},{2,10},{4,12},{6,14},{8,0},{10,2},{12,4},{14,6},{16,24},{18,... | collective-permute-start | bytes 1544 | tf_op jit(solution)/shard_map/ppermute | solution.py:1617
  32.2 16.3 %collective-permute-start.8 = (f32[1,128]{1,0:T(1,128)}, f32[1,128]{1,0:T(1,128)S(1)}, u32[]{:S(2)}, u32[]{:S(2)}) collective-permute-start(f32[1,128]{1,0:T(1,128)} %add_all.2.refs_0_), channel_id=1, source_target_pairs={{0,16},{2,18},{4,20},{6,22},{8,24},{10,26},{12,28},{14,30},{16,0},... | collective-permute-start | bytes 1544 | tf_op jit(solution)/shard_map/ppermute | solution.py:1617
  34.8 13.8 %collective-permute-start.9 = (f32[1,128]{1,0:T(1,128)}, f32[1,128]{1,0:T(1,128)S(1)}, u32[]{:S(2)}, u32[]{:S(2)}) collective-permute-start(f32[1,128]{1,0:T(1,128)} %add_all.2.refs_0_), channel_id=1, source_target_pairs={{0,24},{2,26},{4,28},{6,30},{8,16},{10,18},{12,20},{14,22},{16,8},... | collective-permute-start | bytes 1544 | tf_op jit(solution)/shard_map/ppermute | solution.py:1617
  170.0 26.2 %collective-permute-start.15 = (bf16[3072,384]{1,0:T(8,128)(2,1)}, bf16[3072,384]{1,0:T(8,128)(2,1)S(1)}, u32[]{:S(2)}, u32[]{:S(2)}) collective-permute-start(bf16[3072,384]{1,0:T(8,128)(2,1)} %get-tuple-element.174), channel_id=1, source_target_pairs={{0,1},{1,0},{2,3},{3,2},{4,5},{5,4},{6,7},{7,6},{8,9},{9,8},{10,11... | collective-permute-start | bytes 7077896 | tf_op jit(solution)/shard_map/ppermute | solution.py:1459
  205.4 70.4 %collective-permute-start.19 = (bf16[1536,384]{1,0:T(8,128)(2,1)}, bf16[1536,384]{1,0:T(8,128)(2,1)S(1)}, u32[]{:S(2)}, u32[]{:S(2)}) collective-permute-start(bf16[1536,384]{1,0:T(8,128)(2,1)} %get-tuple-element.184), channel_id=1, source_target_pairs={{0,8},{2,10},{4,12},{6,14},{8,0},{10,2},{12,4},{14,6},{16,24},{18,... | collective-permute-start | bytes 3538952 | tf_op jit(solution)/shard_map/ppermute | solution.py:1603
  214.9 41.1 %collective-permute-start.16 = (bf16[1120,384]{1,0:T(8,128)(2,1)}, bf16[1120,384]{1,0:T(8,128)(2,1)S(1)}, u32[]{:S(2)}, u32[]{:S(2)}) collective-permute-start(bf16[1120,384]{1,0:T(8,128)(2,1)} %get-tuple-element.176.refs_7_), channel_id=1, source_target_pairs={{0,4},{2,6},{4,0},{6,2},{8,12},{10,14},{12,8},{14,10},{16,20},{18,... | collective-permute-start | bytes 2580488 | tf_op jit(solution)/shard_map/ppermute | solution.py:1603
  236.6 22.4 %collective-permute-start.17 = (bf16[1120,384]{1,0:T(8,128)(2,1)}, bf16[1120,384]{1,0:T(8,128)(2,1)}, u32[]{:S(2)}, u32[]{:S(2)}) collective-permute-start(bf16[1120,384]{1,0:T(8,128)(2,1)} %get-tuple-element.177), channel_id=1, source_target_pairs={{0,2},{2,0},{4,6},{6,4},{8,10},{10,8},{12,14},{14,12},{16,18},{18,... | collective-permute-start | bytes 2580488 | tf_op jit(solution)/shard_map/ppermute | solution.py:1603
  236.6 39.1 %collective-permute-start.18 = (bf16[1120,384]{1,0:T(8,128)(2,1)}, bf16[1120,384]{1,0:T(8,128)(2,1)}, u32[]{:S(2)}, u32[]{:S(2)}) collective-permute-start(bf16[1120,384]{1,0:T(8,128)(2,1)} %get-tuple-element.178), channel_id=1, source_target_pairs={{0,6},{2,4},{4,2},{6,0},{8,14},{10,12},{12,10},{14,8},{16,22},{18,... | collective-permute-start | bytes 2580488 | tf_op jit(solution)/shard_map/ppermute | solution.py:1603
  253.8 106.3 %collective-permute-start.24 = (bf16[1568,512]{1,0:T(8,128)(2,1)}, bf16[1568,512]{1,0:T(8,128)(2,1)S(1)}, u32[]{:S(2)}, u32[]{:S(2)}) collective-permute-start(bf16[1568,512]{1,0:T(8,128)(2,1)} %get-tuple-element.205), channel_id=1, source_target_pairs={{0,1},{1,0},{2,3},{3,2},{4,5},{5,4},{6,7},{7,6},{8,9},{9,8},{10,11... | collective-permute-start | bytes 4816904 | tf_op jit(solution)/shard_map/ppermute | solution.py:1699
  281.4 75.1 %collective-permute-start.23 = (bf16[768,384]{1,0:T(8,128)(2,1)}, bf16[768,384]{1,0:T(8,128)(2,1)S(1)}, u32[]{:S(2)}, u32[]{:S(2)}) collective-permute-start(bf16[768,384]{1,0:T(8,128)(2,1)} %get-tuple-element.199), channel_id=1, source_target_pairs={{0,16},{2,18},{4,20},{6,22},{8,24},{10,26},{12,28},{14,30},{16,0},... | collective-permute-start | bytes 1769480 | tf_op jit(solution)/shard_map/ppermute | solution.py:1603
  311.5 38.9 %collective-permute-start.20 = (bf16[352,384]{1,0:T(8,128)(2,1)}, bf16[352,384]{1,0:T(8,128)(2,1)S(1)}, u32[]{:S(2)}, u32[]{:S(2)}) collective-permute-start(bf16[352,384]{1,0:T(8,128)(2,1)} %get-tuple-element.191.refs_7_), channel_id=1, source_target_pairs={{0,16},{2,18},{4,20},{6,22},{8,24},{10,26},{12,28},{14,30},{16,0},... | collective-permute-start | bytes 811016 | tf_op jit(solution)/shard_map/ppermute | solution.py:1603
  311.6 38.8 %collective-permute-start.21 = (bf16[352,384]{1,0:T(8,128)(2,1)}, bf16[352,384]{1,0:T(8,128)(2,1)}, u32[]{:S(2)}, u32[]{:S(2)}) collective-permute-start(bf16[352,384]{1,0:T(8,128)(2,1)} %get-tuple-element.192), channel_id=1, source_target_pairs={{0,8},{2,10},{4,12},{6,14},{8,0},{10,2},{12,4},{14,6},{16,24},{18,... | collective-permute-start | bytes 811016 | tf_op jit(solution)/shard_map/ppermute | solution.py:1603
  325.8 30.7 %collective-permute-start.22 = (bf16[352,384]{1,0:T(8,128)(2,1)}, bf16[352,384]{1,0:T(8,128)(2,1)}, u32[]{:S(2)}, u32[]{:S(2)}) collective-permute-start(bf16[352,384]{1,0:T(8,128)(2,1)} %get-tuple-element.193), channel_id=1, source_target_pairs={{0,24},{2,26},{4,28},{6,30},{8,16},{10,18},{12,20},{14,22},{16,8},... | collective-permute-start | bytes 811016 | tf_op jit(solution)/shard_map/ppermute | solution.py:1603
  350.4 27.5 %collective-permute-start.25 = (bf16[1568,512]{1,0:T(8,128)(2,1)}, bf16[1568,512]{1,0:T(8,128)(2,1)S(1)}, u32[]{:S(2)}, u32[]{:S(2)}) collective-permute-start(bf16[1568,512]{1,0:T(8,128)(2,1)} %get-tuple-element.210), channel_id=1, source_target_pairs={{0,1},{1,0},{2,3},{3,2},{4,5},{5,4},{6,7},{7,6},{8,9},{9,8},{10,11... | collective-permute-start | bytes 4816904 | tf_op jit(solution)/shard_map/ppermute | solution.py:1699
  377.9 58.8 %collective-permute-start.26 = (bf16[1568,256]{1,0:T(8,128)(2,1)}, bf16[1568,256]{1,0:T(8,128)(2,1)S(1)}, u32[]{:S(2)}, u32[]{:S(2)}) collective-permute-start(bf16[1568,256]{1,0:T(8,128)(2,1)} %get-tuple-element.216), channel_id=1, source_target_pairs={{0,1},{1,0},{2,3},{3,2},{4,5},{5,4},{6,7},{7,6},{8,9},{9,8},{10,11... | collective-permute-start | bytes 2408456 | tf_op jit(solution)/shard_map/ppermute | solution.py:1699
  395.9 40.7 %collective-permute-start.27 = (bf16[1568,256]{1,0:T(8,128)(2,1)}, bf16[1568,256]{1,0:T(8,128)(2,1)S(1)}, u32[]{:S(2)}, u32[]{:S(2)}) collective-permute-start(bf16[1568,256]{1,0:T(8,128)(2,1)} %get-tuple-element.217), channel_id=1, source_target_pairs={{0,1},{1,0},{2,3},{3,2},{4,5},{5,4},{6,7},{7,6},{8,9},{9,8},{10,11... | collective-permute-start | bytes 2408456 | tf_op jit(solution)/shard_map/ppermute | solution.py:1699
  396.4 36.2 %collective-permute-start.28 = (bf16[768,384]{1,0:T(8,128)(2,1)S(1)}, bf16[768,384]{1,0:T(8,128)(2,1)S(1)}, u32[]{:S(2)}, u32[]{:S(2)}) collective-permute-start(bf16[768,384]{1,0:T(8,128)(2,1)S(1)} %copy-done.49), channel_id=1, source_target_pairs={{0,1},{1,0},{2,3},{3,2},{4,5},{5,4},{6,7},{7,6},{8,9},{9,8},{10,11... | collective-permute-start | bytes 1769480 | tf_op jit(solution)/shard_map/ppermute | solution.py:1459
  396.5 36.2 %collective-permute-start.29 = (bf16[768,384]{1,0:T(8,128)(2,1)}, bf16[768,384]{1,0:T(8,128)(2,1)S(1)}, u32[]{:S(2)}, u32[]{:S(2)}) collective-permute-start(bf16[768,384]{1,0:T(8,128)(2,1)} %get-tuple-element.212.refs_7_), channel_id=1, source_target_pairs={{0,1},{1,0},{2,3},{3,2},{4,5},{5,4},{6,7},{7,6},{8,9},{9,8},{10,11... | collective-permute-start | bytes 1769480 | tf_op jit(solution)/shard_map/ppermute | solution.py:1459
  396.9 20.2 %collective-permute-start.30 = (bf16[192,384]{1,0:T(8,128)(2,1)S(1)}, bf16[192,384]{1,0:T(8,128)(2,1)S(1)}, u32[]{:S(2)}, u32[]{:S(2)}) collective-permute-start(bf16[192,384]{1,0:T(8,128)(2,1)S(1)} %copy-done.24), channel_id=1, source_target_pairs={{0,4},{2,6},{4,0},{6,2},{8,12},{10,14},{12,8},{14,10},{16,20},{18,... | collective-permute-start | bytes 442376 | tf_op jit(solution)/shard_map/ppermute | solution.py:1603
  444.8 20.3 %collective-permute-start.33 = (bf16[768,384]{1,0:T(8,128)(2,1)}, bf16[768,384]{1,0:T(8,128)(2,1)S(1)}, u32[]{:S(2)}, u32[]{:S(2)}) collective-permute-start(bf16[768,384]{1,0:T(8,128)(2,1)} %get-tuple-element.227), channel_id=1, source_target_pairs={{0,1},{1,0},{2,3},{3,2},{4,5},{5,4},{6,7},{7,6},{8,9},{9,8},{10,11... | collective-permute-start | bytes 1769480 | tf_op jit(solution)/shard_map/ppermute | solution.py:1459
  444.8 20.2 %collective-permute-start.35 = (bf16[384,384]{1,0:T(8,128)(2,1)S(1)}, bf16[384,384]{1,0:T(8,128)(2,1)S(1)}, u32[]{:S(2)}, u32[]{:S(2)}) collective-permute-start(bf16[384,384]{1,0:T(8,128)(2,1)S(1)} %copy-done.12), channel_id=1, source_target_pairs={{0,4},{2,6},{4,0},{6,2},{8,12},{10,14},{12,8},{14,10},{16,20},{18,... | collective-permute-start | bytes 884744 | tf_op jit(solution)/shard_map/ppermute | solution.py:1603
  446.3 18.8 %collective-permute-start.36 = (bf16[384,384]{1,0:T(8,128)(2,1)S(1)}, bf16[384,384]{1,0:T(8,128)(2,1)S(1)}, u32[]{:S(2)}, u32[]{:S(2)}) collective-permute-start(bf16[384,384]{1,0:T(8,128)(2,1)S(1)} %copy-done.51), channel_id=1, source_target_pairs={{0,2},{2,0},{4,6},{6,4},{8,10},{10,8},{12,14},{14,12},{16,18},{18,... | collective-permute-start | bytes 884744 | tf_op jit(solution)/shard_map/ppermute | solution.py:1603
  448.2 16.9 %collective-permute-start.37 = (bf16[384,384]{1,0:T(8,128)(2,1)S(1)}, bf16[384,384]{1,0:T(8,128)(2,1)S(1)}, u32[]{:S(2)}, u32[]{:S(2)}) collective-permute-start(bf16[384,384]{1,0:T(8,128)(2,1)S(1)} %copy-done.50), channel_id=1, source_target_pairs={{0,6},{2,4},{4,2},{6,0},{8,14},{10,12},{12,10},{14,8},{16,22},{18,... | collective-permute-start | bytes 884744 | tf_op jit(solution)/shard_map/ppermute | solution.py:1603
  483.1 80.5 %collective-permute-start.41 = (bf16[176,384]{1,0:T(8,128)(2,1)}, bf16[176,384]{1,0:T(8,128)(2,1)S(1)}, u32[]{:S(2)}, u32[]{:S(2)}) collective-permute-start(bf16[176,384]{1,0:T(8,128)(2,1)} %get-tuple-element.241), channel_id=1, source_target_pairs={{0,16},{2,18},{4,20},{6,22},{8,24},{10,26},{12,28},{14,30},{16,0},... | collective-permute-start | bytes 405512 | tf_op jit(solution)/shard_map/ppermute | solution.py:1603
  520.3 45.5 %collective-permute-start.42 = (bf16[176,384]{1,0:T(8,128)(2,1)}, bf16[176,384]{1,0:T(8,128)(2,1)S(1)}, u32[]{:S(2)}, u32[]{:S(2)}) collective-permute-start(bf16[176,384]{1,0:T(8,128)(2,1)} %get-tuple-element.242), channel_id=1, source_target_pairs={{0,8},{2,10},{4,12},{6,14},{8,0},{10,2},{12,4},{14,6},{16,24},{18,... | collective-permute-start | bytes 405512 | tf_op jit(solution)/shard_map/ppermute | solution.py:1603
  (67 other events, 568.7 us)
